TPU v7x, 256 devices: a whole 4x4x8 slice. The times are simulated.
256 devices in a mesh: dp: 64 (over z_hi, x, y, core), pipe: 4 (over z_lo).
Axes of the slice: x: 4, y: 4, z: 8 (z_hi: 2, z_lo: 4; z = z_hi * 4 + z_lo), core: 2. Of those that a mesh axis runs over, the one named last changes fastest.
Arguments:
- fwd_x: bfloat16 [4, 64, 64, 3584], P('pipe', 'dp'), may hold values from -6 to 6
- fwd_q: bfloat16 [4, 64, 64, 3584], P('pipe', 'dp')
- bwd_x: bfloat16 [4, 64, 64, 3584], P('pipe', 'dp'), may hold values from -16 to 16
- bwd_q: bfloat16 [4, 64, 64, 3584], P('pipe', 'dp')
- bwd_dout: bfloat16 [4, 64, 64, 3584], P('pipe', 'dp'), may hold values from -6 to 6
- cache_kv: bfloat16 [4, 64, 1024, 1024], P('pipe', 'dp'), may hold values from -6 to 6
- kv_weight: bfloat16 [4, 3584, 1024], P('pipe', 'dp'), may hold values from -0.09375 to 0.09375
- seg_lengths: int32 [4, 64, 4], P('pipe', 'dp'), may hold values from 1 to 896, as said below
Outputs:
- next_act: bfloat16 [4, 64, 64, 3584], P('pipe', 'dp')
- grad_q: bfloat16 [4, 64, 64, 3584], P('pipe', 'dp')
- prev_grad: bfloat16 [4, 64, 64, 3584], P('pipe', 'dp')
- weight_grad: float32 [4, 3584, 1024], P('pipe', 'dp')
Inputs may be any that keep to these rules, and one draw needn't show every extreme that they name: `seg_lengths`: each row holds four lengths that sum to 1024; the first is at least 1; the second lies from 64 to 127 and is 64 in some row of every draw; the third is at most 64 and equals 64 in some row of every draw; the fourth lies from 32 to the third.
All inputs are finite; a program needn't handle non-finite values.
Results may differ from a plain program's by a relative error of at most 0.035.
Values may be sent and summed in bfloat16 or wider, within the bound.
No kernel may reach another device: no remote copies, remote signals or barrier semaphores. Data moves between devices by JAX's collectives and lax.ppermute only.
A program may use at most 128 MiB of HBM per device.

v0:
```python
import math

import jax
import jax.numpy as jnp
from jax import lax
from jax.sharding import PartitionSpec as P

HD = 128


def shifted(value, axis, steps):
    count = lax.axis_size(axis)
    first, last = (max(0, -steps), min(count, count - steps))
    return lax.ppermute(value, axis, [(source, source + steps) for source in range(first, last)])


def masked_softmax(scores, allowed):
    masked = jnp.where(allowed[:, None, :], scores, -1e30)
    top = jnp.max(masked, axis=-1, keepdims=True)
    raised = jnp.exp(masked - top)
    return raised / jnp.sum(raised, axis=-1, keepdims=True)


def forward_segment(query, own_kv, cache, length):
    seg = query.shape[0]
    seq_len = cache.shape[0]
    half = cache.shape[1] // 2
    kv_heads = half // HD
    group = query.shape[1] // half
    scale = 1.0 / math.sqrt(HD)
    start = seq_len - length
    rows = jnp.arange(seg, dtype=jnp.int32)
    cache_ok = jnp.broadcast_to(
        jnp.arange(seq_len, dtype=jnp.int32)[None, :] < start, (seg, seq_len)
    )
    own_ok = (rows[None, :] <= rows[:, None]) & (rows[None, :] < length)
    allowed = jnp.concatenate([cache_ok, own_ok], axis=1)
    keys = jnp.concatenate([cache[:, :half], own_kv[:, :half]], axis=0)
    values = jnp.concatenate([cache[:, half:], own_kv[:, half:]], axis=0)
    pieces = []
    for head in range(kv_heads):
        block = query[:, head * group * HD : (head + 1) * group * HD].reshape(seg * group, HD)
        key_head = keys[:, head * HD : (head + 1) * HD]
        scores = (jnp.dot(block, key_head.T, preferred_element_type=jnp.float32) * scale).reshape(
            seg, group, -1
        )
        probs = masked_softmax(scores, allowed).astype(jnp.bfloat16).reshape(seg * group, -1)
        mixed = jnp.dot(
            probs, values[:, head * HD : (head + 1) * HD], preferred_element_type=jnp.float32
        )
        pieces.append(mixed.reshape(seg, group * HD))
    result = jnp.concatenate(pieces, axis=1)
    return jnp.where((rows < length)[:, None], result, 0.0).astype(jnp.bfloat16)


def backward_segment(query, dout, cache, third, fourth):
    seg = query.shape[0]
    seq_len = cache.shape[0]
    half = cache.shape[1] // 2
    kv_heads = half // HD
    group = query.shape[1] // half
    scale = 1.0 / math.sqrt(HD)
    start = seq_len - fourth - third
    rows = jnp.arange(seg, dtype=jnp.int32)
    allowed = jnp.arange(seq_len, dtype=jnp.int32)[None, :] <= start + rows[:, None]
    live = (rows < third)[:, None]
    dout = jnp.where(live, dout, jnp.zeros_like(dout))
    query_parts, key_parts, value_parts = ([], [], [])
    for head in range(kv_heads):
        block = query[:, head * group * HD : (head + 1) * group * HD].reshape(seg * group, HD)
        grad_block = dout[:, head * group * HD : (head + 1) * group * HD].reshape(seg * group, HD)
        key_head = cache[:, head * HD : (head + 1) * HD]
        value_head = cache[:, half + head * HD : half + (head + 1) * HD]
        scores = (jnp.dot(block, key_head.T, preferred_element_type=jnp.float32) * scale).reshape(
            seg, group, seq_len
        )
        probs = masked_softmax(scores, allowed).reshape(seg * group, seq_len)
        rounded = probs.astype(jnp.bfloat16)
        mixed = jnp.dot(rounded, value_head, preferred_element_type=jnp.float32)
        delta = jnp.sum(grad_block.astype(jnp.float32) * mixed, axis=1, keepdims=True)
        along = jnp.dot(grad_block, value_head.T, preferred_element_type=jnp.float32)
        dscore = (probs * (along - delta)).astype(jnp.bfloat16)
        query_parts.append(
            (jnp.dot(dscore, key_head, preferred_element_type=jnp.float32) * scale).reshape(
                seg, group * HD
            )
        )
        dscore_own = lax.dynamic_slice_in_dim(dscore, start, seg, 1)
        rounded_own = lax.dynamic_slice_in_dim(rounded, start, seg, 1)
        key_parts.append(jnp.dot(dscore_own.T, block, preferred_element_type=jnp.float32) * scale)
        value_parts.append(jnp.dot(rounded_own.T, grad_block, preferred_element_type=jnp.float32))
    grad_query = jnp.concatenate(query_parts, axis=1).astype(jnp.bfloat16)
    kv_grad = jnp.concatenate(key_parts + value_parts, axis=1)
    kv_grad = jnp.where(live, kv_grad, 0.0).astype(jnp.bfloat16)
    return (grad_query, kv_grad)


def shards(fwd_x, fwd_q, bwd_x, bwd_q, bwd_dout, cache_kv, kv_weight, seg_lengths):
    front_x = fwd_x[0, 0]
    front_q = fwd_q[0, 0]
    back_x = bwd_x[0, 0]
    back_q = bwd_q[0, 0]
    back_dout = bwd_dout[0, 0]
    cache = cache_kv[0, 0]
    shard = kv_weight[0]
    lengths = seg_lengths[0, 0]
    columns = front_x
    own_kv = jnp.dot(
        columns, lax.all_gather(shard, "dp", axis=0, tiled=True), preferred_element_type=jnp.float32
    ).astype(jnp.bfloat16)
    fwd_out = forward_segment(front_q, own_kv, cache, lengths[3])
    grad_query, kv_grad = backward_segment(back_q, back_dout, cache, lengths[2], lengths[3])
    input_grad = jnp.dot(
        kv_grad,
        lax.all_gather(shard, "dp", axis=0, tiled=True).T,
        preferred_element_type=jnp.float32,
    ).astype(jnp.bfloat16)
    columns = back_x
    weight_grad = lax.psum_scatter(
        jnp.dot(columns.T, kv_grad, preferred_element_type=jnp.float32),
        "dp",
        scatter_dimension=0,
        tiled=True,
    )
    next_act = shifted(fwd_out, "pipe", 1)
    prev_grad = shifted(input_grad, "pipe", -1)
    return (next_act[None, None], grad_query[None, None], prev_grad[None, None], weight_grad[None])


def solution(mesh):
    return jax.shard_map(
        shards,
        mesh=mesh,
        in_specs=(
            P("pipe", "dp", None, None),
            P("pipe", "dp", None, None),
            P("pipe", "dp", None, None),
            P("pipe", "dp", None, None),
            P("pipe", "dp", None, None),
            P("pipe", "dp", None, None),
            P("pipe", "dp", None),
            P("pipe", "dp", None),
        ),
        out_specs=(
            P("pipe", "dp", None, None),
            P("pipe", "dp", None, None),
            P("pipe", "dp", None, None),
            P("pipe", "dp", None),
        ),
        check_vma=False,
    )
```

profile of v0, /device:TPU:64, one launch (start us, length us, event | category | flops | bytes accessed | tf_op | source)
XLA Modules:
  0.0 567.3 jit_solution(12510454710345901472)
XLA Ops:
  7.2 0.7 all-gather.3.cloned.1.call-update
  8.0 1.3 fusion.113
  11.4 0.7 iota_compare_fusion.3
  12.2 0.8 reshape.317
  13.0 0.8 reshape.323
  13.7 0.8 reshape.321
  14.5 0.8 reshape.319
  15.3 1.7 fusion.109
  17.5 1.0 reshape.318
  18.5 0.6 fusion.120
  21.0 0.6 fusion.119
  33.3 0.7 copy-done.4
  33.9 7.5 %convolution_bitcast_fusion = f32[3584,1024]{0,1:T(8,128)} fusion(bf16[1,1,64,3584]{3,2,1,0:T(8,128)(2,1)S(1)} %copy-done, bf16[64,1024]{1,0:T(8,128)(2,1)S(1)} %convolution_dynamic-update-slice_fusion, pred[64]{0:T(512)(128)(4,1)S(1)} %iota_compare_fusion.3), kind=kOutput, calls=%fused_computation | convolution fusion | flops 469827584 | bytes 15269952 | tf_op jit(solution)/shard_map/dot_general | solution.py:120
  41.5 15.4 %copy.15 = f32[3584,1024]{1,0:T(8,128)} copy(f32[3584,1024]{0,1:T(8,128)} %convolution_bitcast_fusion) | data formatting | bytes 29360128
  56.9 1.0 copy-done.7
  57.9 0.8 reshape.308
  58.8 0.8 reshape.312
  59.6 0.8 reshape.310
  60.4 0.6 iota_compare_fusion.4
  61.1 1.1 broadcast_in_dim.140
  62.2 1.6 broadcast_in_dim.141
  63.8 1.6 fusion.31
  65.5 1.6 fusion.32
  67.3 1.6 fusion.33
  69.0 1.6 fusion.30
  70.8 1.7 fusion.108
  72.5 47.4 %all-gather.3.cloned.1.call-done = bf16[1,3584,1024]{2,1,0:T(8,128)(2,1)} async-done(((bf16[1,56,1024]{2,1,0:T(8,128)(2,1)}), bf16[1,3584,1024]{2,1,0:T(8,128)(2,1)}) %all-gather.3.cloned.1.call-update) | async-done | bytes 7340048 | tf_op jit(solution)/shard_map/all_gather | solution.py:109
  119.9 6.4 %fusion.4 = bf16[64,3584]{1,0:T(8,128)(2,1)} fusion(bf16[1,3584,1024]{2,1,0:T(8,128)(2,1)} %all-gather.3.cloned.1.call-done, bf16[64,1024]{1,0:T(8,128)(2,1)S(1)} %copy-done.5, pred[64]{0:T(512)(128)(4,1)S(1)} %iota_compare_fusion.3), kind=kOutput, calls=%fused_computation.5 | convolution fusion | flops 470056960 | bytes 7929920 | tf_op jit(solution)/shard_map/dot_general | solution.py:113
  126.2 3.9 collective-permute-start.1
  130.2 1.4 fusion.27
  131.6 0.6 fusion.117
  132.7 1.2 fusion.42
  133.9 1.0 reshape.309
  135.0 0.6 fusion.116
  136.4 1.2 fusion.43
  137.6 1.0 reshape.311
  138.7 0.6 fusion.114
  140.2 1.2 fusion.45
  141.4 1.0 reshape.315
  142.4 1.5 fusion.115
  145.7 2.8 collective-permute-start
  148.5 0.8 pad_maximum_fusion
  149.3 13.6 %collective-permute-done = bf16[64,3584]{1,0:T(8,128)(2,1)S(1)} collective-permute-done((bf16[64,3584]{1,0:T(8,128)(2,1)S(1)}, bf16[64,3584]{1,0:T(8,128)(2,1)S(1)}, u32[]{:S(2)}, u32[]{:S(2)}) %collective-permute-start) | collective-permute-done | bytes 458784 | tf_op jit(solution)/shard_map/ppermute | solution.py:14
  162.9 392.9 %reduce-scatter.4.cloned.1.call-done = f32[56,1024]{1,0:T(8,128)} async-done(((f32[3584,1024]{1,0:T(8,128)}), f32[56,1024]{1,0:T(8,128)}) %reduce-scatter.4.cloned.1.call-update) | async-done | bytes 229392
  555.8 1.1 copy.16
  557.0 0.9 copy.14
  557.8 0.8 copy.34
  558.6 1.8 copy.35
  (101 shorter events, 19.5 us)
Async XLA Ops:
  7.2 26.8 %copy-start = (bf16[1,1,64,3584]{3,2,1,0:T(8,128)(2,1)S(1)}, bf16[1,1,64,3584]{3,2,1,0:T(8,128)(2,1)}, u32[]{:S(2)}) copy-start(bf16[1,1,64,3584]{3,2,1,0:T(8,128)(2,1)} %param.10) | copy-start | bytes 1376260
  7.2 4.8 copy-start.6
  7.2 112.7 %all-gather.3.cloned.1.call-start = ((), (), s32[]{:S(2)}) async-start(), calls=%async_computation.1 | async-start | bytes 7454720 | tf_op jit(solution)/shard_map/all_gather | solution.py:109
  7.9 547.9 %reduce-scatter.4.cloned.1.call-start = ((), (), s32[]{:S(2)}) async-start(), calls=%async_computation.2 | async-start | bytes 14909440
  12.1 6.4 %copy-start.3 = (bf16[1,1,1024,1024]{3,2,1,0:T(8,128)(2,1)S(1)}, bf16[1,1,1024,1024]{3,2,1,0:T(8,128)(2,1)}, u32[]{:S(2)}) copy-start(bf16[1,1,1024,1024]{3,2,1,0:T(8,128)(2,1)} %param.13) | copy-start | bytes 6291460
  19.5 0.9 copy-start.11
  22.0 0.9 copy-start.9
  24.4 0.9 copy-start.8
  26.9 0.9 copy-start.10
  28.9 1.0 copy-start.19
  29.9 0.9 copy-start.20
  30.8 0.9 copy-start.21
  31.7 1.2 copy-start.22
  33.3 0.7 copy-start.4
  56.8 1.0 copy-start.7
  70.8 49.1 %copy-start.5 = (bf16[64,1024]{1,0:T(8,128)(2,1)S(1)}, bf16[64,1024]{1,0:T(8,128)(2,1)}, u32[]{:S(2)}) copy-start(bf16[64,1024]{1,0:T(8,128)(2,1)} %copy-done.4) | copy-start | bytes 393220
  119.9 10.3 %copy-start.2 = (bf16[1,3584,1024]{2,1,0:T(8,128)(2,1)S(1)}, bf16[1,3584,1024]{2,1,0:T(8,128)(2,1)}, u32[]{:S(2)}) copy-start(bf16[1,3584,1024]{2,1,0:T(8,128)(2,1)} %all-gather.3.cloned.1.call-done) | copy-start | bytes 22020100
  119.9 10.3 %copy-start.14 = (bf16[1,1,64,3584]{3,2,1,0:T(8,128)(2,1)S(1)}, bf16[1,1,64,3584]{3,2,1,0:T(8,128)(2,1)}, u32[]{:S(2)}) copy-start(bf16[1,1,64,3584]{3,2,1,0:T(8,128)(2,1)} %param.8) | copy-start | bytes 1376260
  126.2 5.4 copy-start.13
  126.2 23.1 %collective-permute-start.1 = (bf16[64,3584]{1,0:T(8,128)(2,1)}, bf16[64,3584]{1,0:T(8,128)(2,1)}, u32[]{:S(2)}, u32[]{:S(2)}) collective-permute-start(bf16[64,3584]{1,0:T(8,128)(2,1)} %fusion.4), channel_id=1, source_target_pairs={{1,0},{2,1},{3,2},{5,4},{6,5},{7,6},{9,8},{10,9},{11,10},{13,12},{... | collective-permute-start | bytes 1376264 | tf_op jit(solution)/shard_map/ppermute | solution.py:14
  131.6 1.1 copy-start.15
  132.7 2.2 copy-start.12
  135.6 0.8 copy-start.16
  139.3 0.8 copy-start.17
  143.9 0.8 copy-start.18
  145.7 17.2 %collective-permute-start = (bf16[64,3584]{1,0:T(8,128)(2,1)S(1)}, bf16[64,3584]{1,0:T(8,128)(2,1)S(1)}, u32[]{:S(2)}, u32[]{:S(2)}) collective-permute-start(bf16[64,3584]{1,0:T(8,128)(2,1)S(1)} %fusion.46), channel_id=1, source_target_pairs={{0,1},{1,2},{2,3},{4,5},{5,6},{6,7},{8,9},{9,10},{10,11},{12,13},{... | collective-permute-start | bytes 1376264 | tf_op jit(solution)/shard_map/ppermute | solution.py:14
  148.5 411.9 %copy-start.1 = (bf16[1,1,64,3584]{3,2,1,0:T(8,128)(2,1)S(1)}, bf16[1,1,64,3584]{3,2,1,0:T(8,128)(2,1)}, u32[]{:S(2)}) copy-start(bf16[1,1,64,3584]{3,2,1,0:T(8,128)(2,1)} %param.10) | copy-start | bytes 1376260
Sparse Core Ops, SparseCore 0:
  11.6 108.2 all-gather.2
  122.4 433.3 reduce-scatter.3
where the time goes:
time: 573 us; the launch traced here: 567 us
  waiting for transfers between devices  455 us (79%)
  local copies, waits for them, and re-layouts  44.1 us (8%)
  matrix products  38.3 us (7%)
  between operations  15.9 us (3%)
  other arithmetic  7.64 us (1%)
  starting transfers between devices  6.8 us (1%)
    unnamed x3, waiting for transfers between devices  394 us
    all_gather x1, waiting for transfers between devices, shards(): lax.all_gather(shard, 'dp', axis=0, tiled=True)  47.4 us
    unnamed x51, local copies, waits for them, and re-layouts  25.1 us
    ppermute x2, waiting for transfers between devices, shifted(): lax.ppermute(value, axis, [(source, source + steps) for source in range(f...  13.6 us
  transfers between devices with their start and end apart: 4, of which 3 were waited for; matrix products, arithmetic and copies ran while one was open for 14% of the time, Pallas kernels for 0%

commit v1 on v0

v1 whole, which is shorter than its diff:
```python
import functools
import math

import jax
import jax.numpy as jnp
from jax import lax
from jax.experimental import pallas as pl
from jax.experimental.pallas import tpu as pltpu
from jax.sharding import PartitionSpec as P

HD = 128
GROUP = 7
SEG = 64
BLK = 56
ROWS = GROUP * SEG
WIDE = GROUP * HD
SCALE = 1.0 / math.sqrt(HD)
EXP_SCALE = SCALE * math.log2(math.e)
F32 = jnp.float32
BF16 = jnp.bfloat16
VMEM_LIMIT = 48 * 1024 * 1024


def params():
    return pltpu.CompilerParams(vmem_limit_bytes=VMEM_LIMIT)


def cost(us):
    return pl.CostEstimate(
        flops=int(us * 1.0e9), bytes_accessed=int(us * 1.0e6), transcendentals=0
    )


def dp_target(d, z=0, x=0, y=0, c=0):
    cz, cx, cy, cc = d // 32, (d // 8) % 4, (d // 2) % 4, d % 2
    return ((((cz + z) % 2) * 4 + (cx + x) % 4) * 4 + (cy + y) % 4) * 2 + (cc + c) % 2


def move(value, **steps):
    return lax.ppermute(value, "dp", [(d, dp_target(d, **steps)) for d in range(64)])


def move_back_section(value, **steps):
    pairs = [
        (d * 4 + p, dp_target(d, **steps) * 4 + p - 1) for d in range(64) for p in range(1, 4)
    ]
    return lax.ppermute(value, ("dp", "pipe"), pairs)


def block_index(pos_ref, x, rc, k, rz):
    z, y, c = pos_ref[0], pos_ref[2], pos_ref[3]
    return (((z ^ rz) * 4 + x) * 4 + ((y + 4 - k) & 3)) * 2 + (c ^ rc)


def piece_order():
    return [(rc, k, rz) for rc in range(2) for k in range(4) for rz in range(2)]


def split_kernel(pos_ref, fx_ref, bx_ref, o0, o1, o2, o3, scr):
    for s in range(64):
        scr[s, 0:SEG, :] = fx_ref[:, s * BLK : (s + 1) * BLK]
        scr[s, SEG : 2 * SEG, :] = bx_ref[:, s * BLK : (s + 1) * BLK]
    for dx, out in enumerate((o0, o1, o2, o3)):
        x = (pos_ref[1] + dx) & 3
        out[...] = jnp.concatenate(
            [scr[block_index(pos_ref, x, rc, k, rz)] for rc, k, rz in piece_order()], axis=1
        )


def split_inputs(pos, fx, bx):
    piece = jax.ShapeDtypeStruct((2 * SEG, 16 * BLK), BF16)
    return pl.pallas_call(
        split_kernel,
        out_shape=[piece] * 4,
        in_specs=[
            pl.BlockSpec(memory_space=pltpu.SMEM),
            pl.BlockSpec(memory_space=pltpu.VMEM),
            pl.BlockSpec(memory_space=pltpu.VMEM),
        ],
        out_specs=[pl.BlockSpec(memory_space=pltpu.VMEM)] * 4,
        scratch_shapes=[pltpu.VMEM((64, 2 * SEG, BLK), BF16)],
        compiler_params=params(),
        cost_estimate=cost(3),
        name="split_inputs",
    )(pos, fx, bx)


def join_kernel(pos_ref, g0, g1, g2, g3, out_ref, scr):
    for k0, piece in enumerate((g0, g1, g2, g3)):
        x = (pos_ref[1] + k0) & 3
        for m, (rc, k, rz) in enumerate(piece_order()):
            scr[block_index(pos_ref, x, rc, k, rz)] = piece[:, m * BLK : (m + 1) * BLK]
    out_ref[...] = jnp.concatenate([scr[s] for s in range(64)], axis=1)


def join_pieces(pos, pieces):
    return pl.pallas_call(
        join_kernel,
        out_shape=jax.ShapeDtypeStruct((SEG, 64 * BLK), BF16),
        in_specs=[pl.BlockSpec(memory_space=pltpu.SMEM)]
        + [pl.BlockSpec(memory_space=pltpu.VMEM)] * 4,
        out_specs=pl.BlockSpec(memory_space=pltpu.VMEM),
        scratch_shapes=[pltpu.VMEM((64, SEG, BLK), BF16)],
        compiler_params=params(),
        cost_estimate=cost(2),
        name="join_pieces",
    )(pos, *pieces)


def dot_nt(a, b):
    return lax.dot_general(a, b, (((1,), (1,)), ((), ())), preferred_element_type=F32)


def dot_tn(a, b):
    return lax.dot_general(a, b, (((0,), (0,)), ((), ())), preferred_element_type=F32)


def dot_nn(a, b):
    return lax.dot_general(a, b, (((1,), (0,)), ((), ())), preferred_element_type=F32)


def stack_heads(block):
    return jnp.concatenate([block[:, h * HD : (h + 1) * HD] for h in range(GROUP)], axis=0)


def unstack_heads(rows):
    return jnp.concatenate([rows[h * SEG : (h + 1) * SEG] for h in range(GROUP)], axis=1)


def row_in_segment(shape):
    return lax.broadcasted_iota(jnp.int32, shape, 0) & (SEG - 1)


def backward_kernel(len_ref, q_ref, do_ref, k_ref, v_ref, gq_ref, dk_ref, dv_ref):
    third, fourth = len_ref[2], len_ref[3]
    seq = k_ref.shape[0]
    base = seq - 2 * SEG
    offset = seq - fourth - third - base
    q = stack_heads(q_ref[...])
    live = lax.broadcasted_iota(jnp.int32, (SEG, WIDE), 0) < third
    dout = stack_heads(jnp.where(live, do_ref[...], jnp.zeros((SEG, WIDE), BF16)))
    keys = k_ref[...]
    values = v_ref[...]
    scores = dot_nt(q, keys)
    tail_at = lax.broadcasted_iota(jnp.int32, (ROWS, 2 * SEG), 1)
    tail_ok = tail_at <= offset + row_in_segment((ROWS, 2 * SEG))
    tail = jnp.where(tail_ok, scores[:, base:], -1e30)
    scores = jnp.concatenate([scores[:, :base], tail], axis=1)
    top = jnp.max(scores, axis=1, keepdims=True)
    raised = jnp.exp2((scores - top) * EXP_SCALE)
    probs = raised * (1.0 / jnp.sum(raised, axis=1, keepdims=True))
    rounded = probs.astype(BF16)
    mixed = dot_nn(rounded, values)
    delta = jnp.sum(dout.astype(F32) * mixed, axis=1, keepdims=True)
    along = dot_nt(dout, values)
    dscore = (probs * (along - delta)).astype(BF16)
    gq_ref[...] = unstack_heads((dot_nn(dscore, keys) * SCALE).astype(BF16))
    dk = dot_tn(dscore[:, base:], q) * SCALE
    dv = dot_tn(rounded[:, base:], dout)
    keep = lax.broadcasted_iota(jnp.int32, (SEG, HD), 0) < third
    shift = (2 * SEG - offset) & (2 * SEG - 1)
    dk = pltpu.roll(dk, shift, 0)[:SEG]
    dv = pltpu.roll(dv, shift, 0)[:SEG]
    dk_ref[...] = jnp.where(keep, dk, 0.0).astype(BF16)
    dv_ref[...] = jnp.where(keep, dv, 0.0).astype(BF16)


def group_specs(seq, first):
    rows = pl.BlockSpec((SEG, WIDE), lambda g: (0, g + first))
    key = pl.BlockSpec((seq, HD), lambda g: (0, g + first))
    value = pl.BlockSpec((seq, HD), lambda g: (0, g + first + 4))
    return rows, key, value


def backward_groups(lengths, q, dout, cache, first, count):
    rows, key, value = group_specs(cache.shape[0], first)
    return pl.pallas_call(
        backward_kernel,
        grid=(count,),
        out_shape=[
            jax.ShapeDtypeStruct((SEG, count * WIDE), BF16),
            jax.ShapeDtypeStruct((SEG, count * HD), BF16),
            jax.ShapeDtypeStruct((SEG, count * HD), BF16),
        ],
        in_specs=[pl.BlockSpec(memory_space=pltpu.SMEM), rows, rows, key, value],
        out_specs=[
            pl.BlockSpec((SEG, WIDE), lambda g: (0, g)),
            pl.BlockSpec((SEG, HD), lambda g: (0, g)),
            pl.BlockSpec((SEG, HD), lambda g: (0, g)),
        ],
        compiler_params=params(),
        cost_estimate=cost(4 * count),
        name="backward_groups",
    )(lengths, q, dout, cache, cache)


def stored_kernel(len_ref, q_ref, k_ref, v_ref, acc_ref, stat_ref):
    fourth = len_ref[3]
    seq = k_ref.shape[0]
    base = seq - HD
    q = stack_heads(q_ref[...])
    scores = dot_nt(q, k_ref[...])
    tail_ok = lax.broadcasted_iota(jnp.int32, (ROWS, HD), 1) < HD - fourth
    tail = jnp.where(tail_ok, scores[:, base:], -1e30)
    scores = jnp.concatenate([scores[:, :base], tail], axis=1)
    top = jnp.max(scores, axis=1, keepdims=True)
    raised = jnp.exp2((scores - top) * EXP_SCALE)
    total = jnp.sum(raised, axis=1, keepdims=True)
    acc_ref[...] = unstack_heads(dot_nn(raised.astype(BF16), v_ref[...]))
    lane = lax.broadcasted_iota(jnp.int32, (SEG, HD), 1)
    stat = jnp.zeros((SEG, HD), F32)
    for h in range(GROUP):
        stat = jnp.where(lane == h, top[h * SEG : (h + 1) * SEG], stat)
        stat = jnp.where(lane == 64 + h, total[h * SEG : (h + 1) * SEG], stat)
    stat_ref[...] = stat


def stored_groups(lengths, q, cache, first, count):
    rows, key, value = group_specs(cache.shape[0], first)
    return pl.pallas_call(
        stored_kernel,
        grid=(count,),
        out_shape=[
            jax.ShapeDtypeStruct((SEG, count * WIDE), F32),
            jax.ShapeDtypeStruct((SEG, count * HD), F32),
        ],
        in_specs=[pl.BlockSpec(memory_space=pltpu.SMEM), rows, key, value],
        out_specs=[
            pl.BlockSpec((SEG, WIDE), lambda g: (0, g)),
            pl.BlockSpec((SEG, HD), lambda g: (0, g)),
        ],
        compiler_params=params(),
        cost_estimate=cost(2 * count),
        name="stored_groups",
    )(lengths, q, cache, cache)


def own_kernel(len_ref, q_ref, k0, k1, k2, k3, v0, v1, v2, v3, acc_ref, stat_ref, out_ref):
    fourth = len_ref[3]
    keys = (k0[...] + k1[...].astype(F32) + k2[...].astype(F32) + k3[...].astype(F32)).astype(BF16)
    values = (v0[...] + v1[...].astype(F32) + v2[...].astype(F32) + v3[...].astype(F32)).astype(BF16)
    q = stack_heads(q_ref[...])
    acc = stack_heads(acc_ref[...])
    stat = stat_ref[...]
    top_c = jnp.concatenate([stat[:, h : h + 1] for h in range(GROUP)], axis=0)
    total_c = jnp.concatenate([stat[:, 64 + h : 65 + h] for h in range(GROUP)], axis=0)
    scores = dot_nt(q, keys)
    at = lax.broadcasted_iota(jnp.int32, (ROWS, SEG), 1)
    row = row_in_segment((ROWS, SEG))
    scores = jnp.where((at <= row) & (at < fourth), scores, -1e30)
    top = jnp.maximum(top_c, jnp.max(scores, axis=1, keepdims=True))
    keep = jnp.exp2((top_c - top) * EXP_SCALE)
    raised = jnp.exp2((scores - top) * EXP_SCALE)
    total = total_c * keep + jnp.sum(raised, axis=1, keepdims=True)
    mixed = acc * keep + dot_nn(raised.astype(BF16), values)
    mixed = mixed * (1.0 / total)
    mixed = jnp.where(row_in_segment((ROWS, HD)) < fourth, mixed, 0.0)
    out_ref[...] = unstack_heads(mixed.astype(BF16))


def own_groups(lengths, q, parts, acc, stat):
    rows = pl.BlockSpec((SEG, WIDE), lambda g: (0, g))
    key = pl.BlockSpec((SEG, HD), lambda g: (0, g))
    value = pl.BlockSpec((SEG, HD), lambda g: (0, g + 4))
    return pl.pallas_call(
        own_kernel,
        grid=(4,),
        out_shape=jax.ShapeDtypeStruct((SEG, 4 * WIDE), BF16),
        in_specs=[pl.BlockSpec(memory_space=pltpu.SMEM), rows]
        + [key] * 4
        + [value] * 4
        + [rows, key],
        out_specs=rows,
        compiler_params=params(),
        cost_estimate=cost(4),
        name="own_groups",
    )(lengths, q, *parts, *parts, acc, stat)


def own_kv_kernel(r0, r1, r2, r3, wn_ref, wf_ref, p0, p1, p2, p3):
    x = jnp.concatenate([r[0:SEG, :] for r in (r0, r1, r2, r3)], axis=0)
    half = 8 * BLK
    total = dot_nn(x[:, :half], wn_ref[...]) + dot_nn(x[:, half:], wf_ref[...])
    for k, out in enumerate((p0, p1, p2, p3)):
        out[...] = total[k * SEG : (k + 1) * SEG].astype(out.dtype)


def own_kv_parts(pieces, near, far):
    shape = (SEG, near.shape[1])
    return pl.pallas_call(
        own_kv_kernel,
        out_shape=[jax.ShapeDtypeStruct(shape, F32)] + [jax.ShapeDtypeStruct(shape, BF16)] * 3,
        compiler_params=params(),
        cost_estimate=cost(2),
        name="own_kv_parts",
    )(*pieces, near, far)


def weight_grad_kernel(side, r0, r1, r2, r3, g0, g1, g2, g3, out_ref):
    half = 8 * BLK
    x = jnp.concatenate(
        [r[SEG : 2 * SEG, side * half : (side + 1) * half] for r in (r0, r1, r2, r3)], axis=0
    )
    grads = jnp.concatenate([g[...] for g in (g0, g1, g2, g3)], axis=0)
    out_ref[...] = dot_tn(x, grads).astype(out_ref.dtype)


def weight_grad_half(side, pieces, grads, dtype):
    return pl.pallas_call(
        functools.partial(weight_grad_kernel, side),
        out_shape=jax.ShapeDtypeStruct((8 * BLK, grads[0].shape[1]), dtype),
        compiler_params=params(),
        cost_estimate=cost(2),
        name="weight_grad_half",
    )(*pieces, *grads)


def input_grad_kernel(g0, g1, g2, g3, wn_ref, wf_ref, o0, o1, o2, o3):
    grads = jnp.concatenate([g[...] for g in (g0, g1, g2, g3)], axis=0)
    near = dot_nt(grads, wn_ref[...]).astype(BF16)
    far = dot_nt(grads, wf_ref[...]).astype(BF16)
    both = jnp.concatenate([near, far], axis=1)
    for k, out in enumerate((o0, o1, o2, o3)):
        out[...] = both[k * SEG : (k + 1) * SEG]


def input_grad_pieces(grads, near, far):
    return pl.pallas_call(
        input_grad_kernel,
        out_shape=[jax.ShapeDtypeStruct((SEG, 16 * BLK), BF16)] * 4,
        compiler_params=params(),
        cost_estimate=cost(2),
        name="input_grad_pieces",
    )(*grads, near, far)


def shards(fwd_x, fwd_q, bwd_x, bwd_q, bwd_dout, cache_kv, kv_weight, seg_lengths):
    shard = kv_weight[0]
    lengths = seg_lengths[0, 0]
    cache = cache_kv[0, 0]
    front_q, back_q, back_dout = fwd_q[0, 0], bwd_q[0, 0], bwd_dout[0, 0]
    d = lax.axis_index("dp")
    pos = jnp.stack([d // 32, (d // 8) % 4, (d // 2) % 4, d % 2]).astype(jnp.int32)

    pair = jnp.concatenate([shard, move(shard, z=1)], axis=0)
    split = split_inputs(pos, fwd_x[0, 0], bwd_x[0, 0])
    pieces = [split[0]] + [move(split[k], x=k) for k in (1, 2, 3)]

    gq0, dk0, dv0 = backward_groups(lengths, back_q, back_dout, cache, 0, 2)
    near = jnp.concatenate([pair] + [move(pair, y=k) for k in (1, 2, 3)], axis=0)
    gq1, dk1, dv1 = backward_groups(lengths, back_q, back_dout, cache, 2, 2)
    far = move(near, c=1)
    grad_query = jnp.concatenate([gq0, gq1], axis=1)
    kv_grad = jnp.concatenate([dk0, dk1, dv0, dv1], axis=1)
    grads = [kv_grad] + [move(kv_grad, x=k) for k in (1, 2, 3)]

    own_parts = own_kv_parts(pieces, near, far)
    parts = [own_parts[0]] + [move(own_parts[k], x=-k) for k in (1, 2, 3)]
    acc, stat = stored_groups(lengths, front_q, cache, 0, 4)

    away = weight_grad_half(1, pieces, grads, BF16)
    swapped = move(away, c=1)
    home = weight_grad_half(0, pieces, grads, F32)
    backs = input_grad_pieces(grads, near, far)
    backs = [move_back_section(backs[k], x=-k) for k in range(4)]

    summed = home + swapped.astype(F32)
    rows = 2 * BLK
    held = summed[:rows]
    for k in (1, 2, 3):
        held = held + move(summed[k * rows : (k + 1) * rows].astype(BF16), y=-k).astype(F32)
    weight_grad = held[:BLK] + move(held[BLK:].astype(BF16), z=1).astype(F32)

    fwd_out = own_groups(lengths, front_q, parts, acc, stat)
    next_act = lax.ppermute(fwd_out, "pipe", [(p, p + 1) for p in range(3)])
    prev_grad = join_pieces(pos, backs)
    return (next_act[None, None], grad_query[None, None], prev_grad[None, None], weight_grad[None])


def solution(mesh):
    return jax.shard_map(
        shards,
        mesh=mesh,
        in_specs=(
            P("pipe", "dp", None, None),
            P("pipe", "dp", None, None),
            P("pipe", "dp", None, None),
            P("pipe", "dp", None, None),
            P("pipe", "dp", None, None),
            P("pipe", "dp", None, None),
            P("pipe", "dp", None),
            P("pipe", "dp", None),
        ),
        out_specs=(
            P("pipe", "dp", None, None),
            P("pipe", "dp", None, None),
            P("pipe", "dp", None, None),
            P("pipe", "dp", None),
        ),
        check_vma=False,
    )
```

time: 573 us -> 103 us (0.18)
  waiting for transfers between devices: 455 us -> 20.5 us
  starting transfers between devices: 6.8 us -> 47.7 us
  local copies, waits for them, and re-layouts: 44.1 us -> 5.23 us
  matrix products: 38.3 us -> 0 us
  Pallas kernels: 0 us -> 26.3 us
  between operations: 15.9 us -> 1.01 us
    unnamed x3 -> x0, waiting for transfers between devices: 394 us -> none
    all_gather x1 -> x0, waiting for transfers between devices: 47.4 us -> none  [shards(): lax.all_gather(shard, 'dp', axis=0, tiled=True)]
    ppermute x2 -> x24, starting transfers between devices: 6.73 us -> 47.7 us  [the longest x19 32.6 us: move(): lax.ppermute(value, 'dp', [(d, dp_target(d, **steps)) for d in range(64)])]
    dot_general x35 -> x0, matrix products: 38.3 us -> none  [the longest x1 7.54 us: shards(): jnp.dot(columns.T, kv_grad, preferred_element_type=jnp.float32)]
    pallas_call x0 -> x10, Pallas kernels: none -> 26.3 us  [the longest x2 9.57 us: backward_groups(): pl.pallas_call(backward_kernel, grid=(count,), out_shape=[jax.ShapeDtypeS...]
    unnamed x51 -> x28, local copies, waits for them, and re-layouts: 25.1 us -> 5.14 us
    reshape x16 -> x0, local copies, waits for them, and re-layouts: 10.2 us -> none  [the longest x4 3.25 us: forward_segment(): pieces.append(mixed.reshape(seg, group * HD))]
    ppermute x2 -> x24, waiting for transfers between devices: 13.6 us -> 20.5 us  [the longest x19 19.6 us: move(): lax.ppermute(value, 'dp', [(d, dp_target(d, **steps)) for d in range(64)])]
  transfers between devices with their start and end apart: 4 -> 24, of which waited for: 3 -> 6; matrix products, arithmetic and copies ran while one was open for 14% -> 2% of each run, Pallas kernels for 0% -> 16%
where the time goes in v1:
time: 103 us
  starting transfers between devices  47.7 us (46%)
  Pallas kernels  26.3 us (26%)
  waiting for transfers between devices  20.5 us (20%)
  local copies, waits for them, and re-layouts  5.23 us (5%)
  other arithmetic  2.11 us (2%)
    ppermute x19, starting transfers between devices, move(): lax.ppermute(value, 'dp', [(d, dp_target(d, **steps)) for d in range(64)])  32.6 us
    ppermute x19, waiting for transfers between devices, move(): lax.ppermute(value, 'dp', [(d, dp_target(d, **steps)) for d in range(64)])  19.6 us
    ppermute x4, starting transfers between devices, move_back_section(): return lax.ppermute(value, ('dp', 'pipe'), pairs)  11 us
    pallas_call x2, Pallas kernels, backward_groups(): pl.pallas_call(backward_kernel, grid=(count,), out_shape=[jax.ShapeDtypeS...  9.57 us
    pallas_call x1, Pallas kernels, stored_groups(): pl.pallas_call(stored_kernel, grid=(count,), out_shape=[jax.ShapeDtypeStr...  6.38 us
    unnamed x28, local copies, waits for them, and re-layouts  5.14 us
    ppermute x1, starting transfers between devices, shards(): next_act = lax.ppermute(fwd_out, 'pipe', [(p, p + 1) for p in range(3)])  4.1 us
    pallas_call x1, Pallas kernels, own_groups(): pl.pallas_call(own_kernel, grid=(4,), out_shape=jax.ShapeDtypeStruct((SEG...  3.46 us
  transfers between devices with their start and end apart: 24, of which 6 were waited for; matrix products, arithmetic and copies ran while one was open for 2% of the time, Pallas kernels for 16%

profile of v1, /device:TPU:64, one launch (start us, length us, event | category | flops | bytes accessed | tf_op | source)
XLA Modules:
  0.0 102.8 jit_solution(14951277829887099150)
XLA Ops:
  0.6 1.6 %copy-done = bf16[1,1,1024,1024]{3,2,1,0:T(8,128)(2,1)S(1)} copy-done((bf16[1,1,1024,1024]{3,2,1,0:T(8,128)(2,1)S(1)}, bf16[1,1,1024,1024]{3,2,1,0:T(8,128)(2,1)}, u32[]{:S(2)}) %copy-start) | copy-done | bytes 2097176
  2.2 1.0 copy-done.2
  3.2 1.0 copy-done.3
  4.3 0.7 copy-done.7
  4.9 4.8 %backward_groups.3 = (bf16[64,1792]{1,0:T(8,128)(2,1)S(1)}, bf16[64,256]{1,0:T(8,128)(2,1)S(1)}, bf16[64,256]{1,0:T(8,128)(2,1)S(1)}) custom-call(s32[4]{0:T(128)S(1)} %bitcast.33, bf16[64,3584]{1,0:T(8,128)(2,1)S(1)} %bitcast.25, bf16[64,3584]{1,0:T(8,128)(2,1)S(1)} %bitcast.27, bf16[1024,1024]{1,0:T(8,128)(2,1)S(1)} %bitcast.19, ...), custom_call_target="tpu_custom_call" | custom-call | flops 8000000000 | bytes 8000000 | tf_op jit(solution)/shard_map/backward_groups/pallas_call | solution.py:177
  9.7 4.8 %backward_groups.2 = (bf16[64,1792]{1,0:T(8,128)(2,1)S(1)}, bf16[64,256]{1,0:T(8,128)(2,1)S(1)}, bf16[64,256]{1,0:T(8,128)(2,1)S(1)}) custom-call(s32[4]{0:T(128)S(1)} %bitcast.34, bf16[64,3584]{1,0:T(8,128)(2,1)S(1)} %bitcast.26, bf16[64,3584]{1,0:T(8,128)(2,1)S(1)} %bitcast.28, bf16[1024,1024]{1,0:T(8,128)(2,1)S(1)} %bitcast.21, ...), custom_call_target="tpu_custom_call" | custom-call | flops 8000000000 | bytes 8000000 | tf_op jit(solution)/shard_map/backward_groups/pallas_call | solution.py:177
  14.6 1.6 %collective-permute-start.12 = (bf16[64,1024]{1,0:T(8,128)(2,1)S(1)}, bf16[64,1024]{1,0:T(8,128)(2,1)S(1)}, u32[]{:S(2)}, u32[]{:S(2)}) collective-permute-start(bf16[64,1024]{1,0:T(8,128)(2,1)S(1)} %constant_dynamic-update-slice_fusion.5.g0), channel_id=1, source_target_pairs={{0,32},{4,36},{8,40},{12,44},{16,48},{20,52},{24,56},{28,60},{32,6... | collective-permute-start | bytes 393224 | tf_op jit(solution)/shard_map/ppermute | solution.py:40
  16.1 2.7 %collective-permute-start.13 = (bf16[64,1024]{1,0:T(8,128)(2,1)S(1)}, bf16[64,1024]{1,0:T(8,128)(2,1)S(1)}, u32[]{:S(2)}, u32[]{:S(2)}) collective-permute-start(bf16[64,1024]{1,0:T(8,128)(2,1)S(1)} %constant_dynamic-update-slice_fusion.5.g0), channel_id=1, source_target_pairs={{0,64},{4,68},{8,72},{12,76},{16,80},{20,84},{24,88},{28,92},{32,9... | collective-permute-start | bytes 393224 | tf_op jit(solution)/shard_map/ppermute | solution.py:40
  18.9 1.4 %collective-permute-start.14 = (bf16[64,1024]{1,0:T(8,128)(2,1)S(1)}, bf16[64,1024]{1,0:T(8,128)(2,1)S(1)}, u32[]{:S(2)}, u32[]{:S(2)}) collective-permute-start(bf16[64,1024]{1,0:T(8,128)(2,1)S(1)} %constant_dynamic-update-slice_fusion.5.g0), channel_id=1, source_target_pairs={{0,96},{4,100},{8,104},{12,108},{16,112},{20,116},{24,120},{28,124... | collective-permute-start | bytes 393224 | tf_op jit(solution)/shard_map/ppermute | solution.py:40
  20.4 2.2 %split_inputs.1 = (bf16[128,896]{1,0:T(8,128)(2,1)S(1)}, bf16[128,896]{1,0:T(8,128)(2,1)S(1)}, bf16[128,896]{1,0:T(8,128)(2,1)S(1)}, bf16[128,896]{1,0:T(8,128)(2,1)S(1)}) custom-call(s32[4]{0:T(128)S(1)} %pad_add_fusion.pos_ref, bf16[64,3584]{1,0:T(8,128)(2,1)S(1)} %bitcast.29, bf16[64,3584]{1,0:T(8,128)(2,1)S(1)} %bitcast.30), custom_call_target="tpu_custom_call" | custom-call | flops 3000000000 | bytes 3000000 | tf_op jit(solution)/shard_map/split_inputs/pallas_call | solution.py:72
  22.6 0.7 collective-permute-start
  23.3 5.4 %collective-permute-start.3 = (bf16[56,1024]{1,0:T(8,128)(2,1)S(1)}, bf16[56,1024]{1,0:T(8,128)(2,1)S(1)}, u32[]{:S(2)}, u32[]{:S(2)}) collective-permute-start(bf16[56,1024]{1,0:T(8,128)(2,1)S(1)} %bitcast.37), channel_id=1, source_target_pairs={{0,128},{4,132},{8,136},{12,140},{16,144},{20,148},{24,152},{28,15... | collective-permute-start | bytes 344072 | tf_op jit(solution)/shard_map/ppermute | solution.py:40
  28.7 6.4 %stored_groups.1 = (f32[64,3584]{1,0:T(8,128)S(1)}, f32[64,512]{1,0:T(8,128)S(1)}) custom-call(s32[4]{0:T(128)S(1)} %bitcast.35, bf16[64,3584]{1,0:T(8,128)(2,1)S(1)} %bitcast.31, bf16[1024,1024]{1,0:T(8,128)(2,1)S(1)} %bitcast.23, bf16[1024,1024]{1,0:T(8,128)(2,1)S(1)} %bitcast.24), custom_call_target="tpu_custom_call" | custom-call | flops 8000000000 | bytes 8000000 | tf_op jit(solution)/shard_map/stored_groups/pallas_call | solution.py:220
  35.1 1.0 collective-permute-start.1
  36.1 1.9 %collective-permute-start.2 = (bf16[128,896]{1,0:T(8,128)(2,1)S(1)}, bf16[128,896]{1,0:T(8,128)(2,1)S(1)}, u32[]{:S(2)}, u32[]{:S(2)}) collective-permute-start(bf16[128,896]{1,0:T(8,128)(2,1)S(1)} %get-tuple-element.27), channel_id=1, source_target_pairs={{0,96},{4,100},{8,104},{12,108},{16,112},{20,116},{24,120},{28,124... | collective-permute-start | bytes 688136 | tf_op jit(solution)/shard_map/ppermute | solution.py:40
  38.0 1.8 %collective-permute-start.4 = (bf16[112,1024]{1,0:T(8,128)(2,1)S(1)}, bf16[112,1024]{1,0:T(8,128)(2,1)S(1)}, u32[]{:S(2)}, u32[]{:S(2)}) collective-permute-start(bf16[112,1024]{1,0:T(8,128)(2,1)S(1)} %pad_maximum_fusion), channel_id=1, source_target_pairs={{0,8},{4,12},{8,16},{12,20},{16,24},{20,28},{24,0},{28,4},{32,40},... | collective-permute-start | bytes 688136 | tf_op jit(solution)/shard_map/ppermute | solution.py:40
  39.9 3.0 %collective-permute-start.5 = (bf16[112,1024]{1,0:T(8,128)(2,1)S(1)}, bf16[112,1024]{1,0:T(8,128)(2,1)S(1)}, u32[]{:S(2)}, u32[]{:S(2)}) collective-permute-start(bf16[112,1024]{1,0:T(8,128)(2,1)S(1)} %pad_maximum_fusion), channel_id=1, source_target_pairs={{0,16},{4,20},{8,24},{12,28},{16,0},{20,4},{24,8},{28,12},{32,48},... | collective-permute-start | bytes 688136 | tf_op jit(solution)/shard_map/ppermute | solution.py:40
  42.9 1.3 %collective-permute-start.6 = (bf16[112,1024]{1,0:T(8,128)(2,1)S(1)}, bf16[112,1024]{1,0:T(8,128)(2,1)S(1)}, u32[]{:S(2)}, u32[]{:S(2)}) collective-permute-start(bf16[112,1024]{1,0:T(8,128)(2,1)S(1)} %pad_maximum_fusion), channel_id=1, source_target_pairs={{0,24},{4,28},{8,0},{12,4},{16,8},{20,12},{24,16},{28,20},{32,56},... | collective-permute-start | bytes 688136 | tf_op jit(solution)/shard_map/ppermute | solution.py:40
  44.2 3.4 %collective-permute-done.2.r3 = bf16[128,896]{1,0:T(8,128)(2,1)S(1)} collective-permute-done((bf16[128,896]{1,0:T(8,128)(2,1)S(1)}, bf16[128,896]{1,0:T(8,128)(2,1)S(1)}, u32[]{:S(2)}, u32[]{:S(2)}) %collective-permute-start.2) | collective-permute-done | bytes 229408 | tf_op jit(solution)/shard_map/ppermute | solution.py:40
  47.6 0.5 weight_grad_half.3
  48.1 0.1 collective-permute-start.19
  48.3 3.0 %collective-permute-done.5 = bf16[112,1024]{1,0:T(8,128)(2,1)S(1)} collective-permute-done((bf16[112,1024]{1,0:T(8,128)(2,1)S(1)}, bf16[112,1024]{1,0:T(8,128)(2,1)S(1)}, u32[]{:S(2)}, u32[]{:S(2)}) %collective-permute-start.5) | collective-permute-done | bytes 229408 | tf_op jit(solution)/shard_map/ppermute | solution.py:40
  51.5 0.8 maximum_bitcast_fusion
  52.3 0.4 weight_grad_half.2
  52.7 0.4 fusion.3
  53.1 1.3 %collective-permute-start.22 = (bf16[112,1024]{1,0:T(8,128)(2,1)S(1)}, bf16[112,1024]{1,0:T(8,128)(2,1)S(1)}, u32[]{:S(2)}, u32[]{:S(2)}) collective-permute-start(bf16[112,1024]{1,0:T(8,128)(2,1)S(1)} %get-tuple-element.47), channel_id=1, source_target_pairs={{0,8},{4,12},{8,16},{12,20},{16,24},{20,28},{24,0},{28,4},{32,40},... | collective-permute-start | bytes 688136 | tf_op jit(solution)/shard_map/ppermute | solution.py:40
  54.5 2.4 %collective-permute-start.21 = (bf16[112,1024]{1,0:T(8,128)(2,1)S(1)}, bf16[112,1024]{1,0:T(8,128)(2,1)S(1)}, u32[]{:S(2)}, u32[]{:S(2)}) collective-permute-start(bf16[112,1024]{1,0:T(8,128)(2,1)S(1)} %get-tuple-element.48), channel_id=1, source_target_pairs={{0,16},{4,20},{8,24},{12,28},{16,0},{20,4},{24,8},{28,12},{32,48},... | collective-permute-start | bytes 688136 | tf_op jit(solution)/shard_map/ppermute | solution.py:40
  56.8 0.8 own_kv_parts.1
  57.6 1.4 %collective-permute-start.8 = (bf16[64,1024]{1,0:T(8,128)(2,1)S(1)}, bf16[64,1024]{1,0:T(8,128)(2,1)S(1)}, u32[]{:S(2)}, u32[]{:S(2)}) collective-permute-start(bf16[64,1024]{1,0:T(8,128)(2,1)S(1)} %get-tuple-element.29), channel_id=1, source_target_pairs={{0,96},{4,100},{8,104},{12,108},{16,112},{20,116},{24,120},{28,124... | collective-permute-start | bytes 393224 | tf_op jit(solution)/shard_map/ppermute | solution.py:40
  59.0 1.5 %collective-permute-start.9 = (bf16[64,1024]{1,0:T(8,128)(2,1)S(1)}, bf16[64,1024]{1,0:T(8,128)(2,1)S(1)}, u32[]{:S(2)}, u32[]{:S(2)}) collective-permute-start(bf16[64,1024]{1,0:T(8,128)(2,1)S(1)} %get-tuple-element.30), channel_id=1, source_target_pairs={{0,64},{4,68},{8,72},{12,76},{16,80},{20,84},{24,88},{28,92},{32,9... | collective-permute-start | bytes 393224 | tf_op jit(solution)/shard_map/ppermute | solution.py:40
  60.5 1.1 %collective-permute-start.10 = (bf16[64,1024]{1,0:T(8,128)(2,1)S(1)}, bf16[64,1024]{1,0:T(8,128)(2,1)S(1)}, u32[]{:S(2)}, u32[]{:S(2)}) collective-permute-start(bf16[64,1024]{1,0:T(8,128)(2,1)S(1)} %get-tuple-element.31), channel_id=1, source_target_pairs={{0,32},{4,36},{8,40},{12,44},{16,48},{20,52},{24,56},{28,60},{32,6... | collective-permute-start | bytes 393224 | tf_op jit(solution)/shard_map/ppermute | solution.py:40
  61.6 0.8 input_grad_pieces.1
  62.4 1.6 %collective-permute-done.8.k1.v1 = bf16[64,1024]{1,0:T(8,128)(2,1)S(1)} collective-permute-done((bf16[64,1024]{1,0:T(8,128)(2,1)S(1)}, bf16[64,1024]{1,0:T(8,128)(2,1)S(1)}, u32[]{:S(2)}, u32[]{:S(2)}) %collective-permute-start.8) | collective-permute-done | bytes 131104 | tf_op jit(solution)/shard_map/ppermute | solution.py:40
  64.1 1.7 %collective-permute-start.20 = (bf16[112,1024]{1,0:T(8,128)(2,1)S(1)}, bf16[112,1024]{1,0:T(8,128)(2,1)S(1)}, u32[]{:S(2)}, u32[]{:S(2)}) collective-permute-start(bf16[112,1024]{1,0:T(8,128)(2,1)S(1)} %get-tuple-element.46), channel_id=1, source_target_pairs={{0,24},{4,28},{8,0},{12,4},{16,8},{20,12},{24,16},{28,20},{32,56},... | collective-permute-start | bytes 688136 | tf_op jit(solution)/shard_map/ppermute | solution.py:40
  65.7 1.0 collective-permute-done.9.k2.v2
  66.7 2.9 %collective-permute-start.15 = (bf16[64,896]{1,0:T(8,128)(2,1)S(1)}, bf16[64,896]{1,0:T(8,128)(2,1)S(1)}, u32[]{:S(2)}, u32[]{:S(2)}) collective-permute-start(bf16[64,896]{1,0:T(8,128)(2,1)S(1)} %get-tuple-element.40), channel_id=1, source_target_pairs={{1,0},{2,1},{3,2},{5,4},{6,5},{7,6},{9,8},{10,9},{11,10},{13,12},{... | collective-permute-start | bytes 344072 | tf_op jit(solution)/shard_map/ppermute | solution.py:47
  69.6 4.1 %collective-permute-start.16 = (bf16[64,896]{1,0:T(8,128)(2,1)S(1)}, bf16[64,896]{1,0:T(8,128)(2,1)S(1)}, u32[]{:S(2)}, u32[]{:S(2)}) collective-permute-start(bf16[64,896]{1,0:T(8,128)(2,1)S(1)} %get-tuple-element.41), channel_id=1, source_target_pairs={{1,96},{2,97},{3,98},{5,100},{6,101},{7,102},{9,104},{10,105},{11,... | collective-permute-start | bytes 344072 | tf_op jit(solution)/shard_map/ppermute | solution.py:47
  73.8 3.5 %own_groups.1 = bf16[64,3584]{1,0:T(8,128)(2,1)S(1)} custom-call(s32[4]{0:T(128)S(1)} %bitcast.36, bf16[64,3584]{1,0:T(8,128)(2,1)S(1)} %bitcast.32, f32[64,1024]{1,0:T(8,128)S(1)} %get-tuple-element.28.k0.v0, bf16[64,1024]{1,0:T(8,128)(2,1)S(1)} %collective-permute-done.8.k1.v1, bf16[64,1024]{1,0:T(8,128)(2,1)S(1)} %collective-permute-done.9.k2.v2, ...), custom_call_target="tpu_custom_call" | custom-call | flops 4000000000 | bytes 4000000 | tf_op jit(solution)/shard_map/own_groups/pallas_call | solution.py:265
  77.3 2.0 %collective-permute-start.17 = (bf16[64,896]{1,0:T(8,128)(2,1)S(1)}, bf16[64,896]{1,0:T(8,128)(2,1)S(1)}, u32[]{:S(2)}, u32[]{:S(2)}) collective-permute-start(bf16[64,896]{1,0:T(8,128)(2,1)S(1)} %get-tuple-element.42), channel_id=1, source_target_pairs={{1,64},{2,65},{3,66},{5,68},{6,69},{7,70},{9,72},{10,73},{11,74},{... | collective-permute-start | bytes 344072 | tf_op jit(solution)/shard_map/ppermute | solution.py:47
  79.3 1.9 %collective-permute-start.18 = (bf16[64,896]{1,0:T(8,128)(2,1)S(1)}, bf16[64,896]{1,0:T(8,128)(2,1)S(1)}, u32[]{:S(2)}, u32[]{:S(2)}) collective-permute-start(bf16[64,896]{1,0:T(8,128)(2,1)S(1)} %get-tuple-element.43), channel_id=1, source_target_pairs={{1,32},{2,33},{3,34},{5,36},{6,37},{7,38},{9,40},{10,41},{11,42},{... | collective-permute-start | bytes 344072 | tf_op jit(solution)/shard_map/ppermute | solution.py:47
  81.2 4.1 %collective-permute-start.11 = (bf16[64,3584]{1,0:T(8,128)(2,1)S(1)}, bf16[64,3584]{1,0:T(8,128)(2,1)S(1)}, u32[]{:S(2)}, u32[]{:S(2)}) collective-permute-start(bf16[64,3584]{1,0:T(8,128)(2,1)S(1)} %own_groups.1), channel_id=1, source_target_pairs={{0,1},{1,2},{2,3},{4,5},{5,6},{6,7},{8,9},{9,10},{10,11},{12,13},{... | collective-permute-start | bytes 1376264 | tf_op jit(solution)/shard_map/ppermute | solution.py:375
  85.4 0.1 fusion.1
  85.5 2.2 %collective-permute-start.23 = (bf16[56,1024]{1,0:T(8,128)(2,1)S(1)}, bf16[56,1024]{1,0:T(8,128)(2,1)S(1)}, u32[]{:S(2)}, u32[]{:S(2)}) collective-permute-start(bf16[56,1024]{1,0:T(8,128)(2,1)S(1)} %slice.43), channel_id=1, source_target_pairs={{0,128},{4,132},{8,136},{12,140},{16,144},{20,148},{24,152},{28,15... | collective-permute-start | bytes 344072 | tf_op jit(solution)/shard_map/ppermute | solution.py:40
  87.7 0.9 collective-permute-done.18.g3
  88.6 2.2 %join_pieces.1 = bf16[64,3584]{1,0:T(8,128)(2,1)} custom-call(s32[4]{0:T(128)S(1)} %pad_add_fusion.pos_ref, bf16[64,896]{1,0:T(8,128)(2,1)S(1)} %collective-permute-done.15.g0, bf16[64,896]{1,0:T(8,128)(2,1)S(1)} %collective-permute-done.16.g1, bf16[64,896]{1,0:T(8,128)(2,1)S(1)} %collective-permute-done.17.g2, bf16[64,896]{1,0:T(8,128)(2,1)S(1)} %collective-permute-done.18.g3), custom_call_target="tpu_custom_call" | custom-call | flops 2000000000 | bytes 2000000 | tf_op jit(solution)/shard_map/join_pieces/pallas_call | solution.py:97
  90.8 10.5 %collective-permute-done.23 = bf16[56,1024]{1,0:T(8,128)(2,1)S(1)} collective-permute-done((bf16[56,1024]{1,0:T(8,128)(2,1)S(1)}, bf16[56,1024]{1,0:T(8,128)(2,1)S(1)}, u32[]{:S(2)}, u32[]{:S(2)}) %collective-permute-start.23) | collective-permute-done | bytes 114720 | tf_op jit(solution)/shard_map/ppermute | solution.py:40
  101.3 0.7 fusion.2
  102.0 0.8 copy.20
  (48 shorter events, 0.4 us)
Async XLA Ops:
  0.6 1.6 %copy-start = (bf16[1,1,1024,1024]{3,2,1,0:T(8,128)(2,1)S(1)}, bf16[1,1,1024,1024]{3,2,1,0:T(8,128)(2,1)}, u32[]{:S(2)}) copy-start(bf16[1,1,1024,1024]{3,2,1,0:T(8,128)(2,1)} %param.13) | copy-start | bytes 6291460
  2.2 1.0 copy-start.2
  3.2 1.0 copy-start.3
  4.3 0.7 copy-start.7
  9.7 10.7 %copy-start.4 = (bf16[1,1,64,3584]{3,2,1,0:T(8,128)(2,1)S(1)}, bf16[1,1,64,3584]{3,2,1,0:T(8,128)(2,1)}, u32[]{:S(2)}) copy-start(bf16[1,1,64,3584]{3,2,1,0:T(8,128)(2,1)} %param.8) | copy-start | bytes 1376260
  9.7 10.7 %copy-start.5 = (bf16[1,1,64,3584]{3,2,1,0:T(8,128)(2,1)S(1)}, bf16[1,1,64,3584]{3,2,1,0:T(8,128)(2,1)}, u32[]{:S(2)}) copy-start(bf16[1,1,64,3584]{3,2,1,0:T(8,128)(2,1)} %param.10) | copy-start | bytes 1376260
  14.6 21.5 %collective-permute-start.12 = (bf16[64,1024]{1,0:T(8,128)(2,1)S(1)}, bf16[64,1024]{1,0:T(8,128)(2,1)S(1)}, u32[]{:S(2)}, u32[]{:S(2)}) collective-permute-start(bf16[64,1024]{1,0:T(8,128)(2,1)S(1)} %constant_dynamic-update-slice_fusion.5.g0), channel_id=1, source_target_pairs={{0,32},{4,36},{8,40},{12,44},{16,48},{20,52},{24,56},{28,60},{32,6... | collective-permute-start | bytes 393224 | tf_op jit(solution)/shard_map/ppermute | solution.py:40
  16.1 21.9 %collective-permute-start.13 = (bf16[64,1024]{1,0:T(8,128)(2,1)S(1)}, bf16[64,1024]{1,0:T(8,128)(2,1)S(1)}, u32[]{:S(2)}, u32[]{:S(2)}) collective-permute-start(bf16[64,1024]{1,0:T(8,128)(2,1)S(1)} %constant_dynamic-update-slice_fusion.5.g0), channel_id=1, source_target_pairs={{0,64},{4,68},{8,72},{12,76},{16,80},{20,84},{24,88},{28,92},{32,9... | collective-permute-start | bytes 393224 | tf_op jit(solution)/shard_map/ppermute | solution.py:40
  18.9 21.0 %collective-permute-start.14 = (bf16[64,1024]{1,0:T(8,128)(2,1)S(1)}, bf16[64,1024]{1,0:T(8,128)(2,1)S(1)}, u32[]{:S(2)}, u32[]{:S(2)}) collective-permute-start(bf16[64,1024]{1,0:T(8,128)(2,1)S(1)} %constant_dynamic-update-slice_fusion.5.g0), channel_id=1, source_target_pairs={{0,96},{4,100},{8,104},{12,108},{16,112},{20,116},{24,120},{28,124... | collective-permute-start | bytes 393224 | tf_op jit(solution)/shard_map/ppermute | solution.py:40
  20.4 2.9 %copy-start.9 = (bf16[1,56,1024]{2,1,0:T(8,128)(2,1)S(1)}, bf16[1,56,1024]{2,1,0:T(8,128)(2,1)}, u32[]{:S(2)}) copy-start(bf16[1,56,1024]{2,1,0:T(8,128)(2,1)} %param.14) | copy-start | bytes 344068
  20.4 8.3 %copy-start.1 = (bf16[1,1,1024,1024]{3,2,1,0:T(8,128)(2,1)S(1)}, bf16[1,1,1024,1024]{3,2,1,0:T(8,128)(2,1)}, u32[]{:S(2)}) copy-start(bf16[1,1,1024,1024]{3,2,1,0:T(8,128)(2,1)} %param.13) | copy-start | bytes 6291460
  20.4 8.3 %copy-start.6 = (bf16[1,1,64,3584]{3,2,1,0:T(8,128)(2,1)S(1)}, bf16[1,1,64,3584]{3,2,1,0:T(8,128)(2,1)}, u32[]{:S(2)}) copy-start(bf16[1,1,64,3584]{3,2,1,0:T(8,128)(2,1)} %param.9) | copy-start | bytes 1376260
  20.4 8.3 %copy-start.8 = (s32[1,1,4]{2,1,0:T(1,128)S(1)}, s32[1,1,4]{2,1,0:T(1,128)}, u32[]{:S(2)}) copy-start(s32[1,1,4]{2,1,0:T(1,128)} %param.15) | copy-start | bytes 52
  22.6 20.2 %collective-permute-start = (bf16[128,896]{1,0:T(8,128)(2,1)S(1)}, bf16[128,896]{1,0:T(8,128)(2,1)S(1)}, u32[]{:S(2)}, u32[]{:S(2)}) collective-permute-start(bf16[128,896]{1,0:T(8,128)(2,1)S(1)} %get-tuple-element.25), channel_id=1, source_target_pairs={{0,32},{4,36},{8,40},{12,44},{16,48},{20,52},{24,56},{28,60},{32,6... | collective-permute-start | bytes 688136 | tf_op jit(solution)/shard_map/ppermute | solution.py:40
  23.3 11.8 %collective-permute-start.3 = (bf16[56,1024]{1,0:T(8,128)(2,1)S(1)}, bf16[56,1024]{1,0:T(8,128)(2,1)S(1)}, u32[]{:S(2)}, u32[]{:S(2)}) collective-permute-start(bf16[56,1024]{1,0:T(8,128)(2,1)S(1)} %bitcast.37), channel_id=1, source_target_pairs={{0,128},{4,132},{8,136},{12,140},{16,144},{20,148},{24,152},{28,15... | collective-permute-start | bytes 344072 | tf_op jit(solution)/shard_map/ppermute | solution.py:40
  35.1 9.1 %collective-permute-start.1 = (bf16[128,896]{1,0:T(8,128)(2,1)S(1)}, bf16[128,896]{1,0:T(8,128)(2,1)S(1)}, u32[]{:S(2)}, u32[]{:S(2)}) collective-permute-start(bf16[128,896]{1,0:T(8,128)(2,1)S(1)} %get-tuple-element.26), channel_id=1, source_target_pairs={{0,64},{4,68},{8,72},{12,76},{16,80},{20,84},{24,88},{28,92},{32,9... | collective-permute-start | bytes 688136 | tf_op jit(solution)/shard_map/ppermute | solution.py:40
  36.1 11.5 %collective-permute-start.2 = (bf16[128,896]{1,0:T(8,128)(2,1)S(1)}, bf16[128,896]{1,0:T(8,128)(2,1)S(1)}, u32[]{:S(2)}, u32[]{:S(2)}) collective-permute-start(bf16[128,896]{1,0:T(8,128)(2,1)S(1)} %get-tuple-element.27), channel_id=1, source_target_pairs={{0,96},{4,100},{8,104},{12,108},{16,112},{20,116},{24,120},{28,124... | collective-permute-start | bytes 688136 | tf_op jit(solution)/shard_map/ppermute | solution.py:40
  38.0 10.2 %collective-permute-start.4 = (bf16[112,1024]{1,0:T(8,128)(2,1)S(1)}, bf16[112,1024]{1,0:T(8,128)(2,1)S(1)}, u32[]{:S(2)}, u32[]{:S(2)}) collective-permute-start(bf16[112,1024]{1,0:T(8,128)(2,1)S(1)} %pad_maximum_fusion), channel_id=1, source_target_pairs={{0,8},{4,12},{8,16},{12,20},{16,24},{20,28},{24,0},{28,4},{32,40},... | collective-permute-start | bytes 688136 | tf_op jit(solution)/shard_map/ppermute | solution.py:40
  39.9 11.4 %collective-permute-start.5 = (bf16[112,1024]{1,0:T(8,128)(2,1)S(1)}, bf16[112,1024]{1,0:T(8,128)(2,1)S(1)}, u32[]{:S(2)}, u32[]{:S(2)}) collective-permute-start(bf16[112,1024]{1,0:T(8,128)(2,1)S(1)} %pad_maximum_fusion), channel_id=1, source_target_pairs={{0,16},{4,20},{8,24},{12,28},{16,0},{20,4},{24,8},{28,12},{32,48},... | collective-permute-start | bytes 688136 | tf_op jit(solution)/shard_map/ppermute | solution.py:40
  42.9 8.5 %collective-permute-start.6 = (bf16[112,1024]{1,0:T(8,128)(2,1)S(1)}, bf16[112,1024]{1,0:T(8,128)(2,1)S(1)}, u32[]{:S(2)}, u32[]{:S(2)}) collective-permute-start(bf16[112,1024]{1,0:T(8,128)(2,1)S(1)} %pad_maximum_fusion), channel_id=1, source_target_pairs={{0,24},{4,28},{8,0},{12,4},{16,8},{20,12},{24,16},{28,20},{32,56},... | collective-permute-start | bytes 688136 | tf_op jit(solution)/shard_map/ppermute | solution.py:40
  48.1 4.6 %collective-permute-start.19 = (bf16[448,1024]{1,0:T(8,128)(2,1)S(1)}, bf16[448,1024]{1,0:T(8,128)(2,1)S(1)}, u32[]{:S(2)}, u32[]{:S(2)}) collective-permute-start(bf16[448,1024]{1,0:T(8,128)(2,1)S(1)} %weight_grad_half.3), channel_id=1, source_target_pairs={{0,4},{4,0},{8,12},{12,8},{16,20},{20,16},{24,28},{28,24},{32,36},... | collective-permute-start | bytes 2752520 | tf_op jit(solution)/shard_map/ppermute | solution.py:40
  51.4 5.5 %collective-permute-start.7 = (bf16[448,1024]{1,0:T(8,128)(2,1)S(1)}, bf16[448,1024]{1,0:T(8,128)(2,1)S(1)}, u32[]{:S(2)}, u32[]{:S(2)}) collective-permute-start(bf16[448,1024]{1,0:T(8,128)(2,1)S(1)} %constant_dynamic-update-slice_fusion.wn_ref), channel_id=1, source_target_pairs={{0,4},{4,0},{8,12},{12,8},{16,20},{20,16},{24,28},{28,24},{32,36},... | collective-permute-start | bytes 2752520 | tf_op jit(solution)/shard_map/ppermute | solution.py:40
  53.1 24.1 %collective-permute-start.22 = (bf16[112,1024]{1,0:T(8,128)(2,1)S(1)}, bf16[112,1024]{1,0:T(8,128)(2,1)S(1)}, u32[]{:S(2)}, u32[]{:S(2)}) collective-permute-start(bf16[112,1024]{1,0:T(8,128)(2,1)S(1)} %get-tuple-element.47), channel_id=1, source_target_pairs={{0,8},{4,12},{8,16},{12,20},{16,24},{20,28},{24,0},{28,4},{32,40},... | collective-permute-start | bytes 688136 | tf_op jit(solution)/shard_map/ppermute | solution.py:40
  54.5 24.8 %collective-permute-start.21 = (bf16[112,1024]{1,0:T(8,128)(2,1)S(1)}, bf16[112,1024]{1,0:T(8,128)(2,1)S(1)}, u32[]{:S(2)}, u32[]{:S(2)}) collective-permute-start(bf16[112,1024]{1,0:T(8,128)(2,1)S(1)} %get-tuple-element.48), channel_id=1, source_target_pairs={{0,16},{4,20},{8,24},{12,28},{16,0},{20,4},{24,8},{28,12},{32,48},... | collective-permute-start | bytes 688136 | tf_op jit(solution)/shard_map/ppermute | solution.py:40
  57.6 6.4 %collective-permute-start.8 = (bf16[64,1024]{1,0:T(8,128)(2,1)S(1)}, bf16[64,1024]{1,0:T(8,128)(2,1)S(1)}, u32[]{:S(2)}, u32[]{:S(2)}) collective-permute-start(bf16[64,1024]{1,0:T(8,128)(2,1)S(1)} %get-tuple-element.29), channel_id=1, source_target_pairs={{0,96},{4,100},{8,104},{12,108},{16,112},{20,116},{24,120},{28,124... | collective-permute-start | bytes 393224 | tf_op jit(solution)/shard_map/ppermute | solution.py:40
  59.0 7.7 %collective-permute-start.9 = (bf16[64,1024]{1,0:T(8,128)(2,1)S(1)}, bf16[64,1024]{1,0:T(8,128)(2,1)S(1)}, u32[]{:S(2)}, u32[]{:S(2)}) collective-permute-start(bf16[64,1024]{1,0:T(8,128)(2,1)S(1)} %get-tuple-element.30), channel_id=1, source_target_pairs={{0,64},{4,68},{8,72},{12,76},{16,80},{20,84},{24,88},{28,92},{32,9... | collective-permute-start | bytes 393224 | tf_op jit(solution)/shard_map/ppermute | solution.py:40
  60.5 9.1 %collective-permute-start.10 = (bf16[64,1024]{1,0:T(8,128)(2,1)S(1)}, bf16[64,1024]{1,0:T(8,128)(2,1)S(1)}, u32[]{:S(2)}, u32[]{:S(2)}) collective-permute-start(bf16[64,1024]{1,0:T(8,128)(2,1)S(1)} %get-tuple-element.31), channel_id=1, source_target_pairs={{0,32},{4,36},{8,40},{12,44},{16,48},{20,52},{24,56},{28,60},{32,6... | collective-permute-start | bytes 393224 | tf_op jit(solution)/shard_map/ppermute | solution.py:40
  64.1 17.2 %collective-permute-start.20 = (bf16[112,1024]{1,0:T(8,128)(2,1)S(1)}, bf16[112,1024]{1,0:T(8,128)(2,1)S(1)}, u32[]{:S(2)}, u32[]{:S(2)}) collective-permute-start(bf16[112,1024]{1,0:T(8,128)(2,1)S(1)} %get-tuple-element.46), channel_id=1, source_target_pairs={{0,24},{4,28},{8,0},{12,4},{16,8},{20,12},{24,16},{28,20},{32,56},... | collective-permute-start | bytes 688136 | tf_op jit(solution)/shard_map/ppermute | solution.py:40
  66.7 18.8 %collective-permute-start.15 = (bf16[64,896]{1,0:T(8,128)(2,1)S(1)}, bf16[64,896]{1,0:T(8,128)(2,1)S(1)}, u32[]{:S(2)}, u32[]{:S(2)}) collective-permute-start(bf16[64,896]{1,0:T(8,128)(2,1)S(1)} %get-tuple-element.40), channel_id=1, source_target_pairs={{1,0},{2,1},{3,2},{5,4},{6,5},{7,6},{9,8},{10,9},{11,10},{13,12},{... | collective-permute-start | bytes 344072 | tf_op jit(solution)/shard_map/ppermute | solution.py:47
  69.6 18.1 %collective-permute-start.16 = (bf16[64,896]{1,0:T(8,128)(2,1)S(1)}, bf16[64,896]{1,0:T(8,128)(2,1)S(1)}, u32[]{:S(2)}, u32[]{:S(2)}) collective-permute-start(bf16[64,896]{1,0:T(8,128)(2,1)S(1)} %get-tuple-element.41), channel_id=1, source_target_pairs={{1,96},{2,97},{3,98},{5,100},{6,101},{7,102},{9,104},{10,105},{11,... | collective-permute-start | bytes 344072 | tf_op jit(solution)/shard_map/ppermute | solution.py:47
  77.3 10.5 %collective-permute-start.17 = (bf16[64,896]{1,0:T(8,128)(2,1)S(1)}, bf16[64,896]{1,0:T(8,128)(2,1)S(1)}, u32[]{:S(2)}, u32[]{:S(2)}) collective-permute-start(bf16[64,896]{1,0:T(8,128)(2,1)S(1)} %get-tuple-element.42), channel_id=1, source_target_pairs={{1,64},{2,65},{3,66},{5,68},{6,69},{7,70},{9,72},{10,73},{11,74},{... | collective-permute-start | bytes 344072 | tf_op jit(solution)/shard_map/ppermute | solution.py:47
  79.3 9.3 %collective-permute-start.18 = (bf16[64,896]{1,0:T(8,128)(2,1)S(1)}, bf16[64,896]{1,0:T(8,128)(2,1)S(1)}, u32[]{:S(2)}, u32[]{:S(2)}) collective-permute-start(bf16[64,896]{1,0:T(8,128)(2,1)S(1)} %get-tuple-element.43), channel_id=1, source_target_pairs={{1,32},{2,33},{3,34},{5,36},{6,37},{7,38},{9,40},{10,41},{11,42},{... | collective-permute-start | bytes 344072 | tf_op jit(solution)/shard_map/ppermute | solution.py:47
  81.2 20.8 %collective-permute-start.11 = (bf16[64,3584]{1,0:T(8,128)(2,1)S(1)}, bf16[64,3584]{1,0:T(8,128)(2,1)S(1)}, u32[]{:S(2)}, u32[]{:S(2)}) collective-permute-start(bf16[64,3584]{1,0:T(8,128)(2,1)S(1)} %own_groups.1), channel_id=1, source_target_pairs={{0,1},{1,2},{2,3},{4,5},{5,6},{6,7},{8,9},{9,10},{10,11},{12,13},{... | collective-permute-start | bytes 1376264 | tf_op jit(solution)/shard_map/ppermute | solution.py:375
  85.5 15.8 %collective-permute-start.23 = (bf16[56,1024]{1,0:T(8,128)(2,1)S(1)}, bf16[56,1024]{1,0:T(8,128)(2,1)S(1)}, u32[]{:S(2)}, u32[]{:S(2)}) collective-permute-start(bf16[56,1024]{1,0:T(8,128)(2,1)S(1)} %slice.43), channel_id=1, source_target_pairs={{0,128},{4,132},{8,136},{12,140},{16,144},{20,148},{24,152},{28,15... | collective-permute-start | bytes 344072 | tf_op jit(solution)/shard_map/ppermute | solution.py:40

commit v2 on v0

v2 whole, which is shorter than its diff:
```python
import functools
import math

import jax
import jax.numpy as jnp
from jax import lax
from jax.experimental import pallas as pl
from jax.experimental.pallas import tpu as pltpu
from jax.sharding import PartitionSpec as P

HD = 128
GROUP = 7
SEG = 64
BLK = 56
PART = 8 * BLK
ROWS = GROUP * SEG
WIDE = GROUP * HD
SCALE = 1.0 / math.sqrt(HD)
EXP_SCALE = SCALE * math.log2(math.e)
F32 = jnp.float32
BF16 = jnp.bfloat16
VMEM_LIMIT = 32 * 1024 * 1024
VMEM_MOST = 60 * 1024 * 1024


def params(limit=VMEM_LIMIT):
    return pltpu.CompilerParams(vmem_limit_bytes=limit)


def cost(us):
    return pl.CostEstimate(
        flops=int(us * 5.0e8), bytes_accessed=int(us * 1.0e6), transcendentals=0
    )


def partner(d, z=0, x=0, y=0, c=0):
    return d ^ (z * 32 + x * 8 + y * 2 + c)


def place():
    d = lax.axis_index("dp")
    return d >> 5, (d >> 3) & 3, (d >> 1) & 3, d & 1


def swap(value, **steps):
    return lax.ppermute(value, "dp", [(d, partner(d, **steps)) for d in range(64)])


def swap_back_section(value, **steps):
    pairs = [(d * 4 + p, partner(d, **steps) * 4 + p - 1) for d in range(64) for p in range(1, 4)]
    return lax.ppermute(value, ("dp", "pipe"), pairs)


def split_kernel(fx_hbm, bx_hbm, o0, o1, o2, o3, fx_ref, bx_ref, scr, sems):
    half = 4 * PART
    copies = []
    for i, (source, held) in enumerate(((fx_hbm, fx_ref), (bx_hbm, bx_ref))):
        for j in range(2):
            cols = pl.ds(j * half, half)
            copy = pltpu.make_async_copy(source.at[:, cols], held.at[:, cols], sems.at[2 * i + j])
            copy.start()
            copies.append(copy)
    for copy in copies:
        copy.wait()
    for s in range(8):
        scr[s, 0:SEG, :] = fx_ref[:, s * PART : (s + 1) * PART]
        scr[s, SEG : 2 * SEG, :] = bx_ref[:, s * PART : (s + 1) * PART]
    z, x, _, _ = place()
    for r, out in enumerate((o0, o1, o2, o3)):
        near = scr[z * 4 + (x ^ r)]
        far = scr[(z ^ 1) * 4 + (x ^ r)]
        out[...] = jnp.concatenate([near, far], axis=1)


def split_inputs(fx, bx):
    vmem = pl.BlockSpec(memory_space=pltpu.VMEM)
    hbm = pl.BlockSpec(memory_space=pltpu.HBM)
    return pl.pallas_call(
        split_kernel,
        out_shape=[jax.ShapeDtypeStruct((2 * SEG, 2 * PART), BF16)] * 4,
        in_specs=[hbm, hbm],
        out_specs=[vmem] * 4,
        scratch_shapes=[
            pltpu.VMEM((SEG, 8 * PART), BF16),
            pltpu.VMEM((SEG, 8 * PART), BF16),
            pltpu.VMEM((8, 2 * SEG, PART), BF16),
            pltpu.SemaphoreType.DMA((4,)),
        ],
        compiler_params=params(VMEM_MOST),
        cost_estimate=cost(1.5),
        name="split_inputs",
    )(fx, bx)


def join_kernel(g03, g12, out_ref, scr):
    z, x, _, _ = place()
    for r, (piece, at) in enumerate(((g03, 0), (g12, 0), (g12, SEG), (g03, SEG))):
        scr[z * 4 + (x ^ r)] = piece[at : at + SEG, :PART]
        scr[(z ^ 1) * 4 + (x ^ r)] = piece[at : at + SEG, PART:]
    out_ref[...] = jnp.concatenate([scr[s] for s in range(8)], axis=1)


def join_pieces(g03, g12):
    vmem = pl.BlockSpec(memory_space=pltpu.VMEM)
    return pl.pallas_call(
        join_kernel,
        out_shape=jax.ShapeDtypeStruct((SEG, 8 * PART), BF16),
        in_specs=[vmem, vmem],
        out_specs=vmem,
        scratch_shapes=[pltpu.VMEM((8, SEG, PART), BF16)],
        compiler_params=params(),
        cost_estimate=cost(1),
        name="join_pieces",
    )(g03, g12)


def dot_nt(a, b):
    return lax.dot_general(a, b, (((1,), (1,)), ((), ())), preferred_element_type=F32)


def dot_tn(a, b):
    return lax.dot_general(a, b, (((0,), (0,)), ((), ())), preferred_element_type=F32)


def dot_nn(a, b):
    return lax.dot_general(a, b, (((1,), (0,)), ((), ())), preferred_element_type=F32)


def stack_heads(block, heads):
    return jnp.concatenate([block[:, h * HD : (h + 1) * HD] for h in heads], axis=0)


def unstack_heads(parts):
    heads = [part[i : i + SEG] for part in parts for i in range(0, part.shape[0], SEG)]
    return jnp.concatenate(heads, axis=1)


def row_in_segment(shape):
    return lax.broadcasted_iota(jnp.int32, shape, 0) & (SEG - 1)


def group_columns(g):
    wide = pl.ds(pl.multiple_of(g * WIDE, HD), WIDE)
    key = pl.ds(pl.multiple_of(g * HD, HD), HD)
    return wide, key, pl.ds(pl.multiple_of((g + 4) * HD, HD), HD)


CHUNKS = (range(0, 4), range(4, 7))


def backward_kernel(len_ref, q_ref, do_ref, cache_ref, gq_ref, kv_ref):
    third, fourth = len_ref[2], len_ref[3]
    base = cache_ref.shape[0] - 2 * SEG
    offset = 2 * SEG - fourth - third

    @pl.loop(0, 4)
    def _(g):
        wide, key, value = group_columns(g)
        keys, values = cache_ref[:, key], cache_ref[:, value]
        queries = q_ref[:, wide]
        live = lax.broadcasted_iota(jnp.int32, (SEG, WIDE), 0) < third
        douts = jnp.where(live, do_ref[:, wide], jnp.zeros((SEG, WIDE), BF16))
        dk = jnp.zeros((2 * SEG, HD), F32)
        dv = jnp.zeros((2 * SEG, HD), F32)
        grads = []
        for heads in CHUNKS:
            q, dout = stack_heads(queries, heads), stack_heads(douts, heads)
            scores = dot_nt(q, keys)
            along = dot_nt(dout, values)
            shape = (q.shape[0], 2 * SEG)
            ok = lax.broadcasted_iota(jnp.int32, shape, 1) <= offset + row_in_segment(shape)
            tail = jnp.where(ok, scores[:, base:], -1e30)
            scores = jnp.concatenate([scores[:, :base], tail], axis=1)
            top = jnp.max(scores, axis=1, keepdims=True)
            raised = jnp.exp2((scores - top) * EXP_SCALE)
            probs = raised * (1.0 / jnp.sum(raised, axis=1, keepdims=True))
            weighed = probs * along
            delta = jnp.sum(weighed, axis=1, keepdims=True)
            dscore = (weighed - probs * delta).astype(BF16)
            grads.append((dot_nn(dscore, keys) * SCALE).astype(BF16))
            dk = dk + dot_tn(dscore[:, base:], q)
            dv = dv + dot_tn(probs[:, base:].astype(BF16), dout)
        gq_ref[:, wide] = unstack_heads(grads)
        keep = lax.broadcasted_iota(jnp.int32, (SEG, HD), 0) < third
        shift = (2 * SEG - offset) & (2 * SEG - 1)
        dk = pltpu.roll(dk * SCALE, shift, 0)[:SEG]
        dv = pltpu.roll(dv, shift, 0)[:SEG]
        kv_ref[:, key] = jnp.where(keep, dk, 0.0).astype(BF16)
        kv_ref[:, value] = jnp.where(keep, dv, 0.0).astype(BF16)


def backward_groups(lengths, q, dout, cache):
    vmem = pl.BlockSpec(memory_space=pltpu.VMEM)
    return pl.pallas_call(
        backward_kernel,
        out_shape=[
            jax.ShapeDtypeStruct(q.shape, BF16),
            jax.ShapeDtypeStruct((SEG, 8 * HD), BF16),
        ],
        in_specs=[pl.BlockSpec(memory_space=pltpu.SMEM)] + [vmem] * 3,
        out_specs=[vmem] * 2,
        compiler_params=params(),
        cost_estimate=cost(7),
        name="backward_groups",
    )(lengths, q, dout, cache)


def stored_kernel(first, len_ref, q_ref, cache_ref, acc_ref, stat_ref):
    fourth = len_ref[3]
    base = cache_ref.shape[0] - HD

    @pl.loop(0, 2)
    def _(i):
        wide, key, value = group_columns(i + first)
        keys, values = cache_ref[:, key], cache_ref[:, value]
        queries = q_ref[:, wide]
        lane = lax.broadcasted_iota(jnp.int32, (SEG, HD), 1)
        stat = jnp.zeros((SEG, HD), F32)
        mixed = []
        for heads in CHUNKS:
            q = stack_heads(queries, heads)
            scores = dot_nt(q, keys)
            ok = lax.broadcasted_iota(jnp.int32, (q.shape[0], HD), 1) < HD - fourth
            tail = jnp.where(ok, scores[:, base:], -1e30)
            scores = jnp.concatenate([scores[:, :base], tail], axis=1)
            top = jnp.max(scores, axis=1, keepdims=True)
            raised = jnp.exp2((scores - top) * EXP_SCALE)
            total = jnp.sum(raised, axis=1, keepdims=True)
            mixed.append(dot_nn(raised.astype(BF16), values))
            for at, h in enumerate(heads):
                rows = slice(at * SEG, (at + 1) * SEG)
                stat = jnp.where(lane == h, top[rows], stat)
                stat = jnp.where(lane == SEG + h, total[rows], stat)
        wide, key, _ = group_columns(i)
        acc_ref[:, wide] = unstack_heads(mixed)
        stat_ref[:, key] = stat


def stored_groups(lengths, q, cache, first):
    vmem = pl.BlockSpec(memory_space=pltpu.VMEM)
    return pl.pallas_call(
        functools.partial(stored_kernel, first),
        out_shape=[
            jax.ShapeDtypeStruct((SEG, 2 * WIDE), F32),
            jax.ShapeDtypeStruct((SEG, 2 * HD), F32),
        ],
        in_specs=[pl.BlockSpec(memory_space=pltpu.SMEM)] + [vmem] * 2,
        out_specs=[vmem] * 2,
        compiler_params=params(),
        cost_estimate=cost(2.4),
        name="stored_groups",
    )(lengths, q, cache)


def own_kernel(len_ref, q_ref, k0, k1, k3, acc_a, stat_a, acc_b, stat_b, out_ref):
    fourth = len_ref[3]
    own = (k0[...] + k1[0:SEG, :].astype(F32) + k3[...].astype(F32)).astype(BF16)
    shape = (ROWS, SEG)
    at, row = lax.broadcasted_iota(jnp.int32, shape, 1), row_in_segment(shape)
    ok = (at <= row) & (at < fourth)
    heads = range(GROUP)
    for g in range(4):
        acc_ref, stat_ref = ((acc_a, stat_a), (acc_b, stat_b))[g // 2]
        i = g % 2
        q = stack_heads(q_ref[:, g * WIDE : (g + 1) * WIDE], heads)
        acc = stack_heads(acc_ref[:, i * WIDE : (i + 1) * WIDE], heads)
        stat = stat_ref[:, i * HD : (i + 1) * HD]
        top_c = jnp.concatenate([stat[:, h : h + 1] for h in heads], axis=0)
        total_c = jnp.concatenate([stat[:, SEG + h : SEG + h + 1] for h in heads], axis=0)
        scores = jnp.where(ok, dot_nt(q, own[:, g * HD : (g + 1) * HD]), -1e30)
        top = jnp.maximum(top_c, jnp.max(scores, axis=1, keepdims=True))
        keep = jnp.exp2((top_c - top) * EXP_SCALE)
        raised = jnp.exp2((scores - top) * EXP_SCALE)
        total = total_c * keep + jnp.sum(raised, axis=1, keepdims=True)
        values = own[:, (g + 4) * HD : (g + 5) * HD]
        mixed = acc * keep + dot_nn(raised.astype(BF16), values)
        mixed = mixed * (1.0 / total)
        mixed = jnp.where(row_in_segment((ROWS, HD)) < fourth, mixed, 0.0)
        out_ref[:, g * WIDE : (g + 1) * WIDE] = unstack_heads([mixed.astype(BF16)])


def own_groups(lengths, q, parts, held):
    vmem = pl.BlockSpec(memory_space=pltpu.VMEM)
    return pl.pallas_call(
        own_kernel,
        out_shape=jax.ShapeDtypeStruct(q.shape, BF16),
        in_specs=[pl.BlockSpec(memory_space=pltpu.SMEM)] + [vmem] * 8,
        out_specs=vmem,
        compiler_params=params(),
        cost_estimate=cost(2),
        name="own_groups",
    )(lengths, q, *parts, *held)


def own_kv_kernel(r0, r1, r2, r3, a_ref, b_ref, o0, o12, o3, weight_ref, scr):
    _, _, y, c = place()
    for rc, part in enumerate((a_ref, b_ref)):
        for m, r in enumerate((0, 1, 3, 2)):
            for rz in range(2):
                at = (2 * m + rz) * BLK
                scr[rz * 8 + (y ^ r) * 2 + (c ^ rc)] = part[at : at + BLK, :]
    weight = jnp.concatenate([scr[s] for s in range(16)], axis=0)
    weight_ref[...] = weight
    x = jnp.concatenate([r[0:SEG, :] for r in (r0, r1, r2, r3)], axis=0)
    total = dot_nn(x, weight)
    o0[...] = total[0:SEG]
    o12[...] = total[SEG : 3 * SEG].astype(BF16)
    o3[...] = total[3 * SEG :]


def own_kv_parts(pieces, halves):
    vmem = pl.BlockSpec(memory_space=pltpu.VMEM)
    cols = halves[0].shape[1]
    return pl.pallas_call(
        own_kv_kernel,
        out_shape=[
            jax.ShapeDtypeStruct((SEG, cols), F32),
            jax.ShapeDtypeStruct((2 * SEG, cols), BF16),
            jax.ShapeDtypeStruct((SEG, cols), F32),
            jax.ShapeDtypeStruct((2 * PART, cols), BF16),
        ],
        in_specs=[vmem] * 6,
        out_specs=[vmem] * 4,
        scratch_shapes=[pltpu.VMEM((16, BLK, cols), BF16)],
        compiler_params=params(),
        cost_estimate=cost(1.5),
        name="own_kv_parts",
    )(*pieces, *halves)


def token_grads(r0, r1, r2, r3, g0, g1, g32):
    x = jnp.concatenate([r[SEG:, :] for r in (r0, r1, r3, r2)], axis=0)
    grads = jnp.concatenate([g0[...], g1[...], g32[...]], axis=0)
    return dot_tn(x, grads)


def half_rows(total, side):
    _, _, y, c = place()
    blocks = []
    for r in range(4):
        for rz in range(2):
            start = pl.multiple_of(rz * PART + ((y ^ r) * 2 + (c ^ side)) * BLK, 8)
            blocks.append(total[pl.ds(start, BLK), :])
    return blocks


def weight_grad_kernel(r0, r1, r2, r3, g0, g1, g32, away_ref, home_ref, total):
    total[...] = token_grads(r0, r1, r2, r3, g0, g1, g32)
    away_ref[...] = jnp.concatenate(half_rows(total, 1), axis=0).astype(BF16)
    home_ref[...] = jnp.concatenate(half_rows(total, 0), axis=0)


def weight_grad_halves(pieces, grads):
    vmem = pl.BlockSpec(memory_space=pltpu.VMEM)
    cols = grads[0].shape[1]
    return pl.pallas_call(
        weight_grad_kernel,
        out_shape=[
            jax.ShapeDtypeStruct((PART, cols), BF16),
            jax.ShapeDtypeStruct((PART, cols), F32),
        ],
        in_specs=[vmem] * 7,
        out_specs=[vmem] * 2,
        scratch_shapes=[pltpu.VMEM((2 * PART, cols), F32)],
        compiler_params=params(),
        cost_estimate=cost(1.5),
        name="weight_grad_halves",
    )(*pieces, *grads)


def chip_sum_kernel(home_ref, other_ref, s0, s12, s3):
    rows = 2 * BLK
    total = home_ref[...] + other_ref[...].astype(F32)
    s0[...] = total[:rows]
    s12[...] = total[rows : 3 * rows].astype(BF16)
    s3[...] = total[3 * rows :]


def chip_sum(home, other):
    vmem = pl.BlockSpec(memory_space=pltpu.VMEM)
    cols = home.shape[1]
    return pl.pallas_call(
        chip_sum_kernel,
        out_shape=[
            jax.ShapeDtypeStruct((2 * BLK, cols), F32),
            jax.ShapeDtypeStruct((4 * BLK, cols), BF16),
            jax.ShapeDtypeStruct((2 * BLK, cols), F32),
        ],
        in_specs=[vmem] * 2,
        out_specs=[vmem] * 3,
        compiler_params=params(),
        cost_estimate=cost(0.5),
        name="chip_sum",
    )(home, other)


def input_grad_kernel(g0, g1, g32, weight_ref, o0, o1, o32):
    grads = jnp.concatenate([g0[...], g1[...], g32[...]], axis=0)
    total = dot_nt(grads, weight_ref[...]).astype(BF16)
    o0[...] = total[0:SEG]
    o1[...] = total[SEG : 2 * SEG]
    o32[...] = total[2 * SEG :]


def input_grad_pieces(grads, weight):
    vmem = pl.BlockSpec(memory_space=pltpu.VMEM)
    return pl.pallas_call(
        input_grad_kernel,
        out_shape=[
            jax.ShapeDtypeStruct((SEG, 2 * PART), BF16),
            jax.ShapeDtypeStruct((SEG, 2 * PART), BF16),
            jax.ShapeDtypeStruct((2 * SEG, 2 * PART), BF16),
        ],
        in_specs=[vmem] * 4,
        out_specs=[vmem] * 3,
        compiler_params=params(),
        cost_estimate=cost(0.8),
        name="input_grad_pieces",
    )(*grads, weight)


def shards(fwd_x, fwd_q, bwd_x, bwd_q, bwd_dout, cache_kv, kv_weight, seg_lengths):
    shard = kv_weight[0]
    lengths = seg_lengths[0, 0]
    cache = cache_kv[0, 0]
    front_q, back_q, back_dout = fwd_q[0, 0], bwd_q[0, 0], bwd_dout[0, 0]
    together = lax.optimization_barrier
    rows = functools.partial(jnp.concatenate, axis=0)

    across = swap(shard, z=1)
    split = split_inputs(fwd_x[0, 0], bwd_x[0, 0])
    pieces = [split[0]] + [swap(split[r], x=r) for r in (1, 2, 3)]

    pair = rows([shard, across])
    token, pair, pieces[0] = together((lengths, pair, pieces[0]))
    pair_came = swap(pair, y=1)
    grad_query, kv_grad = backward_groups(token, back_q, back_dout, cache)
    pairs = rows([pair, pair_came])
    token, kv_grad, pairs, *pieces = together((lengths, kv_grad, pairs, *pieces))
    kv_came = swap(kv_grad, x=1)
    pairs_came = swap(pairs, y=3)
    held_a = stored_groups(token, front_q, cache, 0)

    kv_pair = rows([kv_grad, kv_came])
    token, kv_pair, *held_a = together((lengths, kv_pair, *held_a))
    grads = (kv_grad, kv_came, swap(kv_pair, x=3))
    held_b = stored_groups(token, front_q, cache, 2)

    half = rows([pairs, pairs_came])
    half, *grads, acc, stat = together((half, *grads, *held_b))
    held = (*held_a, acc, stat)
    other_half = swap(half, c=1)
    away, home = weight_grad_halves(pieces, grads)
    away, other_half, *pieces = together((away, other_half, *pieces))
    other_away = swap(away, c=1)
    own0, own12, own3, weight = own_kv_parts(pieces, (half, other_half))
    own12, weight = together((own12, weight))
    own_came = swap(own12, x=1)
    in0, in1, in32 = input_grad_pieces(grads, weight)
    in_came = swap(in32, x=3)
    other_away, in0 = together((other_away, in0))
    sum0, sum12, sum3 = chip_sum(home, other_away)
    sum_came = swap(sum12, y=1)

    own_came = together((own_came, sum12))[0]
    own_leave = (own3 + own_came[SEG:].astype(F32)).astype(BF16)
    own_last = swap(own_leave, x=3)
    in_came = together((in_came, own_leave))[0]
    leave03 = rows([in0, in_came[:SEG]])
    leave12 = rows([in1, in_came[SEG:]])
    back03 = swap_back_section(leave03)
    back12 = swap_back_section(leave12, x=1)
    token = together((lengths, leave03, leave12))[0]
    fwd_out = own_groups(token, front_q, (own0, own_came, own_last), held)
    next_act = lax.ppermute(fwd_out, "pipe", [(p, p + 1) for p in range(3)])

    sum_came = together((sum_came, fwd_out))[0]
    sum_leave = (sum3 + sum_came[2 * BLK :].astype(F32)).astype(BF16)
    sum_last = swap(sum_leave, y=3)
    total = sum0 + sum_came[: 2 * BLK].astype(F32) + sum_last.astype(F32)
    far_total = total[BLK:].astype(BF16)
    far_came = swap(far_total, z=1)
    back03 = together((back03, far_total))[0]
    prev_grad = join_pieces(back03, back12)
    weight_grad = total[:BLK] + far_came.astype(F32)
    return (next_act[None, None], grad_query[None, None], prev_grad[None, None], weight_grad[None])


def solution(mesh):
    return jax.shard_map(
        shards,
        mesh=mesh,
        in_specs=(
            P("pipe", "dp", None, None),
            P("pipe", "dp", None, None),
            P("pipe", "dp", None, None),
            P("pipe", "dp", None, None),
            P("pipe", "dp", None, None),
            P("pipe", "dp", None, None),
            P("pipe", "dp", None),
            P("pipe", "dp", None),
        ),
        out_specs=(
            P("pipe", "dp", None, None),
            P("pipe", "dp", None, None),
            P("pipe", "dp", None, None),
            P("pipe", "dp", None),
        ),
        check_vma=False,
    )
```

time: 573 us -> 86.3 us (0.15)
  the two profiles are of different devices: /device:TPU:64 before, /device:TPU:32 now
where the time goes in v2:
time: 86.3 us; the launch traced here: 86.1 us
  waiting for transfers between devices  33.4 us (39%)
  starting transfers between devices  27.9 us (32%)
  Pallas kernels  22.2 us (26%)
  other arithmetic  1.04 us (1%)
  between operations  0.88 us (1%)
    ppermute x16, waiting for transfers between devices, swap(): lax.ppermute(value, 'dp', [(d, partner(d, **steps)) for d in range(64)])  25.7 us
    ppermute x16, starting transfers between devices, swap(): lax.ppermute(value, 'dp', [(d, partner(d, **steps)) for d in range(64)])  20.1 us
    pallas_call x1, Pallas kernels, backward_groups(): pl.pallas_call(backward_kernel, out_shape=[jax.ShapeDtypeStruct(q.shape,...  7.87 us
    pallas_call x2, Pallas kernels, stored_groups(): pl.pallas_call(functools.partial(stored_kernel, first), out_shape=[jax.Sh...  5.23 us
    ppermute x1, waiting for transfers between devices, shards(): next_act = lax.ppermute(fwd_out, 'pipe', [(p, p + 1) for p in range(3)])  5.1 us
    ppermute x2, starting transfers between devices, swap_back_section(): return lax.ppermute(value, ('dp', 'pipe'), pairs)  4.86 us
    ppermute x1, starting transfers between devices, shards(): next_act = lax.ppermute(fwd_out, 'pipe', [(p, p + 1) for p in range(3)])  2.92 us
    pallas_call x1, Pallas kernels, own_groups(): pl.pallas_call(own_kernel, out_shape=jax.ShapeDtypeStruct(q.shape, BF16),...  2.89 us
  transfers between devices with their start and end apart: 19, of which 12 were waited for; matrix products, arithmetic and copies ran while one was open for 0% of the time, Pallas kernels for 26%

profile of v2, /device:TPU:32, one launch (start us, length us, event | category | flops | bytes accessed | tf_op | source)
XLA Modules:
  0.0 86.1 jit_solution(4009311020556862439)
XLA Ops:
  0.7 6.4 %collective-permute-start = (bf16[56,1024]{1,0:T(8,128)(2,1)}, bf16[56,1024]{1,0:T(8,128)(2,1)S(1)}, u32[]{:S(2)}, u32[]{:S(2)}) collective-permute-start(bf16[56,1024]{1,0:T(8,128)(2,1)} %bitcast.26), channel_id=1, source_target_pairs={{0,128},{4,132},{8,136},{12,140},{16,144},{20,148},{24,152},{28,15... | collective-permute-start | bytes 344072 | tf_op jit(solution)/shard_map/ppermute | solution.py:46
  7.1 2.5 %split_inputs.1 = (bf16[128,896]{1,0:T(8,128)(2,1)}, bf16[128,896]{1,0:T(8,128)(2,1)}, bf16[128,896]{1,0:T(8,128)(2,1)}, bf16[128,896]{1,0:T(8,128)(2,1)}) custom-call(bf16[64,3584]{1,0:T(8,128)(2,1)} %bitcast.28, bf16[64,3584]{1,0:T(8,128)(2,1)} %bitcast.29), custom_call_target="tpu_custom_call" | custom-call | flops 750000000 | bytes 1500000 | tf_op jit(solution)/shard_map/split_inputs/pallas_call | solution.py:78
  9.6 1.6 %collective-permute-start.2 = (bf16[128,896]{1,0:T(8,128)(2,1)}, bf16[128,896]{1,0:T(8,128)(2,1)S(1)}, u32[]{:S(2)}, u32[]{:S(2)}) collective-permute-start(bf16[128,896]{1,0:T(8,128)(2,1)} %get-tuple-element.66), channel_id=1, source_target_pairs={{0,32},{4,36},{8,40},{12,44},{16,48},{20,52},{24,56},{28,60},{32,0... | collective-permute-start | bytes 688136 | tf_op jit(solution)/shard_map/ppermute | solution.py:46
  11.2 2.7 %collective-permute-start.3 = (bf16[128,896]{1,0:T(8,128)(2,1)}, bf16[128,896]{1,0:T(8,128)(2,1)S(1)}, u32[]{:S(2)}, u32[]{:S(2)}) collective-permute-start(bf16[128,896]{1,0:T(8,128)(2,1)} %get-tuple-element.67), channel_id=1, source_target_pairs={{0,64},{4,68},{8,72},{12,76},{16,80},{20,84},{24,88},{28,92},{32,9... | collective-permute-start | bytes 688136 | tf_op jit(solution)/shard_map/ppermute | solution.py:46
  13.9 0.5 collective-permute-start.4
  14.4 0.0 collective-permute-done
  14.4 1.7 %collective-permute-start.1 = (bf16[112,1024]{1,0:T(8,128)(2,1)S(1)}, bf16[112,1024]{1,0:T(8,128)(2,1)S(1)}, u32[]{:S(2)}, u32[]{:S(2)}) collective-permute-start(bf16[112,1024]{1,0:T(8,128)(2,1)S(1)} %pad_maximum_fusion.3), channel_id=1, source_target_pairs={{0,8},{4,12},{8,0},{12,4},{16,24},{20,28},{24,16},{28,20},{32,40},... | collective-permute-start | bytes 688136 | tf_op jit(solution)/shard_map/ppermute | solution.py:46
  16.1 0.0 copy-start.3
  16.1 7.9 %backward_groups.1 = (bf16[64,3584]{1,0:T(8,128)(2,1)}, bf16[64,1024]{1,0:T(8,128)(2,1)S(1)}) custom-call(s32[4]{0:T(128)S(1)} %bitcast.21, bf16[64,3584]{1,0:T(8,128)(2,1)S(1)} %bitcast.16, bf16[64,3584]{1,0:T(8,128)(2,1)S(1)} %bitcast.17, bf16[1024,1024]{1,0:T(8,128)(2,1)S(1)} %bitcast.13), custom_call_target="tpu_custom_call" | custom-call | flops 3500000000 | bytes 7000000 | tf_op jit(solution)/shard_map/backward_groups/pallas_call | solution.py:194
  24.0 0.0 collective-permute-done.2.r1
  24.0 0.2 collective-permute-done.3.r2
  24.2 2.6 %collective-permute-done.4.r3 = bf16[128,896]{1,0:T(8,128)(2,1)S(1)} collective-permute-done((bf16[128,896]{1,0:T(8,128)(2,1)}, bf16[128,896]{1,0:T(8,128)(2,1)S(1)}, u32[]{:S(2)}, u32[]{:S(2)}) %collective-permute-start.4) | collective-permute-done | bytes 229408 | tf_op jit(solution)/shard_map/ppermute | solution.py:46
  26.7 3.0 %collective-permute-start.5 = (bf16[224,1024]{1,0:T(8,128)(2,1)S(1)}, bf16[224,1024]{1,0:T(8,128)(2,1)S(1)}, u32[]{:S(2)}, u32[]{:S(2)}) collective-permute-start(bf16[224,1024]{1,0:T(8,128)(2,1)S(1)} %pad_maximum_fusion.1), channel_id=1, source_target_pairs={{0,24},{4,28},{8,16},{12,20},{16,8},{20,12},{24,0},{28,4},{32,56},... | collective-permute-start | bytes 1376264 | tf_op jit(solution)/shard_map/ppermute | solution.py:46
  29.8 2.6 %stored_groups.2 = (f32[64,1792]{1,0:T(8,128)S(1)}, f32[64,256]{1,0:T(8,128)S(1)}) custom-call(s32[4]{0:T(128)S(1)} %bitcast.22, bf16[64,3584]{1,0:T(8,128)(2,1)S(1)} %bitcast.18, bf16[1024,1024]{1,0:T(8,128)(2,1)S(1)} %bitcast.14), custom_call_target="tpu_custom_call" | custom-call | flops 1200000000 | bytes 2400000 | tf_op jit(solution)/shard_map/stored_groups/pallas_call | solution.py:241
  32.4 2.3 %collective-permute-done.6.g1 = bf16[64,1024]{1,0:T(8,128)(2,1)S(1)} collective-permute-done((bf16[64,1024]{1,0:T(8,128)(2,1)S(1)}, bf16[64,1024]{1,0:T(8,128)(2,1)S(1)}, u32[]{:S(2)}, u32[]{:S(2)}) %collective-permute-start.6) | collective-permute-done | bytes 131104 | tf_op jit(solution)/shard_map/ppermute | solution.py:46
  34.7 0.6 collective-permute-start.7
  35.3 2.6 %stored_groups.3 = (f32[64,1792]{1,0:T(8,128)S(1)}, f32[64,256]{1,0:T(8,128)S(1)}) custom-call(s32[4]{0:T(128)S(1)} %bitcast.23, bf16[64,3584]{1,0:T(8,128)(2,1)S(1)} %bitcast.19, bf16[1024,1024]{1,0:T(8,128)(2,1)S(1)} %bitcast.15), custom_call_target="tpu_custom_call" | custom-call | flops 1200000000 | bytes 2400000 | tf_op jit(solution)/shard_map/stored_groups/pallas_call | solution.py:241
  37.9 0.0 copy-start.5
  38.0 1.2 %collective-permute-done.5 = bf16[224,1024]{1,0:T(8,128)(2,1)S(1)} collective-permute-done((bf16[224,1024]{1,0:T(8,128)(2,1)S(1)}, bf16[224,1024]{1,0:T(8,128)(2,1)S(1)}, u32[]{:S(2)}, u32[]{:S(2)}) %collective-permute-start.5) | collective-permute-done | bytes 458784 | tf_op jit(solution)/shard_map/ppermute | solution.py:46
  39.1 0.1 pad_maximum_fusion.a_ref
  39.2 3.2 %collective-permute-done.7.g32 = bf16[128,1024]{1,0:T(8,128)(2,1)S(1)} collective-permute-done((bf16[128,1024]{1,0:T(8,128)(2,1)S(1)}, bf16[128,1024]{1,0:T(8,128)(2,1)S(1)}, u32[]{:S(2)}, u32[]{:S(2)}) %collective-permute-start.7) | collective-permute-done | bytes 262176 | tf_op jit(solution)/shard_map/ppermute | solution.py:46
  42.4 0.9 %weight_grad_halves.1 = (bf16[448,1024]{1,0:T(8,128)(2,1)S(1)}, f32[448,1024]{1,0:T(8,128)S(1)}) custom-call(bf16[128,896]{1,0:T(8,128)(2,1)S(1)} %copy-done.5, bf16[128,896]{1,0:T(8,128)(2,1)S(1)} %collective-permute-done.2.r1, bf16[128,896]{1,0:T(8,128)(2,1)S(1)} %collective-permute-done.3.r2, bf16[128,896]{1,0:T(8,128)(2,1)S(1)} %collective-permute-done.4.r3, ...), custom_call_target="tpu_custom_call" | custom-call | flops 750000000 | bytes 1500000 | tf_op jit(solution)/shard_map/weight_grad_halves/pallas_call | solution.py:356
  43.3 1.6 %collective-permute-done.8.b_ref = bf16[448,1024]{1,0:T(8,128)(2,1)S(1)} collective-permute-done((bf16[448,1024]{1,0:T(8,128)(2,1)S(1)}, bf16[448,1024]{1,0:T(8,128)(2,1)S(1)}, u32[]{:S(2)}, u32[]{:S(2)}) %collective-permute-start.8) | collective-permute-done | bytes 917536 | tf_op jit(solution)/shard_map/ppermute | solution.py:46
  44.9 0.1 collective-permute-start.9
  45.0 0.9 own_kv_parts.1
  45.9 0.1 collective-permute-start.11
  46.0 0.7 input_grad_pieces.1
  46.7 0.8 collective-permute-start.10
  47.5 0.0 collective-permute-done.9.other_ref
  47.5 0.1 chip_sum.1
  47.7 0.2 collective-permute-start.15
  47.9 6.7 %collective-permute-done.11.k1 = bf16[128,1024]{1,0:T(8,128)(2,1)S(1)} collective-permute-done((bf16[128,1024]{1,0:T(8,128)(2,1)S(1)}, bf16[128,1024]{1,0:T(8,128)(2,1)S(1)}, u32[]{:S(2)}, u32[]{:S(2)}) %collective-permute-start.11) | collective-permute-done | bytes 262176 | tf_op jit(solution)/shard_map/ppermute | solution.py:46
  54.6 0.6 collective-permute-start.12
  55.2 0.9 %collective-permute-done.10 = bf16[128,896]{1,0:T(8,128)(2,1)S(1)} collective-permute-done((bf16[128,896]{1,0:T(8,128)(2,1)S(1)}, bf16[128,896]{1,0:T(8,128)(2,1)S(1)}, u32[]{:S(2)}, u32[]{:S(2)}) %collective-permute-start.10) | collective-permute-done | bytes 229408 | tf_op jit(solution)/shard_map/ppermute | solution.py:46
  56.2 4.7 %collective-permute-done.12.k3 = bf16[64,1024]{1,0:T(8,128)(2,1)S(1)} collective-permute-done((bf16[64,1024]{1,0:T(8,128)(2,1)S(1)}, bf16[64,1024]{1,0:T(8,128)(2,1)S(1)}, u32[]{:S(2)}, u32[]{:S(2)}) %collective-permute-start.12) | collective-permute-done | bytes 131104 | tf_op jit(solution)/shard_map/ppermute | solution.py:46
  60.9 2.9 %own_groups.1 = bf16[64,3584]{1,0:T(8,128)(2,1)S(1)} custom-call(s32[4]{0:T(128)S(1)} %bitcast.24, bf16[64,3584]{1,0:T(8,128)(2,1)S(1)} %bitcast.20, f32[64,1024]{1,0:T(8,128)S(1)} %get-tuple-element.108.k0, bf16[128,1024]{1,0:T(8,128)(2,1)S(1)} %collective-permute-done.11.k1, bf16[64,1024]{1,0:T(8,128)(2,1)S(1)} %collective-permute-done.12.k3, ...), custom_call_target="tpu_custom_call" | custom-call | flops 1000000000 | bytes 2000000 | tf_op jit(solution)/shard_map/own_groups/pallas_call | solution.py:284
  63.8 0.3 collective-permute-start.16
  64.1 2.9 %collective-permute-start.13 = (bf16[64,3584]{1,0:T(8,128)(2,1)S(1)}, bf16[64,3584]{1,0:T(8,128)(2,1)S(1)}, u32[]{:S(2)}, u32[]{:S(2)}) collective-permute-start(bf16[64,3584]{1,0:T(8,128)(2,1)S(1)} %own_groups.1), channel_id=1, source_target_pairs={{0,1},{1,2},{2,3},{4,5},{5,6},{6,7},{8,9},{9,10},{10,11},{12,13},{... | collective-permute-start | bytes 1376264 | tf_op jit(solution)/shard_map/ppermute | solution.py:475
  67.0 2.9 %collective-permute-start.14 = (bf16[128,896]{1,0:T(8,128)(2,1)S(1)}, bf16[128,896]{1,0:T(8,128)(2,1)S(1)}, u32[]{:S(2)}, u32[]{:S(2)}) collective-permute-start(bf16[128,896]{1,0:T(8,128)(2,1)S(1)} %pad_maximum_fusion.4), channel_id=1, source_target_pairs={{1,0},{2,1},{3,2},{5,4},{6,5},{7,6},{9,8},{10,9},{11,10},{13,12},{... | collective-permute-start | bytes 688136 | tf_op jit(solution)/shard_map/ppermute | solution.py:51
  70.0 1.9 %collective-permute-start.17 = (bf16[128,896]{1,0:T(8,128)(2,1)S(1)}, bf16[128,896]{1,0:T(8,128)(2,1)S(1)}, u32[]{:S(2)}, u32[]{:S(2)}) collective-permute-start(bf16[128,896]{1,0:T(8,128)(2,1)S(1)} %pad_maximum_fusion.5), channel_id=1, source_target_pairs={{1,32},{2,33},{3,34},{5,36},{6,37},{7,38},{9,40},{10,41},{11,42},{... | collective-permute-start | bytes 688136 | tf_op jit(solution)/shard_map/ppermute | solution.py:51
  71.9 0.1 convert_add_fusion
  72.0 1.6 %collective-permute-start.18 = (bf16[56,1024]{1,0:T(8,128)(2,1)S(1)}, bf16[56,1024]{1,0:T(8,128)(2,1)S(1)}, u32[]{:S(2)}, u32[]{:S(2)}) collective-permute-start(bf16[56,1024]{1,0:T(8,128)(2,1)S(1)} %slice.38), channel_id=1, source_target_pairs={{0,128},{4,132},{8,136},{12,140},{16,144},{20,148},{24,152},{28,15... | collective-permute-start | bytes 344072 | tf_op jit(solution)/shard_map/ppermute | solution.py:46
  73.6 5.1 %collective-permute-done.13 = bf16[64,3584]{1,0:T(8,128)(2,1)S(1)} collective-permute-done((bf16[64,3584]{1,0:T(8,128)(2,1)S(1)}, bf16[64,3584]{1,0:T(8,128)(2,1)S(1)}, u32[]{:S(2)}, u32[]{:S(2)}) %collective-permute-start.13) | collective-permute-done | bytes 458784 | tf_op jit(solution)/shard_map/ppermute | solution.py:475
  78.7 2.5 %collective-permute-done.17.g12 = bf16[128,896]{1,0:T(8,128)(2,1)S(1)} collective-permute-done((bf16[128,896]{1,0:T(8,128)(2,1)S(1)}, bf16[128,896]{1,0:T(8,128)(2,1)S(1)}, u32[]{:S(2)}, u32[]{:S(2)}) %collective-permute-start.17) | collective-permute-done | bytes 229408 | tf_op jit(solution)/shard_map/ppermute | solution.py:51
  81.3 1.0 %join_pieces.1 = bf16[64,3584]{1,0:T(8,128)(2,1)} custom-call(bf16[128,896]{1,0:T(8,128)(2,1)S(1)} %collective-permute-done.14.g03, bf16[128,896]{1,0:T(8,128)(2,1)S(1)} %collective-permute-done.17.g12), custom_call_target="tpu_custom_call" | custom-call | flops 500000000 | bytes 1000000 | tf_op jit(solution)/shard_map/join_pieces/pallas_call | solution.py:105
  82.3 2.4 %collective-permute-done.18 = bf16[56,1024]{1,0:T(8,128)(2,1)S(1)} collective-permute-done((bf16[56,1024]{1,0:T(8,128)(2,1)S(1)}, bf16[56,1024]{1,0:T(8,128)(2,1)S(1)}, u32[]{:S(2)}, u32[]{:S(2)}) %collective-permute-start.18) | collective-permute-done | bytes 114720 | tf_op jit(solution)/shard_map/ppermute | solution.py:46
  84.7 0.7 fusion
  85.4 0.8 copy.13
  (27 shorter events, 0.3 us)
Async XLA Ops:
  0.6 13.8 %copy-start.6 = (bf16[1,56,1024]{2,1,0:T(8,128)(2,1)S(1)}, bf16[1,56,1024]{2,1,0:T(8,128)(2,1)}, u32[]{:S(2)}) copy-start(bf16[1,56,1024]{2,1,0:T(8,128)(2,1)} %param.14) | copy-start | bytes 344068
  0.6 15.4 %copy-start.4 = (s32[1,1,4]{2,1,0:T(1,128)S(1)}, s32[1,1,4]{2,1,0:T(1,128)}, u32[]{:S(2)}) copy-start(s32[1,1,4]{2,1,0:T(1,128)} %param.15) | copy-start | bytes 52
  0.7 15.4 %copy-start = (bf16[1,1,1024,1024]{3,2,1,0:T(8,128)(2,1)S(1)}, bf16[1,1,1024,1024]{3,2,1,0:T(8,128)(2,1)}, u32[]{:S(2)}) copy-start(bf16[1,1,1024,1024]{3,2,1,0:T(8,128)(2,1)} %param.13) | copy-start | bytes 6291460
  0.7 15.4 %copy-start.2 = (bf16[1,1,64,3584]{3,2,1,0:T(8,128)(2,1)S(1)}, bf16[1,1,64,3584]{3,2,1,0:T(8,128)(2,1)}, u32[]{:S(2)}) copy-start(bf16[1,1,64,3584]{3,2,1,0:T(8,128)(2,1)} %param.12) | copy-start | bytes 1376260
  0.7 15.4 %copy-start.1 = (bf16[1,1,64,3584]{3,2,1,0:T(8,128)(2,1)S(1)}, bf16[1,1,64,3584]{3,2,1,0:T(8,128)(2,1)}, u32[]{:S(2)}) copy-start(bf16[1,1,64,3584]{3,2,1,0:T(8,128)(2,1)} %param.11) | copy-start | bytes 1376260
  0.7 13.7 %collective-permute-start = (bf16[56,1024]{1,0:T(8,128)(2,1)}, bf16[56,1024]{1,0:T(8,128)(2,1)S(1)}, u32[]{:S(2)}, u32[]{:S(2)}) collective-permute-start(bf16[56,1024]{1,0:T(8,128)(2,1)} %bitcast.26), channel_id=1, source_target_pairs={{0,128},{4,132},{8,136},{12,140},{16,144},{20,148},{24,152},{28,15... | collective-permute-start | bytes 344072 | tf_op jit(solution)/shard_map/ppermute | solution.py:46
  9.6 14.4 %collective-permute-start.2 = (bf16[128,896]{1,0:T(8,128)(2,1)}, bf16[128,896]{1,0:T(8,128)(2,1)S(1)}, u32[]{:S(2)}, u32[]{:S(2)}) collective-permute-start(bf16[128,896]{1,0:T(8,128)(2,1)} %get-tuple-element.66), channel_id=1, source_target_pairs={{0,32},{4,36},{8,40},{12,44},{16,48},{20,52},{24,56},{28,60},{32,0... | collective-permute-start | bytes 688136 | tf_op jit(solution)/shard_map/ppermute | solution.py:46
  11.2 13.0 %collective-permute-start.3 = (bf16[128,896]{1,0:T(8,128)(2,1)}, bf16[128,896]{1,0:T(8,128)(2,1)S(1)}, u32[]{:S(2)}, u32[]{:S(2)}) collective-permute-start(bf16[128,896]{1,0:T(8,128)(2,1)} %get-tuple-element.67), channel_id=1, source_target_pairs={{0,64},{4,68},{8,72},{12,76},{16,80},{20,84},{24,88},{28,92},{32,9... | collective-permute-start | bytes 688136 | tf_op jit(solution)/shard_map/ppermute | solution.py:46
  13.9 12.8 %collective-permute-start.4 = (bf16[128,896]{1,0:T(8,128)(2,1)}, bf16[128,896]{1,0:T(8,128)(2,1)S(1)}, u32[]{:S(2)}, u32[]{:S(2)}) collective-permute-start(bf16[128,896]{1,0:T(8,128)(2,1)} %get-tuple-element.68), channel_id=1, source_target_pairs={{0,96},{4,100},{8,104},{12,108},{16,112},{20,116},{24,120},{28,124... | collective-permute-start | bytes 688136 | tf_op jit(solution)/shard_map/ppermute | solution.py:46
  14.4 9.6 %collective-permute-start.1 = (bf16[112,1024]{1,0:T(8,128)(2,1)S(1)}, bf16[112,1024]{1,0:T(8,128)(2,1)S(1)}, u32[]{:S(2)}, u32[]{:S(2)}) collective-permute-start(bf16[112,1024]{1,0:T(8,128)(2,1)S(1)} %pad_maximum_fusion.3), channel_id=1, source_target_pairs={{0,8},{4,12},{8,0},{12,4},{16,24},{20,28},{24,16},{28,20},{32,40},... | collective-permute-start | bytes 688136 | tf_op jit(solution)/shard_map/ppermute | solution.py:46
  16.1 13.7 %copy-start.3 = (bf16[1,1,64,3584]{3,2,1,0:T(8,128)(2,1)S(1)}, bf16[1,1,64,3584]{3,2,1,0:T(8,128)(2,1)}, u32[]{:S(2)}) copy-start(bf16[1,1,64,3584]{3,2,1,0:T(8,128)(2,1)} %param.9) | copy-start | bytes 1376260
  26.7 12.4 %collective-permute-start.5 = (bf16[224,1024]{1,0:T(8,128)(2,1)S(1)}, bf16[224,1024]{1,0:T(8,128)(2,1)S(1)}, u32[]{:S(2)}, u32[]{:S(2)}) collective-permute-start(bf16[224,1024]{1,0:T(8,128)(2,1)S(1)} %pad_maximum_fusion.1), channel_id=1, source_target_pairs={{0,24},{4,28},{8,16},{12,20},{16,8},{20,12},{24,0},{28,4},{32,56},... | collective-permute-start | bytes 1376264 | tf_op jit(solution)/shard_map/ppermute | solution.py:46
  29.8 5.0 %collective-permute-start.6 = (bf16[64,1024]{1,0:T(8,128)(2,1)S(1)}, bf16[64,1024]{1,0:T(8,128)(2,1)S(1)}, u32[]{:S(2)}, u32[]{:S(2)}) collective-permute-start(bf16[64,1024]{1,0:T(8,128)(2,1)S(1)} %get-tuple-element.82.g0), channel_id=1, source_target_pairs={{0,32},{4,36},{8,40},{12,44},{16,48},{20,52},{24,56},{28,60},{32,0... | collective-permute-start | bytes 393224 | tf_op jit(solution)/shard_map/ppermute | solution.py:46
  34.7 7.7 %collective-permute-start.7 = (bf16[128,1024]{1,0:T(8,128)(2,1)S(1)}, bf16[128,1024]{1,0:T(8,128)(2,1)S(1)}, u32[]{:S(2)}, u32[]{:S(2)}) collective-permute-start(bf16[128,1024]{1,0:T(8,128)(2,1)S(1)} %pad_maximum_fusion.2), channel_id=1, source_target_pairs={{0,96},{4,100},{8,104},{12,108},{16,112},{20,116},{24,120},{28,124... | collective-permute-start | bytes 786440 | tf_op jit(solution)/shard_map/ppermute | solution.py:46
  37.9 4.5 %copy-start.5 = (bf16[128,896]{1,0:T(8,128)(2,1)S(1)}, bf16[128,896]{1,0:T(8,128)(2,1)}, u32[]{:S(2)}) copy-start(bf16[128,896]{1,0:T(8,128)(2,1)} %get-tuple-element.88.r0) | copy-start | bytes 688132
  42.4 2.5 %collective-permute-start.8 = (bf16[448,1024]{1,0:T(8,128)(2,1)S(1)}, bf16[448,1024]{1,0:T(8,128)(2,1)S(1)}, u32[]{:S(2)}, u32[]{:S(2)}) collective-permute-start(bf16[448,1024]{1,0:T(8,128)(2,1)S(1)} %pad_maximum_fusion.a_ref), channel_id=1, source_target_pairs={{0,4},{4,0},{8,12},{12,8},{16,20},{20,16},{24,28},{28,24},{32,36},... | collective-permute-start | bytes 2752520 | tf_op jit(solution)/shard_map/ppermute | solution.py:46
  44.9 2.6 %collective-permute-start.9 = (bf16[448,1024]{1,0:T(8,128)(2,1)S(1)}, bf16[448,1024]{1,0:T(8,128)(2,1)S(1)}, u32[]{:S(2)}, u32[]{:S(2)}) collective-permute-start(bf16[448,1024]{1,0:T(8,128)(2,1)S(1)} %get-tuple-element.87), channel_id=1, source_target_pairs={{0,4},{4,0},{8,12},{12,8},{16,20},{20,16},{24,28},{28,24},{32,36},... | collective-permute-start | bytes 2752520 | tf_op jit(solution)/shard_map/ppermute | solution.py:46
  45.9 8.7 %collective-permute-start.11 = (bf16[128,1024]{1,0:T(8,128)(2,1)S(1)}, bf16[128,1024]{1,0:T(8,128)(2,1)S(1)}, u32[]{:S(2)}, u32[]{:S(2)}) collective-permute-start(bf16[128,1024]{1,0:T(8,128)(2,1)S(1)} %get-tuple-element.100), channel_id=1, source_target_pairs={{0,32},{4,36},{8,40},{12,44},{16,48},{20,52},{24,56},{28,60},{32,0... | collective-permute-start | bytes 786440 | tf_op jit(solution)/shard_map/ppermute | solution.py:46
  46.7 9.4 %collective-permute-start.10 = (bf16[128,896]{1,0:T(8,128)(2,1)S(1)}, bf16[128,896]{1,0:T(8,128)(2,1)S(1)}, u32[]{:S(2)}, u32[]{:S(2)}) collective-permute-start(bf16[128,896]{1,0:T(8,128)(2,1)S(1)} %get-tuple-element.98), channel_id=1, source_target_pairs={{0,96},{4,100},{8,104},{12,108},{16,112},{20,116},{24,120},{28,124... | collective-permute-start | bytes 688136 | tf_op jit(solution)/shard_map/ppermute | solution.py:46
  47.7 16.1 %collective-permute-start.15 = (bf16[224,1024]{1,0:T(8,128)(2,1)S(1)}, bf16[224,1024]{1,0:T(8,128)(2,1)S(1)}, u32[]{:S(2)}, u32[]{:S(2)}) collective-permute-start(bf16[224,1024]{1,0:T(8,128)(2,1)S(1)} %get-tuple-element.103), channel_id=1, source_target_pairs={{0,8},{4,12},{8,0},{12,4},{16,24},{20,28},{24,16},{28,20},{32,40},... | collective-permute-start | bytes 1376264 | tf_op jit(solution)/shard_map/ppermute | solution.py:46
  54.6 6.3 %collective-permute-start.12 = (bf16[64,1024]{1,0:T(8,128)(2,1)S(1)}, bf16[64,1024]{1,0:T(8,128)(2,1)S(1)}, u32[]{:S(2)}, u32[]{:S(2)}) collective-permute-start(bf16[64,1024]{1,0:T(8,128)(2,1)S(1)} %add_convert_fusion.1), channel_id=1, source_target_pairs={{0,96},{4,100},{8,104},{12,108},{16,112},{20,116},{24,120},{28,124... | collective-permute-start | bytes 393224 | tf_op jit(solution)/shard_map/ppermute | solution.py:46
  63.8 8.1 %collective-permute-start.16 = (bf16[112,1024]{1,0:T(8,128)(2,1)S(1)}, bf16[112,1024]{1,0:T(8,128)(2,1)S(1)}, u32[]{:S(2)}, u32[]{:S(2)}) collective-permute-start(bf16[112,1024]{1,0:T(8,128)(2,1)S(1)} %add_convert_fusion), channel_id=1, source_target_pairs={{0,24},{4,28},{8,16},{12,20},{16,8},{20,12},{24,0},{28,4},{32,56},... | collective-permute-start | bytes 688136 | tf_op jit(solution)/shard_map/ppermute | solution.py:46
  64.1 14.6 %collective-permute-start.13 = (bf16[64,3584]{1,0:T(8,128)(2,1)S(1)}, bf16[64,3584]{1,0:T(8,128)(2,1)S(1)}, u32[]{:S(2)}, u32[]{:S(2)}) collective-permute-start(bf16[64,3584]{1,0:T(8,128)(2,1)S(1)} %own_groups.1), channel_id=1, source_target_pairs={{0,1},{1,2},{2,3},{4,5},{5,6},{6,7},{8,9},{9,10},{10,11},{12,13},{... | collective-permute-start | bytes 1376264 | tf_op jit(solution)/shard_map/ppermute | solution.py:475
  67.0 11.7 %collective-permute-start.14 = (bf16[128,896]{1,0:T(8,128)(2,1)S(1)}, bf16[128,896]{1,0:T(8,128)(2,1)S(1)}, u32[]{:S(2)}, u32[]{:S(2)}) collective-permute-start(bf16[128,896]{1,0:T(8,128)(2,1)S(1)} %pad_maximum_fusion.4), channel_id=1, source_target_pairs={{1,0},{2,1},{3,2},{5,4},{6,5},{7,6},{9,8},{10,9},{11,10},{13,12},{... | collective-permute-start | bytes 688136 | tf_op jit(solution)/shard_map/ppermute | solution.py:51
  70.0 11.3 %collective-permute-start.17 = (bf16[128,896]{1,0:T(8,128)(2,1)S(1)}, bf16[128,896]{1,0:T(8,128)(2,1)S(1)}, u32[]{:S(2)}, u32[]{:S(2)}) collective-permute-start(bf16[128,896]{1,0:T(8,128)(2,1)S(1)} %pad_maximum_fusion.5), channel_id=1, source_target_pairs={{1,32},{2,33},{3,34},{5,36},{6,37},{7,38},{9,40},{10,41},{11,42},{... | collective-permute-start | bytes 688136 | tf_op jit(solution)/shard_map/ppermute | solution.py:51
  72.0 12.6 %collective-permute-start.18 = (bf16[56,1024]{1,0:T(8,128)(2,1)S(1)}, bf16[56,1024]{1,0:T(8,128)(2,1)S(1)}, u32[]{:S(2)}, u32[]{:S(2)}) collective-permute-start(bf16[56,1024]{1,0:T(8,128)(2,1)S(1)} %slice.38), channel_id=1, source_target_pairs={{0,128},{4,132},{8,136},{12,140},{16,144},{20,148},{24,152},{28,15... | collective-permute-start | bytes 344072 | tf_op jit(solution)/shard_map/ppermute | solution.py:46

commit v3 on v2

--- a/solution.py
+++ b/solution.py
@@ -29,7 +29,7 @@
 
 def cost(us):
     return pl.CostEstimate(
-        flops=int(us * 5.0e8), bytes_accessed=int(us * 1.0e6), transcendentals=0
+        flops=int(us * 0.5e9), bytes_accessed=int(us * 1e6), transcendentals=0
     )
 
 
@@ -44,11 +44,6 @@
 
 def swap(value, **steps):
     return lax.ppermute(value, "dp", [(d, partner(d, **steps)) for d in range(64)])
-
-
-def swap_back_section(value, **steps):
-    pairs = [(d * 4 + p, partner(d, **steps) * 4 + p - 1) for d in range(64) for p in range(1, 4)]
-    return lax.ppermute(value, ("dp", "pipe"), pairs)
 
 
 def split_kernel(fx_hbm, bx_hbm, o0, o1, o2, o3, fx_ref, bx_ref, scr, sems):
@@ -92,26 +87,27 @@
     )(fx, bx)
 
 
-def join_kernel(g03, g12, out_ref, scr):
+def join_kernel(here, g32, g12, act_ref, out_ref, act_out, scr):
+    act_out[...] = act_ref[...]
     z, x, _, _ = place()
-    for r, (piece, at) in enumerate(((g03, 0), (g12, 0), (g12, SEG), (g03, SEG))):
+    for r, (piece, at) in enumerate(((here, 0), (g12, 0), (g12, SEG), (g32, 0))):
         scr[z * 4 + (x ^ r)] = piece[at : at + SEG, :PART]
         scr[(z ^ 1) * 4 + (x ^ r)] = piece[at : at + SEG, PART:]
     out_ref[...] = jnp.concatenate([scr[s] for s in range(8)], axis=1)
 
 
-def join_pieces(g03, g12):
+def join_pieces(here, g32, g12, act):
     vmem = pl.BlockSpec(memory_space=pltpu.VMEM)
     return pl.pallas_call(
         join_kernel,
-        out_shape=jax.ShapeDtypeStruct((SEG, 8 * PART), BF16),
-        in_specs=[vmem, vmem],
-        out_specs=vmem,
+        out_shape=[jax.ShapeDtypeStruct((SEG, 8 * PART), BF16)] * 2,
+        in_specs=[vmem] * 4,
+        out_specs=[vmem] * 2,
         scratch_shapes=[pltpu.VMEM((8, SEG, PART), BF16)],
         compiler_params=params(),
         cost_estimate=cost(1),
         name="join_pieces",
-    )(g03, g12)
+    )(here, g32, g12, act)
 
 
 def dot_nt(a, b):
@@ -252,9 +248,10 @@
     )(lengths, q, cache)
 
 
-def own_kernel(len_ref, q_ref, k0, k1, k3, acc_a, stat_a, acc_b, stat_b, out_ref):
+def own_kernel(len_ref, q_ref, k0, k1, k2, k3, acc_a, stat_a, acc_b, stat_b, out_ref):
     fourth = len_ref[3]
-    own = (k0[...] + k1[0:SEG, :].astype(F32) + k3[...].astype(F32)).astype(BF16)
+    own = k0[...] + k1[...].astype(F32) + k2[...].astype(F32) + k3[...].astype(F32)
+    own = own.astype(BF16)
     shape = (ROWS, SEG)
     at, row = lax.broadcasted_iota(jnp.int32, shape, 1), row_in_segment(shape)
     ok = (at <= row) & (at < fourth)
@@ -284,7 +281,7 @@
     return pl.pallas_call(
         own_kernel,
         out_shape=jax.ShapeDtypeStruct(q.shape, BF16),
-        in_specs=[pl.BlockSpec(memory_space=pltpu.SMEM)] + [vmem] * 8,
+        in_specs=[pl.BlockSpec(memory_space=pltpu.SMEM)] + [vmem] * 9,
         out_specs=vmem,
         compiler_params=params(),
         cost_estimate=cost(2),
@@ -292,7 +289,7 @@
     )(lengths, q, *parts, *held)
 
 
-def own_kv_kernel(r0, r1, r2, r3, a_ref, b_ref, o0, o12, o3, weight_ref, scr):
+def own_kv_kernel(r0, r1, r2, r3, a_ref, b_ref, o0, o1, o2, o3, weight_ref, scr):
     _, _, y, c = place()
     for rc, part in enumerate((a_ref, b_ref)):
         for m, r in enumerate((0, 1, 3, 2)):
@@ -303,9 +300,8 @@
     weight_ref[...] = weight
     x = jnp.concatenate([r[0:SEG, :] for r in (r0, r1, r2, r3)], axis=0)
     total = dot_nn(x, weight)
-    o0[...] = total[0:SEG]
-    o12[...] = total[SEG : 3 * SEG].astype(BF16)
-    o3[...] = total[3 * SEG :]
+    for r, out in enumerate((o0, o1, o2, o3)):
+        out[...] = total[r * SEG : (r + 1) * SEG].astype(out.dtype)
 
 
 def own_kv_parts(pieces, halves):
@@ -315,12 +311,13 @@
         own_kv_kernel,
         out_shape=[
             jax.ShapeDtypeStruct((SEG, cols), F32),
-            jax.ShapeDtypeStruct((2 * SEG, cols), BF16),
-            jax.ShapeDtypeStruct((SEG, cols), F32),
+            jax.ShapeDtypeStruct((SEG, cols), BF16),
+            jax.ShapeDtypeStruct((SEG, cols), BF16),
+            jax.ShapeDtypeStruct((SEG, cols), BF16),
             jax.ShapeDtypeStruct((2 * PART, cols), BF16),
         ],
         in_specs=[vmem] * 6,
-        out_specs=[vmem] * 4,
+        out_specs=[vmem] * 5,
         scratch_shapes=[pltpu.VMEM((16, BLK, cols), BF16)],
         compiler_params=params(),
         cost_estimate=cost(1.5),
@@ -328,9 +325,9 @@
     )(*pieces, *halves)
 
 
-def token_grads(r0, r1, r2, r3, g0, g1, g32):
+def token_grads(r0, r1, r2, r3, g0, g1, g3, g2):
     x = jnp.concatenate([r[SEG:, :] for r in (r0, r1, r3, r2)], axis=0)
-    grads = jnp.concatenate([g0[...], g1[...], g32[...]], axis=0)
+    grads = jnp.concatenate([g0[...], g1[...], g3[...], g2[...]], axis=0)
     return dot_tn(x, grads)
 
 
@@ -344,8 +341,8 @@
     return blocks
 
 
-def weight_grad_kernel(r0, r1, r2, r3, g0, g1, g32, away_ref, home_ref, total):
-    total[...] = token_grads(r0, r1, r2, r3, g0, g1, g32)
+def weight_grad_kernel(r0, r1, r2, r3, g0, g1, g3, g2, away_ref, home_ref, total):
+    total[...] = token_grads(r0, r1, r2, r3, g0, g1, g3, g2)
     away_ref[...] = jnp.concatenate(half_rows(total, 1), axis=0).astype(BF16)
     home_ref[...] = jnp.concatenate(half_rows(total, 0), axis=0)
 
@@ -359,7 +356,7 @@
             jax.ShapeDtypeStruct((PART, cols), BF16),
             jax.ShapeDtypeStruct((PART, cols), F32),
         ],
-        in_specs=[vmem] * 7,
+        in_specs=[vmem] * 8,
         out_specs=[vmem] * 2,
         scratch_shapes=[pltpu.VMEM((2 * PART, cols), F32)],
         compiler_params=params(),
@@ -394,25 +391,18 @@
     )(home, other)
 
 
-def input_grad_kernel(g0, g1, g32, weight_ref, o0, o1, o32):
-    grads = jnp.concatenate([g0[...], g1[...], g32[...]], axis=0)
-    total = dot_nt(grads, weight_ref[...]).astype(BF16)
-    o0[...] = total[0:SEG]
-    o1[...] = total[SEG : 2 * SEG]
-    o32[...] = total[2 * SEG :]
+def input_grad_kernel(g0, g1, g3, g2, weight_ref, out_ref):
+    grads = jnp.concatenate([g0[...], g1[...], g3[...], g2[...]], axis=0)
+    out_ref[...] = dot_nt(grads, weight_ref[...]).astype(BF16)
 
 
 def input_grad_pieces(grads, weight):
     vmem = pl.BlockSpec(memory_space=pltpu.VMEM)
     return pl.pallas_call(
         input_grad_kernel,
-        out_shape=[
-            jax.ShapeDtypeStruct((SEG, 2 * PART), BF16),
-            jax.ShapeDtypeStruct((SEG, 2 * PART), BF16),
-            jax.ShapeDtypeStruct((2 * SEG, 2 * PART), BF16),
-        ],
-        in_specs=[vmem] * 4,
-        out_specs=[vmem] * 3,
+        out_shape=jax.ShapeDtypeStruct((4 * SEG, 2 * PART), BF16),
+        in_specs=[vmem] * 5,
+        out_specs=vmem,
         compiler_params=params(),
         cost_estimate=cost(0.8),
         name="input_grad_pieces",
@@ -437,13 +427,10 @@
     grad_query, kv_grad = backward_groups(token, back_q, back_dout, cache)
     pairs = rows([pair, pair_came])
     token, kv_grad, pairs, *pieces = together((lengths, kv_grad, pairs, *pieces))
-    kv_came = swap(kv_grad, x=1)
+    grads = [kv_grad] + [swap(kv_grad, x=r) for r in (1, 3, 2)]
     pairs_came = swap(pairs, y=3)
     held_a = stored_groups(token, front_q, cache, 0)
-
-    kv_pair = rows([kv_grad, kv_came])
-    token, kv_pair, *held_a = together((lengths, kv_pair, *held_a))
-    grads = (kv_grad, kv_came, swap(kv_pair, x=3))
+    token = together((lengths, held_a[1]))[0]
     held_b = stored_groups(token, front_q, cache, 2)
 
     half = rows([pairs, pairs_came])
@@ -451,37 +438,31 @@
     held = (*held_a, acc, stat)
     other_half = swap(half, c=1)
     away, home = weight_grad_halves(pieces, grads)
+    other_away = swap(away, c=1)
     away, other_half, *pieces = together((away, other_half, *pieces))
-    other_away = swap(away, c=1)
-    own0, own12, own3, weight = own_kv_parts(pieces, (half, other_half))
-    own12, weight = together((own12, weight))
-    own_came = swap(own12, x=1)
-    in0, in1, in32 = input_grad_pieces(grads, weight)
-    in_came = swap(in32, x=3)
-    other_away, in0 = together((other_away, in0))
+    own0, own1, own2, own3, weight = own_kv_parts(pieces, (half, other_half))
+    own_came = [swap(own2, x=2), swap(own1, x=1), swap(own3, x=3)]
+    other_away, weight = together((other_away, weight))
     sum0, sum12, sum3 = chip_sum(home, other_away)
     sum_came = swap(sum12, y=1)
-
-    own_came = together((own_came, sum12))[0]
-    own_leave = (own3 + own_came[SEG:].astype(F32)).astype(BF16)
-    own_last = swap(own_leave, x=3)
-    in_came = together((in_came, own_leave))[0]
-    leave03 = rows([in0, in_came[:SEG]])
-    leave12 = rows([in1, in_came[SEG:]])
-    back03 = swap_back_section(leave03)
-    back12 = swap_back_section(leave12, x=1)
-    token = together((lengths, leave03, leave12))[0]
-    fwd_out = own_groups(token, front_q, (own0, own_came, own_last), held)
+    weight = together((weight, sum12))[0]
+    leave = input_grad_pieces(grads, weight)
+    here = lax.ppermute(leave, "pipe", [(p + 1, p) for p in range(3)])
+    own_came = together((*own_came, leave))[:3]
+    own2, own1, own3 = own_came
+    fwd_out = own_groups(lengths, front_q, (own0, own1, own2, own3), held)
     next_act = lax.ppermute(fwd_out, "pipe", [(p, p + 1) for p in range(3)])
-
     sum_came = together((sum_came, fwd_out))[0]
     sum_leave = (sum3 + sum_came[2 * BLK :].astype(F32)).astype(BF16)
     sum_last = swap(sum_leave, y=3)
+    here = together((here, sum_leave))[0]
+    in_came = swap(here[2 * SEG :], x=3)
     total = sum0 + sum_came[: 2 * BLK].astype(F32) + sum_last.astype(F32)
     far_total = total[BLK:].astype(BF16)
     far_came = swap(far_total, z=1)
-    back03 = together((back03, far_total))[0]
-    prev_grad = join_pieces(back03, back12)
+    in_came = together((in_came, far_total))[0]
+    in_last = swap(rows([here[SEG : 2 * SEG], in_came[SEG:]]), x=1)
+    prev_grad, next_act = join_pieces(here, in_came, in_last, next_act)
     weight_grad = total[:BLK] + far_came.astype(F32)
     return (next_act[None, None], grad_query[None, None], prev_grad[None, None], weight_grad[None])
 

time: 86.3 us -> 79.8 us (0.925)
  the two profiles are of different devices: /device:TPU:32 before, /device:TPU:64 now
where the time goes in v3:
time: 79.8 us; the launch traced here: 79.6 us
  starting transfers between devices  34.9 us (44%)
  Pallas kernels  22.3 us (28%)
  waiting for transfers between devices  20.3 us (25%)
  other arithmetic  0.96 us (1%)
  between operations  0.91 us (1%)
    ppermute x19, starting transfers between devices, swap(): lax.ppermute(value, 'dp', [(d, partner(d, **steps)) for d in range(64)])  29.1 us
    ppermute x19, waiting for transfers between devices, swap(): lax.ppermute(value, 'dp', [(d, partner(d, **steps)) for d in range(64)])  20.3 us
    pallas_call x1, Pallas kernels, backward_groups(): pl.pallas_call(backward_kernel, out_shape=[jax.ShapeDtypeStruct(q.shape,...  7.85 us
    pallas_call x2, Pallas kernels, stored_groups(): pl.pallas_call(functools.partial(stored_kernel, first), out_shape=[jax.Sh...  5.24 us
    ppermute x1, starting transfers between devices, shards(): next_act = lax.ppermute(fwd_out, 'pipe', [(p, p + 1) for p in range(3)])  2.92 us
    ppermute x1, starting transfers between devices, shards(): here = lax.ppermute(leave, 'pipe', [(p + 1, p) for p in range(3)])  2.92 us
    pallas_call x1, Pallas kernels, own_groups(): pl.pallas_call(own_kernel, out_shape=jax.ShapeDtypeStruct(q.shape, BF16),...  2.91 us
    pallas_call x1, Pallas kernels, split_inputs(): pl.pallas_call(split_kernel, out_shape=[jax.ShapeDtypeStruct((2 * SEG, 2...  2.52 us
  transfers between devices with their start and end apart: 21, of which 10 were waited for; matrix products, arithmetic and copies ran while one was open for 1% of the time, Pallas kernels for 26%

profile of v3, /device:TPU:64, one launch (start us, length us, event | category | flops | bytes accessed | tf_op | source)
XLA Modules:
  0.0 79.6 jit_solution(9976827596215482297)
XLA Ops:
  0.7 5.5 %collective-permute-start = (bf16[56,1024]{1,0:T(8,128)(2,1)}, bf16[56,1024]{1,0:T(8,128)(2,1)S(1)}, u32[]{:S(2)}, u32[]{:S(2)}) collective-permute-start(bf16[56,1024]{1,0:T(8,128)(2,1)} %bitcast.25), channel_id=1, source_target_pairs={{0,128},{4,132},{8,136},{12,140},{16,144},{20,148},{24,152},{28,15... | collective-permute-start | bytes 344072 | tf_op jit(solution)/shard_map/ppermute | solution.py:46
  6.2 2.5 %split_inputs.1 = (bf16[128,896]{1,0:T(8,128)(2,1)}, bf16[128,896]{1,0:T(8,128)(2,1)}, bf16[128,896]{1,0:T(8,128)(2,1)}, bf16[128,896]{1,0:T(8,128)(2,1)}) custom-call(bf16[64,3584]{1,0:T(8,128)(2,1)} %bitcast.27, bf16[64,3584]{1,0:T(8,128)(2,1)} %bitcast.28), custom_call_target="tpu_custom_call" | custom-call | flops 750000000 | bytes 1500000 | tf_op jit(solution)/shard_map/split_inputs/pallas_call | solution.py:73
  8.7 1.6 %collective-permute-start.2 = (bf16[128,896]{1,0:T(8,128)(2,1)}, bf16[128,896]{1,0:T(8,128)(2,1)S(1)}, u32[]{:S(2)}, u32[]{:S(2)}) collective-permute-start(bf16[128,896]{1,0:T(8,128)(2,1)} %get-tuple-element.63), channel_id=1, source_target_pairs={{0,32},{4,36},{8,40},{12,44},{16,48},{20,52},{24,56},{28,60},{32,0... | collective-permute-start | bytes 688136 | tf_op jit(solution)/shard_map/ppermute | solution.py:46
  10.3 2.7 %collective-permute-start.3 = (bf16[128,896]{1,0:T(8,128)(2,1)}, bf16[128,896]{1,0:T(8,128)(2,1)S(1)}, u32[]{:S(2)}, u32[]{:S(2)}) collective-permute-start(bf16[128,896]{1,0:T(8,128)(2,1)} %get-tuple-element.64), channel_id=1, source_target_pairs={{0,64},{4,68},{8,72},{12,76},{16,80},{20,84},{24,88},{28,92},{32,9... | collective-permute-start | bytes 688136 | tf_op jit(solution)/shard_map/ppermute | solution.py:46
  13.0 0.5 collective-permute-start.4
  13.5 0.0 collective-permute-done
  13.5 1.7 %collective-permute-start.1 = (bf16[112,1024]{1,0:T(8,128)(2,1)S(1)}, bf16[112,1024]{1,0:T(8,128)(2,1)S(1)}, u32[]{:S(2)}, u32[]{:S(2)}) collective-permute-start(bf16[112,1024]{1,0:T(8,128)(2,1)S(1)} %pad_maximum_fusion.2), channel_id=1, source_target_pairs={{0,8},{4,12},{8,0},{12,4},{16,24},{20,28},{24,16},{28,20},{32,40},... | collective-permute-start | bytes 688136 | tf_op jit(solution)/shard_map/ppermute | solution.py:46
  15.2 0.0 copy-start.3
  15.2 7.8 %backward_groups.1 = (bf16[64,3584]{1,0:T(8,128)(2,1)}, bf16[64,1024]{1,0:T(8,128)(2,1)S(1)}) custom-call(s32[4]{0:T(128)S(1)} %bitcast.21, bf16[64,3584]{1,0:T(8,128)(2,1)S(1)} %bitcast.16, bf16[64,3584]{1,0:T(8,128)(2,1)S(1)} %bitcast.17, bf16[1024,1024]{1,0:T(8,128)(2,1)S(1)} %bitcast.13), custom_call_target="tpu_custom_call" | custom-call | flops 3500000000 | bytes 7000000 | tf_op jit(solution)/shard_map/backward_groups/pallas_call | solution.py:190
  23.0 0.0 collective-permute-done.1
  23.1 0.2 collective-permute-done.3.r2
  23.3 2.6 %collective-permute-done.4.r3 = bf16[128,896]{1,0:T(8,128)(2,1)S(1)} collective-permute-done((bf16[128,896]{1,0:T(8,128)(2,1)}, bf16[128,896]{1,0:T(8,128)(2,1)S(1)}, u32[]{:S(2)}, u32[]{:S(2)}) %collective-permute-start.4) | collective-permute-done | bytes 229408 | tf_op jit(solution)/shard_map/ppermute | solution.py:46
  25.8 3.0 %collective-permute-start.5 = (bf16[224,1024]{1,0:T(8,128)(2,1)S(1)}, bf16[224,1024]{1,0:T(8,128)(2,1)S(1)}, u32[]{:S(2)}, u32[]{:S(2)}) collective-permute-start(bf16[224,1024]{1,0:T(8,128)(2,1)S(1)} %pad_maximum_fusion.1), channel_id=1, source_target_pairs={{0,24},{4,28},{8,16},{12,20},{16,8},{20,12},{24,0},{28,4},{32,56},... | collective-permute-start | bytes 1376264 | tf_op jit(solution)/shard_map/ppermute | solution.py:46
  28.9 1.7 %collective-permute-start.7 = (bf16[64,1024]{1,0:T(8,128)(2,1)S(1)}, bf16[64,1024]{1,0:T(8,128)(2,1)S(1)}, u32[]{:S(2)}, u32[]{:S(2)}) collective-permute-start(bf16[64,1024]{1,0:T(8,128)(2,1)S(1)} %get-tuple-element.73.g0), channel_id=1, source_target_pairs={{0,96},{4,100},{8,104},{12,108},{16,112},{20,116},{24,120},{28,124... | collective-permute-start | bytes 393224 | tf_op jit(solution)/shard_map/ppermute | solution.py:46
  30.5 1.8 %collective-permute-start.6 = (bf16[64,1024]{1,0:T(8,128)(2,1)S(1)}, bf16[64,1024]{1,0:T(8,128)(2,1)S(1)}, u32[]{:S(2)}, u32[]{:S(2)}) collective-permute-start(bf16[64,1024]{1,0:T(8,128)(2,1)S(1)} %get-tuple-element.73.g0), channel_id=1, source_target_pairs={{0,32},{4,36},{8,40},{12,44},{16,48},{20,52},{24,56},{28,60},{32,0... | collective-permute-start | bytes 393224 | tf_op jit(solution)/shard_map/ppermute | solution.py:46
  32.3 2.6 %stored_groups.2 = (f32[64,1792]{1,0:T(8,128)S(1)}, f32[64,256]{1,0:T(8,128)S(1)}) custom-call(s32[4]{0:T(128)S(1)} %bitcast.22, bf16[64,3584]{1,0:T(8,128)(2,1)S(1)} %bitcast.18, bf16[1024,1024]{1,0:T(8,128)(2,1)S(1)} %bitcast.14), custom_call_target="tpu_custom_call" | custom-call | flops 1200000000 | bytes 2400000 | tf_op jit(solution)/shard_map/stored_groups/pallas_call | solution.py:237
  35.0 2.6 %stored_groups.3 = (f32[64,1792]{1,0:T(8,128)S(1)}, f32[64,256]{1,0:T(8,128)S(1)}) custom-call(s32[4]{0:T(128)S(1)} %bitcast.23, bf16[64,3584]{1,0:T(8,128)(2,1)S(1)} %bitcast.19, bf16[1024,1024]{1,0:T(8,128)(2,1)S(1)} %bitcast.15), custom_call_target="tpu_custom_call" | custom-call | flops 1200000000 | bytes 2400000 | tf_op jit(solution)/shard_map/stored_groups/pallas_call | solution.py:237
  37.6 0.0 copy-start.5
  37.6 0.6 collective-permute-done.5
  38.2 0.1 pad_maximum_fusion.a_ref
  38.3 0.1 collective-permute-start.10
  38.4 0.1 copy-done.5
  38.5 0.9 %weight_grad_halves.1 = (bf16[448,1024]{1,0:T(8,128)(2,1)S(1)}, f32[448,1024]{1,0:T(8,128)S(1)}) custom-call(bf16[128,896]{1,0:T(8,128)(2,1)S(1)} %copy-done.5, bf16[128,896]{1,0:T(8,128)(2,1)S(1)} %collective-permute-done.2.r1, bf16[128,896]{1,0:T(8,128)(2,1)S(1)} %collective-permute-done.3.r2, bf16[128,896]{1,0:T(8,128)(2,1)S(1)} %collective-permute-done.4.r3, ...), custom_call_target="tpu_custom_call" | custom-call | flops 750000000 | bytes 1500000 | tf_op jit(solution)/shard_map/weight_grad_halves/pallas_call | solution.py:353
  39.4 0.4 collective-permute-start.9
  39.9 1.0 %collective-permute-done.10.b_ref = bf16[448,1024]{1,0:T(8,128)(2,1)S(1)} collective-permute-done((bf16[448,1024]{1,0:T(8,128)(2,1)S(1)}, bf16[448,1024]{1,0:T(8,128)(2,1)S(1)}, u32[]{:S(2)}, u32[]{:S(2)}) %collective-permute-start.10) | collective-permute-done | bytes 917536 | tf_op jit(solution)/shard_map/ppermute | solution.py:46
  40.9 0.9 %own_kv_parts.1 = (f32[64,1024]{1,0:T(8,128)S(1)}, bf16[64,1024]{1,0:T(8,128)(2,1)S(1)}, bf16[64,1024]{1,0:T(8,128)(2,1)S(1)}, bf16[64,1024]{1,0:T(8,128)(2,1)S(1)}, bf16[896,1024]{1,0:T(8,128)(2,1)S(1)}) custom-call(bf16[128,896]{1,0:T(8,128)(2,1)S(1)} %copy-done.5, bf16[128,896]{1,0:T(8,128)(2,1)S(1)} %collective-permute-done.2.r1, ...), custom_call_target="tpu_custom_call" | custom-call | flops 750000000 | bytes 1500000 | tf_op jit(solution)/shard_map/own_kv_parts/pallas_call | solution.py:310
  41.7 0.4 collective-permute-done.9.other_ref
  42.2 0.1 chip_sum.1
  42.3 0.6 collective-permute-start.12
  42.9 0.9 %collective-permute-start.13 = (bf16[64,1024]{1,0:T(8,128)(2,1)S(1)}, bf16[64,1024]{1,0:T(8,128)(2,1)S(1)}, u32[]{:S(2)}, u32[]{:S(2)}) collective-permute-start(bf16[64,1024]{1,0:T(8,128)(2,1)S(1)} %get-tuple-element.96), channel_id=1, source_target_pairs={{0,64},{4,68},{8,72},{12,76},{16,80},{20,84},{24,88},{28,92},{32,9... | collective-permute-start | bytes 393224 | tf_op jit(solution)/shard_map/ppermute | solution.py:46
  43.7 0.5 collective-permute-start.14
  44.2 2.8 %collective-permute-start.15 = (bf16[64,1024]{1,0:T(8,128)(2,1)S(1)}, bf16[64,1024]{1,0:T(8,128)(2,1)S(1)}, u32[]{:S(2)}, u32[]{:S(2)}) collective-permute-start(bf16[64,1024]{1,0:T(8,128)(2,1)S(1)} %get-tuple-element.98), channel_id=1, source_target_pairs={{0,96},{4,100},{8,104},{12,108},{16,112},{20,116},{24,120},{28,124... | collective-permute-start | bytes 393224 | tf_op jit(solution)/shard_map/ppermute | solution.py:46
  47.0 0.7 input_grad_pieces.1
  47.7 2.9 %collective-permute-start.11 = (bf16[256,896]{1,0:T(8,128)(2,1)S(1)}, bf16[256,896]{1,0:T(8,128)(2,1)S(1)}, u32[]{:S(2)}, u32[]{:S(2)}) collective-permute-start(bf16[256,896]{1,0:T(8,128)(2,1)S(1)} %input_grad_pieces.1), channel_id=1, source_target_pairs={{1,0},{2,1},{3,2},{5,4},{6,5},{7,6},{9,8},{10,9},{11,10},{13,12},{... | collective-permute-start | bytes 1376264 | tf_op jit(solution)/shard_map/ppermute | solution.py:450
  50.7 0.1 collective-permute-done.13.k2
  50.8 1.8 %collective-permute-done.15.k3 = bf16[64,1024]{1,0:T(8,128)(2,1)S(1)} collective-permute-done((bf16[64,1024]{1,0:T(8,128)(2,1)S(1)}, bf16[64,1024]{1,0:T(8,128)(2,1)S(1)}, u32[]{:S(2)}, u32[]{:S(2)}) %collective-permute-start.15) | collective-permute-done | bytes 131104 | tf_op jit(solution)/shard_map/ppermute | solution.py:46
  52.6 2.9 %own_groups.1 = bf16[64,3584]{1,0:T(8,128)(2,1)S(1)} custom-call(s32[4]{0:T(128)S(1)} %bitcast.24, bf16[64,3584]{1,0:T(8,128)(2,1)S(1)} %bitcast.20, f32[64,1024]{1,0:T(8,128)S(1)} %get-tuple-element.95.k0, bf16[64,1024]{1,0:T(8,128)(2,1)S(1)} %collective-permute-done.14.k1, bf16[64,1024]{1,0:T(8,128)(2,1)S(1)} %collective-permute-done.13.k2, ...), custom_call_target="tpu_custom_call" | custom-call | flops 1000000000 | bytes 2000000 | tf_op jit(solution)/shard_map/own_groups/pallas_call | solution.py:281
  55.6 3.0 %collective-permute-start.17 = (bf16[112,1024]{1,0:T(8,128)(2,1)S(1)}, bf16[112,1024]{1,0:T(8,128)(2,1)S(1)}, u32[]{:S(2)}, u32[]{:S(2)}) collective-permute-start(bf16[112,1024]{1,0:T(8,128)(2,1)S(1)} %add_convert_fusion), channel_id=1, source_target_pairs={{0,24},{4,28},{8,16},{12,20},{16,8},{20,12},{24,0},{28,4},{32,56},... | collective-permute-start | bytes 688136 | tf_op jit(solution)/shard_map/ppermute | solution.py:46
  58.6 2.9 %collective-permute-start.19 = (bf16[64,3584]{1,0:T(8,128)(2,1)S(1)}, bf16[64,3584]{1,0:T(8,128)(2,1)S(1)}, u32[]{:S(2)}, u32[]{:S(2)}) collective-permute-start(bf16[64,3584]{1,0:T(8,128)(2,1)S(1)} %own_groups.1), channel_id=1, source_target_pairs={{0,1},{1,2},{2,3},{4,5},{5,6},{6,7},{8,9},{9,10},{10,11},{12,13},{... | collective-permute-start | bytes 1376264 | tf_op jit(solution)/shard_map/ppermute | solution.py:454
  61.6 0.9 %collective-permute-start.16 = (bf16[128,896]{1,0:T(8,128)(2,1)S(1)}, bf16[128,896]{1,0:T(8,128)(2,1)S(1)}, u32[]{:S(2)}, u32[]{:S(2)}) collective-permute-start(bf16[128,896]{1,0:T(8,128)(2,1)S(1)} %slice.23), channel_id=1, source_target_pairs={{0,96},{4,100},{8,104},{12,108},{16,112},{20,116},{24,120},{28,124... | collective-permute-start | bytes 688136 | tf_op jit(solution)/shard_map/ppermute | solution.py:46
  62.5 1.9 %collective-permute-done.17 = bf16[112,1024]{1,0:T(8,128)(2,1)S(1)} collective-permute-done((bf16[112,1024]{1,0:T(8,128)(2,1)S(1)}, bf16[112,1024]{1,0:T(8,128)(2,1)S(1)}, u32[]{:S(2)}, u32[]{:S(2)}) %collective-permute-start.17) | collective-permute-done | bytes 229408 | tf_op jit(solution)/shard_map/ppermute | solution.py:46
  64.4 0.1 convert_add_fusion
  64.5 1.4 %collective-permute-start.20 = (bf16[56,1024]{1,0:T(8,128)(2,1)S(1)}, bf16[56,1024]{1,0:T(8,128)(2,1)S(1)}, u32[]{:S(2)}, u32[]{:S(2)}) collective-permute-start(bf16[56,1024]{1,0:T(8,128)(2,1)S(1)} %slice.37), channel_id=1, source_target_pairs={{0,128},{4,132},{8,136},{12,140},{16,144},{20,148},{24,152},{28,15... | collective-permute-start | bytes 344072 | tf_op jit(solution)/shard_map/ppermute | solution.py:46
  65.9 4.0 %collective-permute-done.16.g32 = bf16[128,896]{1,0:T(8,128)(2,1)S(1)} collective-permute-done((bf16[128,896]{1,0:T(8,128)(2,1)S(1)}, bf16[128,896]{1,0:T(8,128)(2,1)S(1)}, u32[]{:S(2)}, u32[]{:S(2)}) %collective-permute-start.16) | collective-permute-done | bytes 229408 | tf_op jit(solution)/shard_map/ppermute | solution.py:46
  69.9 0.1 collective-permute-start.18
  70.0 7.7 %collective-permute-done.20 = bf16[56,1024]{1,0:T(8,128)(2,1)S(1)} collective-permute-done((bf16[56,1024]{1,0:T(8,128)(2,1)S(1)}, bf16[56,1024]{1,0:T(8,128)(2,1)S(1)}, u32[]{:S(2)}, u32[]{:S(2)}) %collective-permute-start.20) | collective-permute-done | bytes 114720 | tf_op jit(solution)/shard_map/ppermute | solution.py:46
  77.7 0.7 fusion
  78.5 1.1 %join_pieces.1 = (bf16[64,3584]{1,0:T(8,128)(2,1)}, bf16[64,3584]{1,0:T(8,128)(2,1)}) custom-call(bf16[256,896]{1,0:T(8,128)(2,1)S(1)} %collective-permute-done.11.here, bf16[128,896]{1,0:T(8,128)(2,1)S(1)} %collective-permute-done.16.g32, bf16[128,896]{1,0:T(8,128)(2,1)S(1)} %collective-permute-done.18.g12, bf16[64,3584]{1,0:T(8,128)(2,1)S(1)} %collective-permute-done.19.act_ref), custom_call_target="tpu_custom_call" | custom-call | flops 500000000 | bytes 1000000 | tf_op jit(solution)/shard_map/join_pieces/pallas_call | solution.py:101
  (29 shorter events, 0.2 us)
Async XLA Ops:
  0.6 12.8 %copy-start.6 = (bf16[1,56,1024]{2,1,0:T(8,128)(2,1)S(1)}, bf16[1,56,1024]{2,1,0:T(8,128)(2,1)}, u32[]{:S(2)}) copy-start(bf16[1,56,1024]{2,1,0:T(8,128)(2,1)} %param.14) | copy-start | bytes 344068
  0.6 14.5 %copy-start.4 = (s32[1,1,4]{2,1,0:T(1,128)S(1)}, s32[1,1,4]{2,1,0:T(1,128)}, u32[]{:S(2)}) copy-start(s32[1,1,4]{2,1,0:T(1,128)} %param.15) | copy-start | bytes 52
  0.7 14.5 %copy-start = (bf16[1,1,1024,1024]{3,2,1,0:T(8,128)(2,1)S(1)}, bf16[1,1,1024,1024]{3,2,1,0:T(8,128)(2,1)}, u32[]{:S(2)}) copy-start(bf16[1,1,1024,1024]{3,2,1,0:T(8,128)(2,1)} %param.13) | copy-start | bytes 6291460
  0.7 14.5 %copy-start.2 = (bf16[1,1,64,3584]{3,2,1,0:T(8,128)(2,1)S(1)}, bf16[1,1,64,3584]{3,2,1,0:T(8,128)(2,1)}, u32[]{:S(2)}) copy-start(bf16[1,1,64,3584]{3,2,1,0:T(8,128)(2,1)} %param.12) | copy-start | bytes 1376260
  0.7 14.5 %copy-start.1 = (bf16[1,1,64,3584]{3,2,1,0:T(8,128)(2,1)S(1)}, bf16[1,1,64,3584]{3,2,1,0:T(8,128)(2,1)}, u32[]{:S(2)}) copy-start(bf16[1,1,64,3584]{3,2,1,0:T(8,128)(2,1)} %param.11) | copy-start | bytes 1376260
  0.7 12.8 %collective-permute-start = (bf16[56,1024]{1,0:T(8,128)(2,1)}, bf16[56,1024]{1,0:T(8,128)(2,1)S(1)}, u32[]{:S(2)}, u32[]{:S(2)}) collective-permute-start(bf16[56,1024]{1,0:T(8,128)(2,1)} %bitcast.25), channel_id=1, source_target_pairs={{0,128},{4,132},{8,136},{12,140},{16,144},{20,148},{24,152},{28,15... | collective-permute-start | bytes 344072 | tf_op jit(solution)/shard_map/ppermute | solution.py:46
  8.7 14.4 %collective-permute-start.2 = (bf16[128,896]{1,0:T(8,128)(2,1)}, bf16[128,896]{1,0:T(8,128)(2,1)S(1)}, u32[]{:S(2)}, u32[]{:S(2)}) collective-permute-start(bf16[128,896]{1,0:T(8,128)(2,1)} %get-tuple-element.63), channel_id=1, source_target_pairs={{0,32},{4,36},{8,40},{12,44},{16,48},{20,52},{24,56},{28,60},{32,0... | collective-permute-start | bytes 688136 | tf_op jit(solution)/shard_map/ppermute | solution.py:46
  10.3 13.0 %collective-permute-start.3 = (bf16[128,896]{1,0:T(8,128)(2,1)}, bf16[128,896]{1,0:T(8,128)(2,1)S(1)}, u32[]{:S(2)}, u32[]{:S(2)}) collective-permute-start(bf16[128,896]{1,0:T(8,128)(2,1)} %get-tuple-element.64), channel_id=1, source_target_pairs={{0,64},{4,68},{8,72},{12,76},{16,80},{20,84},{24,88},{28,92},{32,9... | collective-permute-start | bytes 688136 | tf_op jit(solution)/shard_map/ppermute | solution.py:46
  13.0 12.8 %collective-permute-start.4 = (bf16[128,896]{1,0:T(8,128)(2,1)}, bf16[128,896]{1,0:T(8,128)(2,1)S(1)}, u32[]{:S(2)}, u32[]{:S(2)}) collective-permute-start(bf16[128,896]{1,0:T(8,128)(2,1)} %get-tuple-element.65), channel_id=1, source_target_pairs={{0,96},{4,100},{8,104},{12,108},{16,112},{20,116},{24,120},{28,124... | collective-permute-start | bytes 688136 | tf_op jit(solution)/shard_map/ppermute | solution.py:46
  13.5 9.5 %collective-permute-start.1 = (bf16[112,1024]{1,0:T(8,128)(2,1)S(1)}, bf16[112,1024]{1,0:T(8,128)(2,1)S(1)}, u32[]{:S(2)}, u32[]{:S(2)}) collective-permute-start(bf16[112,1024]{1,0:T(8,128)(2,1)S(1)} %pad_maximum_fusion.2), channel_id=1, source_target_pairs={{0,8},{4,12},{8,0},{12,4},{16,24},{20,28},{24,16},{28,20},{32,40},... | collective-permute-start | bytes 688136 | tf_op jit(solution)/shard_map/ppermute | solution.py:46
  15.2 17.2 %copy-start.3 = (bf16[1,1,64,3584]{3,2,1,0:T(8,128)(2,1)S(1)}, bf16[1,1,64,3584]{3,2,1,0:T(8,128)(2,1)}, u32[]{:S(2)}) copy-start(bf16[1,1,64,3584]{3,2,1,0:T(8,128)(2,1)} %param.9) | copy-start | bytes 1376260
  25.8 12.4 %collective-permute-start.5 = (bf16[224,1024]{1,0:T(8,128)(2,1)S(1)}, bf16[224,1024]{1,0:T(8,128)(2,1)S(1)}, u32[]{:S(2)}, u32[]{:S(2)}) collective-permute-start(bf16[224,1024]{1,0:T(8,128)(2,1)S(1)} %pad_maximum_fusion.1), channel_id=1, source_target_pairs={{0,24},{4,28},{8,16},{12,20},{16,8},{20,12},{24,0},{28,4},{32,56},... | collective-permute-start | bytes 1376264 | tf_op jit(solution)/shard_map/ppermute | solution.py:46
  28.9 9.4 %collective-permute-start.8 = (bf16[64,1024]{1,0:T(8,128)(2,1)S(1)}, bf16[64,1024]{1,0:T(8,128)(2,1)S(1)}, u32[]{:S(2)}, u32[]{:S(2)}) collective-permute-start(bf16[64,1024]{1,0:T(8,128)(2,1)S(1)} %get-tuple-element.73.g0), channel_id=1, source_target_pairs={{0,64},{4,68},{8,72},{12,76},{16,80},{20,84},{24,88},{28,92},{32,9... | collective-permute-start | bytes 393224 | tf_op jit(solution)/shard_map/ppermute | solution.py:46
  28.9 9.4 %collective-permute-start.7 = (bf16[64,1024]{1,0:T(8,128)(2,1)S(1)}, bf16[64,1024]{1,0:T(8,128)(2,1)S(1)}, u32[]{:S(2)}, u32[]{:S(2)}) collective-permute-start(bf16[64,1024]{1,0:T(8,128)(2,1)S(1)} %get-tuple-element.73.g0), channel_id=1, source_target_pairs={{0,96},{4,100},{8,104},{12,108},{16,112},{20,116},{24,120},{28,124... | collective-permute-start | bytes 393224 | tf_op jit(solution)/shard_map/ppermute | solution.py:46
  30.5 7.8 %collective-permute-start.6 = (bf16[64,1024]{1,0:T(8,128)(2,1)S(1)}, bf16[64,1024]{1,0:T(8,128)(2,1)S(1)}, u32[]{:S(2)}, u32[]{:S(2)}) collective-permute-start(bf16[64,1024]{1,0:T(8,128)(2,1)S(1)} %get-tuple-element.73.g0), channel_id=1, source_target_pairs={{0,32},{4,36},{8,40},{12,44},{16,48},{20,52},{24,56},{28,60},{32,0... | collective-permute-start | bytes 393224 | tf_op jit(solution)/shard_map/ppermute | solution.py:46
  37.6 0.9 %copy-start.5 = (bf16[128,896]{1,0:T(8,128)(2,1)S(1)}, bf16[128,896]{1,0:T(8,128)(2,1)}, u32[]{:S(2)}) copy-start(bf16[128,896]{1,0:T(8,128)(2,1)} %get-tuple-element.83.r0) | copy-start | bytes 688132
  38.3 2.6 %collective-permute-start.10 = (bf16[448,1024]{1,0:T(8,128)(2,1)S(1)}, bf16[448,1024]{1,0:T(8,128)(2,1)S(1)}, u32[]{:S(2)}, u32[]{:S(2)}) collective-permute-start(bf16[448,1024]{1,0:T(8,128)(2,1)S(1)} %pad_maximum_fusion.a_ref), channel_id=1, source_target_pairs={{0,4},{4,0},{8,12},{12,8},{16,20},{20,16},{24,28},{28,24},{32,36},... | collective-permute-start | bytes 2752520 | tf_op jit(solution)/shard_map/ppermute | solution.py:46
  39.4 2.8 %collective-permute-start.9 = (bf16[448,1024]{1,0:T(8,128)(2,1)S(1)}, bf16[448,1024]{1,0:T(8,128)(2,1)S(1)}, u32[]{:S(2)}, u32[]{:S(2)}) collective-permute-start(bf16[448,1024]{1,0:T(8,128)(2,1)S(1)} %get-tuple-element.81), channel_id=1, source_target_pairs={{0,4},{4,0},{8,12},{12,8},{16,20},{20,16},{24,28},{28,24},{32,36},... | collective-permute-start | bytes 2752520 | tf_op jit(solution)/shard_map/ppermute | solution.py:46
  42.3 13.2 %collective-permute-start.12 = (bf16[224,1024]{1,0:T(8,128)(2,1)S(1)}, bf16[224,1024]{1,0:T(8,128)(2,1)S(1)}, u32[]{:S(2)}, u32[]{:S(2)}) collective-permute-start(bf16[224,1024]{1,0:T(8,128)(2,1)S(1)} %get-tuple-element.92), channel_id=1, source_target_pairs={{0,8},{4,12},{8,0},{12,4},{16,24},{20,28},{24,16},{28,20},{32,40},... | collective-permute-start | bytes 1376264 | tf_op jit(solution)/shard_map/ppermute | solution.py:46
  42.9 7.9 %collective-permute-start.13 = (bf16[64,1024]{1,0:T(8,128)(2,1)S(1)}, bf16[64,1024]{1,0:T(8,128)(2,1)S(1)}, u32[]{:S(2)}, u32[]{:S(2)}) collective-permute-start(bf16[64,1024]{1,0:T(8,128)(2,1)S(1)} %get-tuple-element.96), channel_id=1, source_target_pairs={{0,64},{4,68},{8,72},{12,76},{16,80},{20,84},{24,88},{28,92},{32,9... | collective-permute-start | bytes 393224 | tf_op jit(solution)/shard_map/ppermute | solution.py:46
  43.7 7.0 %collective-permute-start.14 = (bf16[64,1024]{1,0:T(8,128)(2,1)S(1)}, bf16[64,1024]{1,0:T(8,128)(2,1)S(1)}, u32[]{:S(2)}, u32[]{:S(2)}) collective-permute-start(bf16[64,1024]{1,0:T(8,128)(2,1)S(1)} %get-tuple-element.97), channel_id=1, source_target_pairs={{0,32},{4,36},{8,40},{12,44},{16,48},{20,52},{24,56},{28,60},{32,0... | collective-permute-start | bytes 393224 | tf_op jit(solution)/shard_map/ppermute | solution.py:46
  44.2 8.3 %collective-permute-start.15 = (bf16[64,1024]{1,0:T(8,128)(2,1)S(1)}, bf16[64,1024]{1,0:T(8,128)(2,1)S(1)}, u32[]{:S(2)}, u32[]{:S(2)}) collective-permute-start(bf16[64,1024]{1,0:T(8,128)(2,1)S(1)} %get-tuple-element.98), channel_id=1, source_target_pairs={{0,96},{4,100},{8,104},{12,108},{16,112},{20,116},{24,120},{28,124... | collective-permute-start | bytes 393224 | tf_op jit(solution)/shard_map/ppermute | solution.py:46
  47.7 13.8 %collective-permute-start.11 = (bf16[256,896]{1,0:T(8,128)(2,1)S(1)}, bf16[256,896]{1,0:T(8,128)(2,1)S(1)}, u32[]{:S(2)}, u32[]{:S(2)}) collective-permute-start(bf16[256,896]{1,0:T(8,128)(2,1)S(1)} %input_grad_pieces.1), channel_id=1, source_target_pairs={{1,0},{2,1},{3,2},{5,4},{6,5},{7,6},{9,8},{10,9},{11,10},{13,12},{... | collective-permute-start | bytes 1376264 | tf_op jit(solution)/shard_map/ppermute | solution.py:450
  55.6 8.8 %collective-permute-start.17 = (bf16[112,1024]{1,0:T(8,128)(2,1)S(1)}, bf16[112,1024]{1,0:T(8,128)(2,1)S(1)}, u32[]{:S(2)}, u32[]{:S(2)}) collective-permute-start(bf16[112,1024]{1,0:T(8,128)(2,1)S(1)} %add_convert_fusion), channel_id=1, source_target_pairs={{0,24},{4,28},{8,16},{12,20},{16,8},{20,12},{24,0},{28,4},{32,56},... | collective-permute-start | bytes 688136 | tf_op jit(solution)/shard_map/ppermute | solution.py:46
  58.6 19.8 %collective-permute-start.19 = (bf16[64,3584]{1,0:T(8,128)(2,1)S(1)}, bf16[64,3584]{1,0:T(8,128)(2,1)S(1)}, u32[]{:S(2)}, u32[]{:S(2)}) collective-permute-start(bf16[64,3584]{1,0:T(8,128)(2,1)S(1)} %own_groups.1), channel_id=1, source_target_pairs={{0,1},{1,2},{2,3},{4,5},{5,6},{6,7},{8,9},{9,10},{10,11},{12,13},{... | collective-permute-start | bytes 1376264 | tf_op jit(solution)/shard_map/ppermute | solution.py:454
  61.6 8.3 %collective-permute-start.16 = (bf16[128,896]{1,0:T(8,128)(2,1)S(1)}, bf16[128,896]{1,0:T(8,128)(2,1)S(1)}, u32[]{:S(2)}, u32[]{:S(2)}) collective-permute-start(bf16[128,896]{1,0:T(8,128)(2,1)S(1)} %slice.23), channel_id=1, source_target_pairs={{0,96},{4,100},{8,104},{12,108},{16,112},{20,116},{24,120},{28,124... | collective-permute-start | bytes 688136 | tf_op jit(solution)/shard_map/ppermute | solution.py:46
  64.5 13.2 %collective-permute-start.20 = (bf16[56,1024]{1,0:T(8,128)(2,1)S(1)}, bf16[56,1024]{1,0:T(8,128)(2,1)S(1)}, u32[]{:S(2)}, u32[]{:S(2)}) collective-permute-start(bf16[56,1024]{1,0:T(8,128)(2,1)S(1)} %slice.37), channel_id=1, source_target_pairs={{0,128},{4,132},{8,136},{12,140},{16,144},{20,148},{24,152},{28,15... | collective-permute-start | bytes 344072 | tf_op jit(solution)/shard_map/ppermute | solution.py:46
  69.9 8.6 %collective-permute-start.18 = (bf16[128,896]{1,0:T(8,128)(2,1)S(1)}, bf16[128,896]{1,0:T(8,128)(2,1)S(1)}, u32[]{:S(2)}, u32[]{:S(2)}) collective-permute-start(bf16[128,896]{1,0:T(8,128)(2,1)S(1)} %pad_maximum_fusion.3), channel_id=1, source_target_pairs={{0,32},{4,36},{8,40},{12,44},{16,48},{20,52},{24,56},{28,60},{32,0... | collective-permute-start | bytes 688136 | tf_op jit(solution)/shard_map/ppermute | solution.py:46

commit v4 on v3

--- a/solution.py
+++ b/solution.py
@@ -87,27 +87,27 @@
     )(fx, bx)
 
 
-def join_kernel(here, g32, g12, act_ref, out_ref, act_out, scr):
+def join_kernel(g0, g1, g2, g3, act_ref, out_ref, act_out, scr):
     act_out[...] = act_ref[...]
     z, x, _, _ = place()
-    for r, (piece, at) in enumerate(((here, 0), (g12, 0), (g12, SEG), (g32, 0))):
-        scr[z * 4 + (x ^ r)] = piece[at : at + SEG, :PART]
-        scr[(z ^ 1) * 4 + (x ^ r)] = piece[at : at + SEG, PART:]
+    for r, piece in enumerate((g0, g1, g2, g3)):
+        scr[z * 4 + (x ^ r)] = piece[0:SEG, :PART]
+        scr[(z ^ 1) * 4 + (x ^ r)] = piece[0:SEG, PART:]
     out_ref[...] = jnp.concatenate([scr[s] for s in range(8)], axis=1)
 
 
-def join_pieces(here, g32, g12, act):
+def join_pieces(g0, g1, g2, g3, act):
     vmem = pl.BlockSpec(memory_space=pltpu.VMEM)
     return pl.pallas_call(
         join_kernel,
         out_shape=[jax.ShapeDtypeStruct((SEG, 8 * PART), BF16)] * 2,
-        in_specs=[vmem] * 4,
+        in_specs=[vmem] * 5,
         out_specs=[vmem] * 2,
         scratch_shapes=[pltpu.VMEM((8, SEG, PART), BF16)],
         compiler_params=params(),
         cost_estimate=cost(1),
         name="join_pieces",
-    )(here, g32, g12, act)
+    )(g0, g1, g2, g3, act)
 
 
 def dot_nt(a, b):
@@ -144,45 +144,57 @@
 CHUNKS = (range(0, 4), range(4, 7))
 
 
-def backward_kernel(len_ref, q_ref, do_ref, cache_ref, gq_ref, kv_ref):
+def store_group(g, value, held, out_hbm, sems):
+    wide = slice(g * WIDE, (g + 1) * WIDE)
+    held[:, wide] = value
+    copy = pltpu.make_async_copy(held.at[:, wide], out_hbm.at[:, wide], sems.at[g])
+    copy.start()
+    return copy
+
+
+def backward_kernel(len_ref, q_ref, do_ref, cache_ref, gq_hbm, kv_ref, held, sems):
     third, fourth = len_ref[2], len_ref[3]
     base = cache_ref.shape[0] - 2 * SEG
     offset = 2 * SEG - fourth - third
-
-    @pl.loop(0, 4)
-    def _(g):
-        wide, key, value = group_columns(g)
-        keys, values = cache_ref[:, key], cache_ref[:, value]
-        queries = q_ref[:, wide]
-        live = lax.broadcasted_iota(jnp.int32, (SEG, WIDE), 0) < third
-        douts = jnp.where(live, do_ref[:, wide], jnp.zeros((SEG, WIDE), BF16))
-        dk = jnp.zeros((2 * SEG, HD), F32)
-        dv = jnp.zeros((2 * SEG, HD), F32)
-        grads = []
-        for heads in CHUNKS:
-            q, dout = stack_heads(queries, heads), stack_heads(douts, heads)
-            scores = dot_nt(q, keys)
-            along = dot_nt(dout, values)
-            shape = (q.shape[0], 2 * SEG)
-            ok = lax.broadcasted_iota(jnp.int32, shape, 1) <= offset + row_in_segment(shape)
-            tail = jnp.where(ok, scores[:, base:], -1e30)
-            scores = jnp.concatenate([scores[:, :base], tail], axis=1)
-            top = jnp.max(scores, axis=1, keepdims=True)
-            raised = jnp.exp2((scores - top) * EXP_SCALE)
-            probs = raised * (1.0 / jnp.sum(raised, axis=1, keepdims=True))
-            weighed = probs * along
-            delta = jnp.sum(weighed, axis=1, keepdims=True)
-            dscore = (weighed - probs * delta).astype(BF16)
-            grads.append((dot_nn(dscore, keys) * SCALE).astype(BF16))
-            dk = dk + dot_tn(dscore[:, base:], q)
-            dv = dv + dot_tn(probs[:, base:].astype(BF16), dout)
-        gq_ref[:, wide] = unstack_heads(grads)
-        keep = lax.broadcasted_iota(jnp.int32, (SEG, HD), 0) < third
-        shift = (2 * SEG - offset) & (2 * SEG - 1)
-        dk = pltpu.roll(dk * SCALE, shift, 0)[:SEG]
+    live = lax.broadcasted_iota(jnp.int32, (SEG, WIDE), 0) < third
+    keep = lax.broadcasted_iota(jnp.int32, (SEG, HD), 0) < third
+    shift = (2 * SEG - offset) & (2 * SEG - 1)
+    shape = (ROWS, 2 * SEG)
+    ok = lax.broadcasted_iota(jnp.int32, shape, 1) <= offset + row_in_segment(shape)
+
+    def products(g):
+        wide = slice(g * WIDE, (g + 1) * WIDE)
+        keys = cache_ref[:, g * HD : (g + 1) * HD]
+        values = cache_ref[:, (g + 4) * HD : (g + 5) * HD]
+        q = stack_heads(q_ref[:, wide], range(GROUP))
+        dout = jnp.where(live, do_ref[:, wide], jnp.zeros((SEG, WIDE), BF16))
+        dout = stack_heads(dout, range(GROUP))
+        return keys, q, dout, dot_nt(q, keys), dot_nt(dout, values)
+
+    copies = []
+    ahead = products(0)
+    for g in range(4):
+        keys, q, dout, scores, along = ahead
+        if g < 3:
+            ahead = products(g + 1)
+        tail = jnp.where(ok, scores[:, base:], -1e30)
+        scores = jnp.concatenate([scores[:, :base], tail], axis=1)
+        top = jnp.max(scores, axis=1, keepdims=True)
+        raised = jnp.exp2((scores - top) * EXP_SCALE)
+        probs = raised * (1.0 / jnp.sum(raised, axis=1, keepdims=True))
+        weighed = probs * along
+        delta = jnp.sum(weighed, axis=1, keepdims=True)
+        dscore = (weighed - probs * delta).astype(BF16)
+        grads = unstack_heads([(dot_nn(dscore, keys) * SCALE).astype(BF16)])
+        copies.append(store_group(g, grads, held, gq_hbm, sems))
+        dk = dot_tn(dscore[:, base:], q) * SCALE
+        dv = dot_tn(probs[:, base:].astype(BF16), dout)
+        dk = pltpu.roll(dk, shift, 0)[:SEG]
         dv = pltpu.roll(dv, shift, 0)[:SEG]
-        kv_ref[:, key] = jnp.where(keep, dk, 0.0).astype(BF16)
-        kv_ref[:, value] = jnp.where(keep, dv, 0.0).astype(BF16)
+        kv_ref[:, g * HD : (g + 1) * HD] = jnp.where(keep, dk, 0.0).astype(BF16)
+        kv_ref[:, (g + 4) * HD : (g + 5) * HD] = jnp.where(keep, dv, 0.0).astype(BF16)
+    for copy in copies:
+        copy.wait()
 
 
 def backward_groups(lengths, q, dout, cache):
@@ -194,7 +206,8 @@
             jax.ShapeDtypeStruct((SEG, 8 * HD), BF16),
         ],
         in_specs=[pl.BlockSpec(memory_space=pltpu.SMEM)] + [vmem] * 3,
-        out_specs=[vmem] * 2,
+        out_specs=[pl.BlockSpec(memory_space=pltpu.HBM), vmem],
+        scratch_shapes=[pltpu.VMEM((SEG, 4 * WIDE), BF16), pltpu.SemaphoreType.DMA((4,))],
         compiler_params=params(),
         cost_estimate=cost(7),
         name="backward_groups",
@@ -426,43 +439,46 @@
     pair_came = swap(pair, y=1)
     grad_query, kv_grad = backward_groups(token, back_q, back_dout, cache)
     pairs = rows([pair, pair_came])
-    token, kv_grad, pairs, *pieces = together((lengths, kv_grad, pairs, *pieces))
-    grads = [kv_grad] + [swap(kv_grad, x=r) for r in (1, 3, 2)]
+    token, kv_grad, pairs, *came = together((lengths, kv_grad, pairs, *(pieces[r] for r in (2, 1, 3))))
+    pieces = [pieces[0], came[1], came[0], came[2]]
+    far_kv, left_kv, right_kv = [swap(kv_grad, x=r) for r in (2, 3, 1)]
+    grads = [kv_grad, right_kv, left_kv, far_kv]
     pairs_came = swap(pairs, y=3)
     held_a = stored_groups(token, front_q, cache, 0)
-    token = together((lengths, held_a[1]))[0]
-    held_b = stored_groups(token, front_q, cache, 2)
-
-    half = rows([pairs, pairs_came])
-    half, *grads, acc, stat = together((half, *grads, *held_b))
-    held = (*held_a, acc, stat)
-    other_half = swap(half, c=1)
+    far_kv, left_kv, right_kv, acc, stat = together((far_kv, left_kv, right_kv, *held_a))
+    grads = [kv_grad, right_kv, left_kv, far_kv]
     away, home = weight_grad_halves(pieces, grads)
     other_away = swap(away, c=1)
-    away, other_half, *pieces = together((away, other_half, *pieces))
+    half = rows([pairs, pairs_came])
+    token, half, away = together((lengths, half, away))
+    other_half = swap(half, c=1)
+    held = (acc, stat, *stored_groups(token, front_q, cache, 2))
+    other_away, held_last = together((other_away, held[3]))
+    held = (*held[:3], held_last)
+    sum0, sum12, sum3 = chip_sum(home, other_away)
+    sum_came = swap(sum12, y=1)
+    other_half, sum12 = together((other_half, sum12))
     own0, own1, own2, own3, weight = own_kv_parts(pieces, (half, other_half))
     own_came = [swap(own2, x=2), swap(own1, x=1), swap(own3, x=3)]
-    other_away, weight = together((other_away, weight))
-    sum0, sum12, sum3 = chip_sum(home, other_away)
-    sum_came = swap(sum12, y=1)
-    weight = together((weight, sum12))[0]
     leave = input_grad_pieces(grads, weight)
     here = lax.ppermute(leave, "pipe", [(p + 1, p) for p in range(3)])
     own_came = together((*own_came, leave))[:3]
     own2, own1, own3 = own_came
     fwd_out = own_groups(lengths, front_q, (own0, own1, own2, own3), held)
-    next_act = lax.ppermute(fwd_out, "pipe", [(p, p + 1) for p in range(3)])
     sum_came = together((sum_came, fwd_out))[0]
     sum_leave = (sum3 + sum_came[2 * BLK :].astype(F32)).astype(BF16)
+    fwd_out = together((fwd_out, sum_leave))[0]
+    next_act = lax.ppermute(fwd_out, "pipe", [(p, p + 1) for p in range(3)])
     sum_last = swap(sum_leave, y=3)
     here = together((here, sum_leave))[0]
-    in_came = swap(here[2 * SEG :], x=3)
+    blocks = [here[at * SEG : (at + 1) * SEG] for at in (0, 1, 3, 2)]
+    came = [swap(blocks[r], x=r) for r in (2, 1, 3)]
     total = sum0 + sum_came[: 2 * BLK].astype(F32) + sum_last.astype(F32)
     far_total = total[BLK:].astype(BF16)
     far_came = swap(far_total, z=1)
-    in_came = together((in_came, far_total))[0]
-    in_last = swap(rows([here[SEG : 2 * SEG], in_came[SEG:]]), x=1)
-    prev_grad, next_act = join_pieces(here, in_came, in_last, next_act)
+    came = together((*came, far_total))[:3]
+    prev_grad, next_act = join_pieces(blocks[0], came[1], came[0], came[2], next_act)
+    far_came = together((far_came, prev_grad))[0]
     weight_grad = total[:BLK] + far_came.astype(F32)
     return (next_act[None, None], grad_query[None, None], prev_grad[None, None], weight_grad[None])
 

time: 79.8 us -> 76.7 us (0.961)
  waiting for transfers between devices: 20.3 us -> 15.7 us
  starting transfers between devices: 34.9 us -> 38.1 us
  Pallas kernels: 22.3 us -> 20.6 us
    ppermute x19 -> x20, waiting for transfers between devices: 20.3 us -> 12.5 us  [swap(): lax.ppermute(value, 'dp', [(d, partner(d, **steps)) for d in range(64)])]
    ppermute x19 -> x20, starting transfers between devices: 29.1 us -> 32.3 us  [swap(): lax.ppermute(value, 'dp', [(d, partner(d, **steps)) for d in range(64)])]
    ppermute x1, waiting for transfers between devices: 0.01 us -> 3.19 us  [shards(): next_act = lax.ppermute(fwd_out, 'pipe', [(p, p + 1) for p in range(3)])]
    pallas_call x1, Pallas kernels: 7.85 us -> 6.17 us  [backward_groups(): pl.pallas_call(backward_kernel, out_shape=[jax.ShapeDtypeStruct(q.shape,...]
  transfers between devices with their start and end apart: 21 -> 22, of which waited for: 10 -> 13; matrix products, arithmetic and copies ran while one was open for 1% -> 0% of each run, Pallas kernels for 26% -> 27%
where the time goes in v4:
time: 76.7 us; the launch traced here: 76.4 us
  starting transfers between devices  38.1 us (50%)
  Pallas kernels  20.6 us (27%)
  waiting for transfers between devices  15.7 us (20%)
  other arithmetic  0.94 us (1%)
  between operations  0.89 us (1%)
    ppermute x20, starting transfers between devices, swap(): lax.ppermute(value, 'dp', [(d, partner(d, **steps)) for d in range(64)])  32.3 us
    ppermute x20, waiting for transfers between devices, swap(): lax.ppermute(value, 'dp', [(d, partner(d, **steps)) for d in range(64)])  12.5 us
    pallas_call x1, Pallas kernels, backward_groups(): pl.pallas_call(backward_kernel, out_shape=[jax.ShapeDtypeStruct(q.shape,...  6.17 us
    pallas_call x2, Pallas kernels, stored_groups(): pl.pallas_call(functools.partial(stored_kernel, first), out_shape=[jax.Sh...  5.23 us
    ppermute x1, waiting for transfers between devices, shards(): next_act = lax.ppermute(fwd_out, 'pipe', [(p, p + 1) for p in range(3)])  3.19 us
    ppermute x1, starting transfers between devices, shards(): here = lax.ppermute(leave, 'pipe', [(p + 1, p) for p in range(3)])  2.92 us
    pallas_call x1, Pallas kernels, own_groups(): pl.pallas_call(own_kernel, out_shape=jax.ShapeDtypeStruct(q.shape, BF16),...  2.91 us
    ppermute x1, starting transfers between devices, shards(): next_act = lax.ppermute(fwd_out, 'pipe', [(p, p + 1) for p in range(3)])  2.91 us
  transfers between devices with their start and end apart: 22, of which 13 were waited for; matrix products, arithmetic and copies ran while one was open for 0% of the time, Pallas kernels for 27%

profile of v4, /device:TPU:64, one launch (start us, length us, event | category | flops | bytes accessed | tf_op | source)
XLA Modules:
  0.0 76.4 jit_solution(7173337315693838185)
XLA Ops:
  0.7 5.5 %collective-permute-start = (bf16[56,1024]{1,0:T(8,128)(2,1)}, bf16[56,1024]{1,0:T(8,128)(2,1)S(1)}, u32[]{:S(2)}, u32[]{:S(2)}) collective-permute-start(bf16[56,1024]{1,0:T(8,128)(2,1)} %bitcast.25), channel_id=1, source_target_pairs={{0,128},{4,132},{8,136},{12,140},{16,144},{20,148},{24,152},{28,15... | collective-permute-start | bytes 344072 | tf_op jit(solution)/shard_map/ppermute | solution.py:46
  6.2 2.5 %split_inputs.1 = (bf16[128,896]{1,0:T(8,128)(2,1)}, bf16[128,896]{1,0:T(8,128)(2,1)}, bf16[128,896]{1,0:T(8,128)(2,1)}, bf16[128,896]{1,0:T(8,128)(2,1)}) custom-call(bf16[64,3584]{1,0:T(8,128)(2,1)} %bitcast.27, bf16[64,3584]{1,0:T(8,128)(2,1)} %bitcast.28), custom_call_target="tpu_custom_call" | custom-call | flops 750000000 | bytes 1500000 | tf_op jit(solution)/shard_map/split_inputs/pallas_call | solution.py:73
  8.7 3.1 %collective-permute-start.2 = (bf16[128,896]{1,0:T(8,128)(2,1)}, bf16[128,896]{1,0:T(8,128)(2,1)S(1)}, u32[]{:S(2)}, u32[]{:S(2)}) collective-permute-start(bf16[128,896]{1,0:T(8,128)(2,1)} %get-tuple-element.59), channel_id=1, source_target_pairs={{0,64},{4,68},{8,72},{12,76},{16,80},{20,84},{24,88},{28,92},{32,9... | collective-permute-start | bytes 688136 | tf_op jit(solution)/shard_map/ppermute | solution.py:46
  11.8 0.6 collective-permute-start.3
  12.4 0.6 collective-permute-start.4
  13.0 1.7 %collective-permute-start.1 = (bf16[112,1024]{1,0:T(8,128)(2,1)S(1)}, bf16[112,1024]{1,0:T(8,128)(2,1)S(1)}, u32[]{:S(2)}, u32[]{:S(2)}) collective-permute-start(bf16[112,1024]{1,0:T(8,128)(2,1)S(1)} %pad_maximum_fusion.2), channel_id=1, source_target_pairs={{0,8},{4,12},{8,0},{12,4},{16,24},{20,28},{24,16},{28,20},{32,40},... | collective-permute-start | bytes 688136 | tf_op jit(solution)/shard_map/ppermute | solution.py:46
  14.7 6.2 %backward_groups.1 = (bf16[64,3584]{1,0:T(8,128)(2,1)}, bf16[64,1024]{1,0:T(8,128)(2,1)S(1)}) custom-call(s32[4]{0:T(128)S(1)} %bitcast.21, bf16[64,3584]{1,0:T(8,128)(2,1)S(1)} %bitcast.16, bf16[64,3584]{1,0:T(8,128)(2,1)S(1)} %bitcast.17, bf16[1024,1024]{1,0:T(8,128)(2,1)S(1)} %bitcast.13), custom_call_target="tpu_custom_call" | custom-call | flops 3500000000 | bytes 7000000 | tf_op jit(solution)/shard_map/backward_groups/pallas_call | solution.py:202
  20.9 1.7 %collective-permute-done.3.r1 = bf16[128,896]{1,0:T(8,128)(2,1)S(1)} collective-permute-done((bf16[128,896]{1,0:T(8,128)(2,1)}, bf16[128,896]{1,0:T(8,128)(2,1)S(1)}, u32[]{:S(2)}, u32[]{:S(2)}) %collective-permute-start.3) | collective-permute-done | bytes 229408 | tf_op jit(solution)/shard_map/ppermute | solution.py:46
  22.6 3.0 %collective-permute-start.8 = (bf16[224,1024]{1,0:T(8,128)(2,1)S(1)}, bf16[224,1024]{1,0:T(8,128)(2,1)S(1)}, u32[]{:S(2)}, u32[]{:S(2)}) collective-permute-start(bf16[224,1024]{1,0:T(8,128)(2,1)S(1)} %pad_maximum_fusion.1), channel_id=1, source_target_pairs={{0,24},{4,28},{8,16},{12,20},{16,8},{20,12},{24,0},{28,4},{32,56},... | collective-permute-start | bytes 1376264 | tf_op jit(solution)/shard_map/ppermute | solution.py:46
  25.6 2.9 %collective-permute-start.5 = (bf16[64,1024]{1,0:T(8,128)(2,1)S(1)}, bf16[64,1024]{1,0:T(8,128)(2,1)S(1)}, u32[]{:S(2)}, u32[]{:S(2)}) collective-permute-start(bf16[64,1024]{1,0:T(8,128)(2,1)S(1)} %get-tuple-element.62.g0), channel_id=1, source_target_pairs={{0,64},{4,68},{8,72},{12,76},{16,80},{20,84},{24,88},{28,92},{32,9... | collective-permute-start | bytes 393224 | tf_op jit(solution)/shard_map/ppermute | solution.py:46
  28.5 1.2 %collective-permute-start.6 = (bf16[64,1024]{1,0:T(8,128)(2,1)S(1)}, bf16[64,1024]{1,0:T(8,128)(2,1)S(1)}, u32[]{:S(2)}, u32[]{:S(2)}) collective-permute-start(bf16[64,1024]{1,0:T(8,128)(2,1)S(1)} %get-tuple-element.62.g0), channel_id=1, source_target_pairs={{0,96},{4,100},{8,104},{12,108},{16,112},{20,116},{24,120},{28,124... | collective-permute-start | bytes 393224 | tf_op jit(solution)/shard_map/ppermute | solution.py:46
  29.7 2.6 %stored_groups.2 = (f32[64,1792]{1,0:T(8,128)S(1)}, f32[64,256]{1,0:T(8,128)S(1)}) custom-call(s32[4]{0:T(128)S(1)} %bitcast.22, bf16[64,3584]{1,0:T(8,128)(2,1)S(1)} %bitcast.18, bf16[1024,1024]{1,0:T(8,128)(2,1)S(1)} %bitcast.14), custom_call_target="tpu_custom_call" | custom-call | flops 1200000000 | bytes 2400000 | tf_op jit(solution)/shard_map/stored_groups/pallas_call | solution.py:250
  32.4 0.1 collective-permute-done.5.g2
  32.4 2.5 %collective-permute-done.6.g3 = bf16[64,1024]{1,0:T(8,128)(2,1)S(1)} collective-permute-done((bf16[64,1024]{1,0:T(8,128)(2,1)S(1)}, bf16[64,1024]{1,0:T(8,128)(2,1)S(1)}, u32[]{:S(2)}, u32[]{:S(2)}) %collective-permute-start.6) | collective-permute-done | bytes 131104 | tf_op jit(solution)/shard_map/ppermute | solution.py:46
  34.9 0.1 collective-permute-done.7.g1
  35.0 0.9 %weight_grad_halves.1 = (bf16[448,1024]{1,0:T(8,128)(2,1)S(1)}, f32[448,1024]{1,0:T(8,128)S(1)}) custom-call(bf16[128,896]{1,0:T(8,128)(2,1)S(1)} %copy-done.5, bf16[128,896]{1,0:T(8,128)(2,1)S(1)} %collective-permute-done.3.r1, bf16[128,896]{1,0:T(8,128)(2,1)S(1)} %collective-permute-done.2.r2, bf16[128,896]{1,0:T(8,128)(2,1)S(1)} %collective-permute-done.4.r3, ...), custom_call_target="tpu_custom_call" | custom-call | flops 750000000 | bytes 1500000 | tf_op jit(solution)/shard_map/weight_grad_halves/pallas_call | solution.py:366
  35.9 0.1 collective-permute-start.10
  36.0 0.1 pad_maximum_fusion.a_ref
  36.1 0.6 collective-permute-start.9
  36.7 2.6 %stored_groups.3 = (f32[64,1792]{1,0:T(8,128)S(1)}, f32[64,256]{1,0:T(8,128)S(1)}) custom-call(s32[4]{0:T(128)S(1)} %bitcast.23, bf16[64,3584]{1,0:T(8,128)(2,1)S(1)} %bitcast.19, bf16[1024,1024]{1,0:T(8,128)(2,1)S(1)} %bitcast.15), custom_call_target="tpu_custom_call" | custom-call | flops 1200000000 | bytes 2400000 | tf_op jit(solution)/shard_map/stored_groups/pallas_call | solution.py:250
  39.3 0.1 chip_sum.1
  39.5 0.2 collective-permute-start.12
  39.7 0.1 collective-permute-done.9.b_ref
  39.8 0.9 %own_kv_parts.1 = (f32[64,1024]{1,0:T(8,128)S(1)}, bf16[64,1024]{1,0:T(8,128)(2,1)S(1)}, bf16[64,1024]{1,0:T(8,128)(2,1)S(1)}, bf16[64,1024]{1,0:T(8,128)(2,1)S(1)}, bf16[896,1024]{1,0:T(8,128)(2,1)S(1)}) custom-call(bf16[128,896]{1,0:T(8,128)(2,1)S(1)} %copy-done.5, bf16[128,896]{1,0:T(8,128)(2,1)S(1)} %collective-permute-done.3.r1, ...), custom_call_target="tpu_custom_call" | custom-call | flops 750000000 | bytes 1500000 | tf_op jit(solution)/shard_map/own_kv_parts/pallas_call | solution.py:323
  40.7 2.9 %collective-permute-start.13 = (bf16[64,1024]{1,0:T(8,128)(2,1)S(1)}, bf16[64,1024]{1,0:T(8,128)(2,1)S(1)}, u32[]{:S(2)}, u32[]{:S(2)}) collective-permute-start(bf16[64,1024]{1,0:T(8,128)(2,1)S(1)} %get-tuple-element.85), channel_id=1, source_target_pairs={{0,64},{4,68},{8,72},{12,76},{16,80},{20,84},{24,88},{28,92},{32,9... | collective-permute-start | bytes 393224 | tf_op jit(solution)/shard_map/ppermute | solution.py:46
  43.5 0.7 collective-permute-start.14
  44.3 0.6 collective-permute-start.15
  44.9 0.7 input_grad_pieces.1
  45.6 2.9 %collective-permute-start.11 = (bf16[256,896]{1,0:T(8,128)(2,1)S(1)}, bf16[256,896]{1,0:T(8,128)(2,1)S(1)}, u32[]{:S(2)}, u32[]{:S(2)}) collective-permute-start(bf16[256,896]{1,0:T(8,128)(2,1)S(1)} %input_grad_pieces.1), channel_id=1, source_target_pairs={{1,0},{2,1},{3,2},{5,4},{6,5},{7,6},{9,8},{10,9},{11,10},{13,12},{... | collective-permute-start | bytes 1376264 | tf_op jit(solution)/shard_map/ppermute | solution.py:464
  48.6 0.0 collective-permute-done.13.k2
  48.6 2.0 %collective-permute-done.14.k1 = bf16[64,1024]{1,0:T(8,128)(2,1)S(1)} collective-permute-done((bf16[64,1024]{1,0:T(8,128)(2,1)S(1)}, bf16[64,1024]{1,0:T(8,128)(2,1)S(1)}, u32[]{:S(2)}, u32[]{:S(2)}) %collective-permute-start.14) | collective-permute-done | bytes 131104 | tf_op jit(solution)/shard_map/ppermute | solution.py:46
  50.6 0.3 collective-permute-done.15.k3
  50.9 2.9 %own_groups.1 = bf16[64,3584]{1,0:T(8,128)(2,1)S(1)} custom-call(s32[4]{0:T(128)S(1)} %bitcast.24, bf16[64,3584]{1,0:T(8,128)(2,1)S(1)} %bitcast.20, f32[64,1024]{1,0:T(8,128)S(1)} %get-tuple-element.84.k0, bf16[64,1024]{1,0:T(8,128)(2,1)S(1)} %collective-permute-done.14.k1, bf16[64,1024]{1,0:T(8,128)(2,1)S(1)} %collective-permute-done.13.k2, ...), custom_call_target="tpu_custom_call" | custom-call | flops 1000000000 | bytes 2000000 | tf_op jit(solution)/shard_map/own_groups/pallas_call | solution.py:294
  53.9 2.6 %collective-permute-start.19 = (bf16[112,1024]{1,0:T(8,128)(2,1)S(1)}, bf16[112,1024]{1,0:T(8,128)(2,1)S(1)}, u32[]{:S(2)}, u32[]{:S(2)}) collective-permute-start(bf16[112,1024]{1,0:T(8,128)(2,1)S(1)} %add_convert_fusion), channel_id=1, source_target_pairs={{0,24},{4,28},{8,16},{12,20},{16,8},{20,12},{24,0},{28,4},{32,56},... | collective-permute-start | bytes 688136 | tf_op jit(solution)/shard_map/ppermute | solution.py:46
  56.6 2.9 %collective-permute-start.20 = (bf16[64,3584]{1,0:T(8,128)(2,1)S(1)}, bf16[64,3584]{1,0:T(8,128)(2,1)S(1)}, u32[]{:S(2)}, u32[]{:S(2)}) collective-permute-start(bf16[64,3584]{1,0:T(8,128)(2,1)S(1)} %own_groups.1), channel_id=1, source_target_pairs={{0,1},{1,2},{2,3},{4,5},{5,6},{6,7},{8,9},{9,10},{10,11},{12,13},{... | collective-permute-start | bytes 1376264 | tf_op jit(solution)/shard_map/ppermute | solution.py:471
  59.5 0.1 collective-permute-done.11
  59.6 3.0 %collective-permute-start.16 = (bf16[64,896]{1,0:T(8,128)(2,1)S(1)}, bf16[64,896]{1,0:T(8,128)(2,1)S(1)}, u32[]{:S(2)}, u32[]{:S(2)}) collective-permute-start(bf16[64,896]{1,0:T(8,128)(2,1)S(1)} %get-tuple-element.108), channel_id=1, source_target_pairs={{0,64},{4,68},{8,72},{12,76},{16,80},{20,84},{24,88},{28,92},{32,9... | collective-permute-start | bytes 344072 | tf_op jit(solution)/shard_map/ppermute | solution.py:46
  62.5 0.6 collective-permute-start.17
  63.1 0.6 collective-permute-start.18
  63.8 0.1 convert_add_fusion
  63.9 1.8 %collective-permute-start.21 = (bf16[56,1024]{1,0:T(8,128)(2,1)S(1)}, bf16[56,1024]{1,0:T(8,128)(2,1)S(1)}, u32[]{:S(2)}, u32[]{:S(2)}) collective-permute-start(bf16[56,1024]{1,0:T(8,128)(2,1)S(1)} %slice.41), channel_id=1, source_target_pairs={{0,128},{4,132},{8,136},{12,140},{16,144},{20,148},{24,152},{28,15... | collective-permute-start | bytes 344072 | tf_op jit(solution)/shard_map/ppermute | solution.py:46
  65.7 1.3 %collective-permute-done.16.g2 = bf16[64,896]{1,0:T(8,128)(2,1)S(1)} collective-permute-done((bf16[64,896]{1,0:T(8,128)(2,1)S(1)}, bf16[64,896]{1,0:T(8,128)(2,1)S(1)}, u32[]{:S(2)}, u32[]{:S(2)}) %collective-permute-start.16) | collective-permute-done | bytes 114720 | tf_op jit(solution)/shard_map/ppermute | solution.py:46
  67.0 1.1 %collective-permute-done.17.g1 = bf16[64,896]{1,0:T(8,128)(2,1)S(1)} collective-permute-done((bf16[64,896]{1,0:T(8,128)(2,1)S(1)}, bf16[64,896]{1,0:T(8,128)(2,1)S(1)}, u32[]{:S(2)}, u32[]{:S(2)}) %collective-permute-start.17) | collective-permute-done | bytes 114720 | tf_op jit(solution)/shard_map/ppermute | solution.py:46
  68.1 1.0 %collective-permute-done.18.g3 = bf16[64,896]{1,0:T(8,128)(2,1)S(1)} collective-permute-done((bf16[64,896]{1,0:T(8,128)(2,1)S(1)}, bf16[64,896]{1,0:T(8,128)(2,1)S(1)}, u32[]{:S(2)}, u32[]{:S(2)}) %collective-permute-start.18) | collective-permute-done | bytes 114720 | tf_op jit(solution)/shard_map/ppermute | solution.py:46
  69.1 3.2 %collective-permute-done.20.act_ref = bf16[64,3584]{1,0:T(8,128)(2,1)S(1)} collective-permute-done((bf16[64,3584]{1,0:T(8,128)(2,1)S(1)}, bf16[64,3584]{1,0:T(8,128)(2,1)S(1)}, u32[]{:S(2)}, u32[]{:S(2)}) %collective-permute-start.20) | collective-permute-done | bytes 458784 | tf_op jit(solution)/shard_map/ppermute | solution.py:471
  72.3 1.1 %join_pieces.1 = (bf16[64,3584]{1,0:T(8,128)(2,1)}, bf16[64,3584]{1,0:T(8,128)(2,1)}) custom-call(bf16[64,896]{1,0:T(8,128)(2,1)S(1)} %get-tuple-element.109.g0, bf16[64,896]{1,0:T(8,128)(2,1)S(1)} %collective-permute-done.17.g1, bf16[64,896]{1,0:T(8,128)(2,1)S(1)} %collective-permute-done.16.g2, bf16[64,896]{1,0:T(8,128)(2,1)S(1)} %collective-permute-done.18.g3, ...), custom_call_target="tpu_custom_call" | custom-call | flops 500000000 | bytes 1000000 | tf_op jit(solution)/shard_map/join_pieces/pallas_call | solution.py:101
  73.5 2.2 %collective-permute-done.21 = bf16[56,1024]{1,0:T(8,128)(2,1)S(1)} collective-permute-done((bf16[56,1024]{1,0:T(8,128)(2,1)S(1)}, bf16[56,1024]{1,0:T(8,128)(2,1)S(1)}, u32[]{:S(2)}, u32[]{:S(2)}) %collective-permute-start.21) | collective-permute-done | bytes 114720 | tf_op jit(solution)/shard_map/ppermute | solution.py:46
  75.7 0.7 fusion
  (28 shorter events, 0.2 us)
Async XLA Ops:
  0.6 12.3 %copy-start.6 = (bf16[1,56,1024]{2,1,0:T(8,128)(2,1)S(1)}, bf16[1,56,1024]{2,1,0:T(8,128)(2,1)}, u32[]{:S(2)}) copy-start(bf16[1,56,1024]{2,1,0:T(8,128)(2,1)} %param.14) | copy-start | bytes 344068
  0.6 14.0 %copy-start.4 = (s32[1,1,4]{2,1,0:T(1,128)S(1)}, s32[1,1,4]{2,1,0:T(1,128)}, u32[]{:S(2)}) copy-start(s32[1,1,4]{2,1,0:T(1,128)} %param.15) | copy-start | bytes 52
  0.7 14.0 %copy-start = (bf16[1,1,1024,1024]{3,2,1,0:T(8,128)(2,1)S(1)}, bf16[1,1,1024,1024]{3,2,1,0:T(8,128)(2,1)}, u32[]{:S(2)}) copy-start(bf16[1,1,1024,1024]{3,2,1,0:T(8,128)(2,1)} %param.13) | copy-start | bytes 6291460
  0.7 14.0 %copy-start.1 = (bf16[1,1,64,3584]{3,2,1,0:T(8,128)(2,1)S(1)}, bf16[1,1,64,3584]{3,2,1,0:T(8,128)(2,1)}, u32[]{:S(2)}) copy-start(bf16[1,1,64,3584]{3,2,1,0:T(8,128)(2,1)} %param.11) | copy-start | bytes 1376260
  0.7 14.0 %copy-start.2 = (bf16[1,1,64,3584]{3,2,1,0:T(8,128)(2,1)S(1)}, bf16[1,1,64,3584]{3,2,1,0:T(8,128)(2,1)}, u32[]{:S(2)}) copy-start(bf16[1,1,64,3584]{3,2,1,0:T(8,128)(2,1)} %param.12) | copy-start | bytes 1376260
  0.7 12.3 %collective-permute-start = (bf16[56,1024]{1,0:T(8,128)(2,1)}, bf16[56,1024]{1,0:T(8,128)(2,1)S(1)}, u32[]{:S(2)}, u32[]{:S(2)}) collective-permute-start(bf16[56,1024]{1,0:T(8,128)(2,1)} %bitcast.25), channel_id=1, source_target_pairs={{0,128},{4,132},{8,136},{12,140},{16,144},{20,148},{24,152},{28,15... | collective-permute-start | bytes 344072 | tf_op jit(solution)/shard_map/ppermute | solution.py:46
  8.7 12.2 %collective-permute-start.2 = (bf16[128,896]{1,0:T(8,128)(2,1)}, bf16[128,896]{1,0:T(8,128)(2,1)S(1)}, u32[]{:S(2)}, u32[]{:S(2)}) collective-permute-start(bf16[128,896]{1,0:T(8,128)(2,1)} %get-tuple-element.59), channel_id=1, source_target_pairs={{0,64},{4,68},{8,72},{12,76},{16,80},{20,84},{24,88},{28,92},{32,9... | collective-permute-start | bytes 688136 | tf_op jit(solution)/shard_map/ppermute | solution.py:46
  11.8 10.8 %collective-permute-start.3 = (bf16[128,896]{1,0:T(8,128)(2,1)}, bf16[128,896]{1,0:T(8,128)(2,1)S(1)}, u32[]{:S(2)}, u32[]{:S(2)}) collective-permute-start(bf16[128,896]{1,0:T(8,128)(2,1)} %get-tuple-element.60), channel_id=1, source_target_pairs={{0,32},{4,36},{8,40},{12,44},{16,48},{20,52},{24,56},{28,60},{32,0... | collective-permute-start | bytes 688136 | tf_op jit(solution)/shard_map/ppermute | solution.py:46
  12.4 10.2 %collective-permute-start.4 = (bf16[128,896]{1,0:T(8,128)(2,1)}, bf16[128,896]{1,0:T(8,128)(2,1)S(1)}, u32[]{:S(2)}, u32[]{:S(2)}) collective-permute-start(bf16[128,896]{1,0:T(8,128)(2,1)} %get-tuple-element.61), channel_id=1, source_target_pairs={{0,96},{4,100},{8,104},{12,108},{16,112},{20,116},{24,120},{28,124... | collective-permute-start | bytes 688136 | tf_op jit(solution)/shard_map/ppermute | solution.py:46
  13.0 7.9 %collective-permute-start.1 = (bf16[112,1024]{1,0:T(8,128)(2,1)S(1)}, bf16[112,1024]{1,0:T(8,128)(2,1)S(1)}, u32[]{:S(2)}, u32[]{:S(2)}) collective-permute-start(bf16[112,1024]{1,0:T(8,128)(2,1)S(1)} %pad_maximum_fusion.2), channel_id=1, source_target_pairs={{0,8},{4,12},{8,0},{12,4},{16,24},{20,28},{24,16},{28,20},{32,40},... | collective-permute-start | bytes 688136 | tf_op jit(solution)/shard_map/ppermute | solution.py:46
  14.7 15.1 %copy-start.3 = (bf16[1,1,64,3584]{3,2,1,0:T(8,128)(2,1)S(1)}, bf16[1,1,64,3584]{3,2,1,0:T(8,128)(2,1)}, u32[]{:S(2)}) copy-start(bf16[1,1,64,3584]{3,2,1,0:T(8,128)(2,1)} %param.9) | copy-start | bytes 1376260
  22.6 13.4 %collective-permute-start.8 = (bf16[224,1024]{1,0:T(8,128)(2,1)S(1)}, bf16[224,1024]{1,0:T(8,128)(2,1)S(1)}, u32[]{:S(2)}, u32[]{:S(2)}) collective-permute-start(bf16[224,1024]{1,0:T(8,128)(2,1)S(1)} %pad_maximum_fusion.1), channel_id=1, source_target_pairs={{0,24},{4,28},{8,16},{12,20},{16,8},{20,12},{24,0},{28,4},{32,56},... | collective-permute-start | bytes 1376264 | tf_op jit(solution)/shard_map/ppermute | solution.py:46
  25.6 6.8 %collective-permute-start.5 = (bf16[64,1024]{1,0:T(8,128)(2,1)S(1)}, bf16[64,1024]{1,0:T(8,128)(2,1)S(1)}, u32[]{:S(2)}, u32[]{:S(2)}) collective-permute-start(bf16[64,1024]{1,0:T(8,128)(2,1)S(1)} %get-tuple-element.62.g0), channel_id=1, source_target_pairs={{0,64},{4,68},{8,72},{12,76},{16,80},{20,84},{24,88},{28,92},{32,9... | collective-permute-start | bytes 393224 | tf_op jit(solution)/shard_map/ppermute | solution.py:46
  28.5 6.4 %collective-permute-start.6 = (bf16[64,1024]{1,0:T(8,128)(2,1)S(1)}, bf16[64,1024]{1,0:T(8,128)(2,1)S(1)}, u32[]{:S(2)}, u32[]{:S(2)}) collective-permute-start(bf16[64,1024]{1,0:T(8,128)(2,1)S(1)} %get-tuple-element.62.g0), channel_id=1, source_target_pairs={{0,96},{4,100},{8,104},{12,108},{16,112},{20,116},{24,120},{28,124... | collective-permute-start | bytes 393224 | tf_op jit(solution)/shard_map/ppermute | solution.py:46
  29.7 5.3 %collective-permute-start.7 = (bf16[64,1024]{1,0:T(8,128)(2,1)S(1)}, bf16[64,1024]{1,0:T(8,128)(2,1)S(1)}, u32[]{:S(2)}, u32[]{:S(2)}) collective-permute-start(bf16[64,1024]{1,0:T(8,128)(2,1)S(1)} %get-tuple-element.62.g0), channel_id=1, source_target_pairs={{0,32},{4,36},{8,40},{12,44},{16,48},{20,52},{24,56},{28,60},{32,0... | collective-permute-start | bytes 393224 | tf_op jit(solution)/shard_map/ppermute | solution.py:46
  29.7 5.3 %copy-start.5 = (bf16[128,896]{1,0:T(8,128)(2,1)S(1)}, bf16[128,896]{1,0:T(8,128)(2,1)}, u32[]{:S(2)}) copy-start(bf16[128,896]{1,0:T(8,128)(2,1)} %get-tuple-element.69.r0) | copy-start | bytes 688132
  35.9 3.4 %collective-permute-start.10 = (bf16[448,1024]{1,0:T(8,128)(2,1)S(1)}, bf16[448,1024]{1,0:T(8,128)(2,1)S(1)}, u32[]{:S(2)}, u32[]{:S(2)}) collective-permute-start(bf16[448,1024]{1,0:T(8,128)(2,1)S(1)} %get-tuple-element.74), channel_id=1, source_target_pairs={{0,4},{4,0},{8,12},{12,8},{16,20},{20,16},{24,28},{28,24},{32,36},... | collective-permute-start | bytes 2752520 | tf_op jit(solution)/shard_map/ppermute | solution.py:46
  36.1 3.7 %collective-permute-start.9 = (bf16[448,1024]{1,0:T(8,128)(2,1)S(1)}, bf16[448,1024]{1,0:T(8,128)(2,1)S(1)}, u32[]{:S(2)}, u32[]{:S(2)}) collective-permute-start(bf16[448,1024]{1,0:T(8,128)(2,1)S(1)} %pad_maximum_fusion.a_ref), channel_id=1, source_target_pairs={{0,4},{4,0},{8,12},{12,8},{16,20},{20,16},{24,28},{28,24},{32,36},... | collective-permute-start | bytes 2752520 | tf_op jit(solution)/shard_map/ppermute | solution.py:46
  39.5 14.4 %collective-permute-start.12 = (bf16[224,1024]{1,0:T(8,128)(2,1)S(1)}, bf16[224,1024]{1,0:T(8,128)(2,1)S(1)}, u32[]{:S(2)}, u32[]{:S(2)}) collective-permute-start(bf16[224,1024]{1,0:T(8,128)(2,1)S(1)} %get-tuple-element.80), channel_id=1, source_target_pairs={{0,8},{4,12},{8,0},{12,4},{16,24},{20,28},{24,16},{28,20},{32,40},... | collective-permute-start | bytes 1376264 | tf_op jit(solution)/shard_map/ppermute | solution.py:46
  40.7 7.9 %collective-permute-start.13 = (bf16[64,1024]{1,0:T(8,128)(2,1)S(1)}, bf16[64,1024]{1,0:T(8,128)(2,1)S(1)}, u32[]{:S(2)}, u32[]{:S(2)}) collective-permute-start(bf16[64,1024]{1,0:T(8,128)(2,1)S(1)} %get-tuple-element.85), channel_id=1, source_target_pairs={{0,64},{4,68},{8,72},{12,76},{16,80},{20,84},{24,88},{28,92},{32,9... | collective-permute-start | bytes 393224 | tf_op jit(solution)/shard_map/ppermute | solution.py:46
  43.5 7.1 %collective-permute-start.14 = (bf16[64,1024]{1,0:T(8,128)(2,1)S(1)}, bf16[64,1024]{1,0:T(8,128)(2,1)S(1)}, u32[]{:S(2)}, u32[]{:S(2)}) collective-permute-start(bf16[64,1024]{1,0:T(8,128)(2,1)S(1)} %get-tuple-element.86), channel_id=1, source_target_pairs={{0,32},{4,36},{8,40},{12,44},{16,48},{20,52},{24,56},{28,60},{32,0... | collective-permute-start | bytes 393224 | tf_op jit(solution)/shard_map/ppermute | solution.py:46
  44.3 6.7 %collective-permute-start.15 = (bf16[64,1024]{1,0:T(8,128)(2,1)S(1)}, bf16[64,1024]{1,0:T(8,128)(2,1)S(1)}, u32[]{:S(2)}, u32[]{:S(2)}) collective-permute-start(bf16[64,1024]{1,0:T(8,128)(2,1)S(1)} %get-tuple-element.87), channel_id=1, source_target_pairs={{0,96},{4,100},{8,104},{12,108},{16,112},{20,116},{24,120},{28,124... | collective-permute-start | bytes 393224 | tf_op jit(solution)/shard_map/ppermute | solution.py:46
  45.6 13.9 %collective-permute-start.11 = (bf16[256,896]{1,0:T(8,128)(2,1)S(1)}, bf16[256,896]{1,0:T(8,128)(2,1)S(1)}, u32[]{:S(2)}, u32[]{:S(2)}) collective-permute-start(bf16[256,896]{1,0:T(8,128)(2,1)S(1)} %input_grad_pieces.1), channel_id=1, source_target_pairs={{1,0},{2,1},{3,2},{5,4},{6,5},{7,6},{9,8},{10,9},{11,10},{13,12},{... | collective-permute-start | bytes 1376264 | tf_op jit(solution)/shard_map/ppermute | solution.py:464
  53.9 9.9 %collective-permute-start.19 = (bf16[112,1024]{1,0:T(8,128)(2,1)S(1)}, bf16[112,1024]{1,0:T(8,128)(2,1)S(1)}, u32[]{:S(2)}, u32[]{:S(2)}) collective-permute-start(bf16[112,1024]{1,0:T(8,128)(2,1)S(1)} %add_convert_fusion), channel_id=1, source_target_pairs={{0,24},{4,28},{8,16},{12,20},{16,8},{20,12},{24,0},{28,4},{32,56},... | collective-permute-start | bytes 688136 | tf_op jit(solution)/shard_map/ppermute | solution.py:46
  56.6 15.8 %collective-permute-start.20 = (bf16[64,3584]{1,0:T(8,128)(2,1)S(1)}, bf16[64,3584]{1,0:T(8,128)(2,1)S(1)}, u32[]{:S(2)}, u32[]{:S(2)}) collective-permute-start(bf16[64,3584]{1,0:T(8,128)(2,1)S(1)} %own_groups.1), channel_id=1, source_target_pairs={{0,1},{1,2},{2,3},{4,5},{5,6},{6,7},{8,9},{9,10},{10,11},{12,13},{... | collective-permute-start | bytes 1376264 | tf_op jit(solution)/shard_map/ppermute | solution.py:471
  59.6 7.5 %collective-permute-start.16 = (bf16[64,896]{1,0:T(8,128)(2,1)S(1)}, bf16[64,896]{1,0:T(8,128)(2,1)S(1)}, u32[]{:S(2)}, u32[]{:S(2)}) collective-permute-start(bf16[64,896]{1,0:T(8,128)(2,1)S(1)} %get-tuple-element.108), channel_id=1, source_target_pairs={{0,64},{4,68},{8,72},{12,76},{16,80},{20,84},{24,88},{28,92},{32,9... | collective-permute-start | bytes 344072 | tf_op jit(solution)/shard_map/ppermute | solution.py:46
  62.5 5.6 %collective-permute-start.17 = (bf16[64,896]{1,0:T(8,128)(2,1)S(1)}, bf16[64,896]{1,0:T(8,128)(2,1)S(1)}, u32[]{:S(2)}, u32[]{:S(2)}) collective-permute-start(bf16[64,896]{1,0:T(8,128)(2,1)S(1)} %get-tuple-element.107), channel_id=1, source_target_pairs={{0,32},{4,36},{8,40},{12,44},{16,48},{20,52},{24,56},{28,60},{32,0... | collective-permute-start | bytes 344072 | tf_op jit(solution)/shard_map/ppermute | solution.py:46
  63.1 6.0 %collective-permute-start.18 = (bf16[64,896]{1,0:T(8,128)(2,1)S(1)}, bf16[64,896]{1,0:T(8,128)(2,1)S(1)}, u32[]{:S(2)}, u32[]{:S(2)}) collective-permute-start(bf16[64,896]{1,0:T(8,128)(2,1)S(1)} %get-tuple-element.106), channel_id=1, source_target_pairs={{0,96},{4,100},{8,104},{12,108},{16,112},{20,116},{24,120},{28,124... | collective-permute-start | bytes 344072 | tf_op jit(solution)/shard_map/ppermute | solution.py:46
  63.9 11.8 %collective-permute-start.21 = (bf16[56,1024]{1,0:T(8,128)(2,1)S(1)}, bf16[56,1024]{1,0:T(8,128)(2,1)S(1)}, u32[]{:S(2)}, u32[]{:S(2)}) collective-permute-start(bf16[56,1024]{1,0:T(8,128)(2,1)S(1)} %slice.41), channel_id=1, source_target_pairs={{0,128},{4,132},{8,136},{12,140},{16,144},{20,148},{24,152},{28,15... | collective-permute-start | bytes 344072 | tf_op jit(solution)/shard_map/ppermute | solution.py:46

commit v5 on v4

--- a/solution.py
+++ b/solution.py
@@ -450,11 +450,8 @@
     away, home = weight_grad_halves(pieces, grads)
     other_away = swap(away, c=1)
     half = rows([pairs, pairs_came])
-    token, half, away = together((lengths, half, away))
+    half, away = together((half, away))
     other_half = swap(half, c=1)
-    held = (acc, stat, *stored_groups(token, front_q, cache, 2))
-    other_away, held_last = together((other_away, held[3]))
-    held = (*held[:3], held_last)
     sum0, sum12, sum3 = chip_sum(home, other_away)
     sum_came = swap(sum12, y=1)
     other_half, sum12 = together((other_half, sum12))
@@ -462,7 +459,10 @@
     own_came = [swap(own2, x=2), swap(own1, x=1), swap(own3, x=3)]
     leave = input_grad_pieces(grads, weight)
     here = lax.ppermute(leave, "pipe", [(p + 1, p) for p in range(3)])
-    own_came = together((*own_came, leave))[:3]
+    token = together((lengths, leave))[0]
+    held_b = stored_groups(token, front_q, cache, 2)
+    own_came = together((*own_came, held_b[1]))[:3]
+    held = (acc, stat, *held_b)
     own2, own1, own3 = own_came
     fwd_out = own_groups(lengths, front_q, (own0, own1, own2, own3), held)
     sum_came = together((sum_came, fwd_out))[0]

time: 76.7 us -> 75.9 us (0.990)
  transfers between devices with their start and end apart: 22 -> 22, of which waited for: 13 -> 12; matrix products, arithmetic and copies ran while one was open for 0% -> 0% of each run, Pallas kernels for 27% -> 27%
where the time goes in v5:
time: 75.9 us; the launch traced here: 75.4 us
  starting transfers between devices  37.6 us (50%)
  Pallas kernels  20.6 us (27%)
  waiting for transfers between devices  15.3 us (20%)
  other arithmetic  0.94 us (1%)
  between operations  0.9 us (1%)
    ppermute x20, starting transfers between devices, swap(): lax.ppermute(value, 'dp', [(d, partner(d, **steps)) for d in range(64)])  31.7 us
    ppermute x20, waiting for transfers between devices, swap(): lax.ppermute(value, 'dp', [(d, partner(d, **steps)) for d in range(64)])  11.9 us
    pallas_call x1, Pallas kernels, backward_groups(): pl.pallas_call(backward_kernel, out_shape=[jax.ShapeDtypeStruct(q.shape,...  6.17 us
    pallas_call x2, Pallas kernels, stored_groups(): pl.pallas_call(functools.partial(stored_kernel, first), out_shape=[jax.Sh...  5.23 us
    ppermute x1, waiting for transfers between devices, shards(): next_act = lax.ppermute(fwd_out, 'pipe', [(p, p + 1) for p in range(3)])  3.14 us
    ppermute x1, starting transfers between devices, shards(): next_act = lax.ppermute(fwd_out, 'pipe', [(p, p + 1) for p in range(3)])  2.95 us
    pallas_call x1, Pallas kernels, own_groups(): pl.pallas_call(own_kernel, out_shape=jax.ShapeDtypeStruct(q.shape, BF16),...  2.93 us
    ppermute x1, starting transfers between devices, shards(): here = lax.ppermute(leave, 'pipe', [(p + 1, p) for p in range(3)])  2.92 us
  transfers between devices with their start and end apart: 22, of which 12 were waited for; matrix products, arithmetic and copies ran while one was open for 0% of the time, Pallas kernels for 27%

profile of v5, /device:TPU:64, one launch (start us, length us, event | category | flops | bytes accessed | tf_op | source)
XLA Modules:
  0.0 75.4 jit_solution(6087640842503649839)
XLA Ops:
  0.7 5.5 %collective-permute-start = (bf16[56,1024]{1,0:T(8,128)(2,1)}, bf16[56,1024]{1,0:T(8,128)(2,1)S(1)}, u32[]{:S(2)}, u32[]{:S(2)}) collective-permute-start(bf16[56,1024]{1,0:T(8,128)(2,1)} %bitcast.25), channel_id=1, source_target_pairs={{0,128},{4,132},{8,136},{12,140},{16,144},{20,148},{24,152},{28,15... | collective-permute-start | bytes 344072 | tf_op jit(solution)/shard_map/ppermute | solution.py:46
  6.2 2.5 %split_inputs.1 = (bf16[128,896]{1,0:T(8,128)(2,1)}, bf16[128,896]{1,0:T(8,128)(2,1)}, bf16[128,896]{1,0:T(8,128)(2,1)}, bf16[128,896]{1,0:T(8,128)(2,1)}) custom-call(bf16[64,3584]{1,0:T(8,128)(2,1)} %bitcast.27, bf16[64,3584]{1,0:T(8,128)(2,1)} %bitcast.28), custom_call_target="tpu_custom_call" | custom-call | flops 750000000 | bytes 1500000 | tf_op jit(solution)/shard_map/split_inputs/pallas_call | solution.py:73
  8.7 3.1 %collective-permute-start.2 = (bf16[128,896]{1,0:T(8,128)(2,1)}, bf16[128,896]{1,0:T(8,128)(2,1)S(1)}, u32[]{:S(2)}, u32[]{:S(2)}) collective-permute-start(bf16[128,896]{1,0:T(8,128)(2,1)} %get-tuple-element.57), channel_id=1, source_target_pairs={{0,64},{4,68},{8,72},{12,76},{16,80},{20,84},{24,88},{28,92},{32,9... | collective-permute-start | bytes 688136 | tf_op jit(solution)/shard_map/ppermute | solution.py:46
  11.8 0.6 collective-permute-start.3
  12.4 0.6 collective-permute-start.4
  13.0 1.7 %collective-permute-start.1 = (bf16[112,1024]{1,0:T(8,128)(2,1)S(1)}, bf16[112,1024]{1,0:T(8,128)(2,1)S(1)}, u32[]{:S(2)}, u32[]{:S(2)}) collective-permute-start(bf16[112,1024]{1,0:T(8,128)(2,1)S(1)} %pad_maximum_fusion.2), channel_id=1, source_target_pairs={{0,8},{4,12},{8,0},{12,4},{16,24},{20,28},{24,16},{28,20},{32,40},... | collective-permute-start | bytes 688136 | tf_op jit(solution)/shard_map/ppermute | solution.py:46
  14.7 0.0 copy-start.3
  14.7 6.2 %backward_groups.1 = (bf16[64,3584]{1,0:T(8,128)(2,1)}, bf16[64,1024]{1,0:T(8,128)(2,1)S(1)}) custom-call(s32[4]{0:T(128)S(1)} %bitcast.21, bf16[64,3584]{1,0:T(8,128)(2,1)S(1)} %bitcast.16, bf16[64,3584]{1,0:T(8,128)(2,1)S(1)} %bitcast.17, bf16[1024,1024]{1,0:T(8,128)(2,1)S(1)} %bitcast.13), custom_call_target="tpu_custom_call" | custom-call | flops 3500000000 | bytes 7000000 | tf_op jit(solution)/shard_map/backward_groups/pallas_call | solution.py:202
  20.9 1.7 %collective-permute-done.3.r1 = bf16[128,896]{1,0:T(8,128)(2,1)S(1)} collective-permute-done((bf16[128,896]{1,0:T(8,128)(2,1)}, bf16[128,896]{1,0:T(8,128)(2,1)S(1)}, u32[]{:S(2)}, u32[]{:S(2)}) %collective-permute-start.3) | collective-permute-done | bytes 229408 | tf_op jit(solution)/shard_map/ppermute | solution.py:46
  22.6 3.0 %collective-permute-start.8 = (bf16[224,1024]{1,0:T(8,128)(2,1)S(1)}, bf16[224,1024]{1,0:T(8,128)(2,1)S(1)}, u32[]{:S(2)}, u32[]{:S(2)}) collective-permute-start(bf16[224,1024]{1,0:T(8,128)(2,1)S(1)} %pad_maximum_fusion.1), channel_id=1, source_target_pairs={{0,24},{4,28},{8,16},{12,20},{16,8},{20,12},{24,0},{28,4},{32,56},... | collective-permute-start | bytes 1376264 | tf_op jit(solution)/shard_map/ppermute | solution.py:46
  25.6 2.9 %collective-permute-start.5 = (bf16[64,1024]{1,0:T(8,128)(2,1)S(1)}, bf16[64,1024]{1,0:T(8,128)(2,1)S(1)}, u32[]{:S(2)}, u32[]{:S(2)}) collective-permute-start(bf16[64,1024]{1,0:T(8,128)(2,1)S(1)} %get-tuple-element.60.g0), channel_id=1, source_target_pairs={{0,64},{4,68},{8,72},{12,76},{16,80},{20,84},{24,88},{28,92},{32,9... | collective-permute-start | bytes 393224 | tf_op jit(solution)/shard_map/ppermute | solution.py:46
  28.5 1.2 %collective-permute-start.6 = (bf16[64,1024]{1,0:T(8,128)(2,1)S(1)}, bf16[64,1024]{1,0:T(8,128)(2,1)S(1)}, u32[]{:S(2)}, u32[]{:S(2)}) collective-permute-start(bf16[64,1024]{1,0:T(8,128)(2,1)S(1)} %get-tuple-element.60.g0), channel_id=1, source_target_pairs={{0,96},{4,100},{8,104},{12,108},{16,112},{20,116},{24,120},{28,124... | collective-permute-start | bytes 393224 | tf_op jit(solution)/shard_map/ppermute | solution.py:46
  29.7 0.0 collective-permute-start.7
  29.7 2.6 %stored_groups.2 = (f32[64,1792]{1,0:T(8,128)S(1)}, f32[64,256]{1,0:T(8,128)S(1)}) custom-call(s32[4]{0:T(128)S(1)} %bitcast.22, bf16[64,3584]{1,0:T(8,128)(2,1)S(1)} %bitcast.18, bf16[1024,1024]{1,0:T(8,128)(2,1)S(1)} %bitcast.14), custom_call_target="tpu_custom_call" | custom-call | flops 1200000000 | bytes 2400000 | tf_op jit(solution)/shard_map/stored_groups/pallas_call | solution.py:250
  32.4 0.1 collective-permute-done.5.g2
  32.4 2.5 %collective-permute-done.6.g3 = bf16[64,1024]{1,0:T(8,128)(2,1)S(1)} collective-permute-done((bf16[64,1024]{1,0:T(8,128)(2,1)S(1)}, bf16[64,1024]{1,0:T(8,128)(2,1)S(1)}, u32[]{:S(2)}, u32[]{:S(2)}) %collective-permute-start.6) | collective-permute-done | bytes 131104 | tf_op jit(solution)/shard_map/ppermute | solution.py:46
  34.9 0.1 collective-permute-done.7.g1
  35.0 0.9 %weight_grad_halves.1 = (bf16[448,1024]{1,0:T(8,128)(2,1)S(1)}, f32[448,1024]{1,0:T(8,128)S(1)}) custom-call(bf16[128,896]{1,0:T(8,128)(2,1)S(1)} %copy-done.5, bf16[128,896]{1,0:T(8,128)(2,1)S(1)} %collective-permute-done.3.r1, bf16[128,896]{1,0:T(8,128)(2,1)S(1)} %collective-permute-done.2.r2, bf16[128,896]{1,0:T(8,128)(2,1)S(1)} %collective-permute-done.4.r3, ...), custom_call_target="tpu_custom_call" | custom-call | flops 750000000 | bytes 1500000 | tf_op jit(solution)/shard_map/weight_grad_halves/pallas_call | solution.py:366
  35.9 0.1 collective-permute-start.10
  36.0 0.1 pad_maximum_fusion.a_ref
  36.1 0.6 collective-permute-start.9
  36.7 1.8 %collective-permute-done.10.other_ref = bf16[448,1024]{1,0:T(8,128)(2,1)S(1)} collective-permute-done((bf16[448,1024]{1,0:T(8,128)(2,1)S(1)}, bf16[448,1024]{1,0:T(8,128)(2,1)S(1)}, u32[]{:S(2)}, u32[]{:S(2)}) %collective-permute-start.10) | collective-permute-done | bytes 917536 | tf_op jit(solution)/shard_map/ppermute | solution.py:46
  38.5 0.1 chip_sum.1
  38.6 0.2 collective-permute-start.12
  38.8 0.9 %collective-permute-done.9.b_ref = bf16[448,1024]{1,0:T(8,128)(2,1)S(1)} collective-permute-done((bf16[448,1024]{1,0:T(8,128)(2,1)S(1)}, bf16[448,1024]{1,0:T(8,128)(2,1)S(1)}, u32[]{:S(2)}, u32[]{:S(2)}) %collective-permute-start.9) | collective-permute-done | bytes 917536 | tf_op jit(solution)/shard_map/ppermute | solution.py:46
  39.8 0.9 %own_kv_parts.1 = (f32[64,1024]{1,0:T(8,128)S(1)}, bf16[64,1024]{1,0:T(8,128)(2,1)S(1)}, bf16[64,1024]{1,0:T(8,128)(2,1)S(1)}, bf16[64,1024]{1,0:T(8,128)(2,1)S(1)}, bf16[896,1024]{1,0:T(8,128)(2,1)S(1)}) custom-call(bf16[128,896]{1,0:T(8,128)(2,1)S(1)} %copy-done.5, bf16[128,896]{1,0:T(8,128)(2,1)S(1)} %collective-permute-done.3.r1, ...), custom_call_target="tpu_custom_call" | custom-call | flops 750000000 | bytes 1500000 | tf_op jit(solution)/shard_map/own_kv_parts/pallas_call | solution.py:323
  40.7 2.2 %collective-permute-start.13 = (bf16[64,1024]{1,0:T(8,128)(2,1)S(1)}, bf16[64,1024]{1,0:T(8,128)(2,1)S(1)}, u32[]{:S(2)}, u32[]{:S(2)}) collective-permute-start(bf16[64,1024]{1,0:T(8,128)(2,1)S(1)} %get-tuple-element.80), channel_id=1, source_target_pairs={{0,64},{4,68},{8,72},{12,76},{16,80},{20,84},{24,88},{28,92},{32,9... | collective-permute-start | bytes 393224 | tf_op jit(solution)/shard_map/ppermute | solution.py:46
  42.8 1.5 %collective-permute-start.14 = (bf16[64,1024]{1,0:T(8,128)(2,1)S(1)}, bf16[64,1024]{1,0:T(8,128)(2,1)S(1)}, u32[]{:S(2)}, u32[]{:S(2)}) collective-permute-start(bf16[64,1024]{1,0:T(8,128)(2,1)S(1)} %get-tuple-element.81), channel_id=1, source_target_pairs={{0,32},{4,36},{8,40},{12,44},{16,48},{20,52},{24,56},{28,60},{32,0... | collective-permute-start | bytes 393224 | tf_op jit(solution)/shard_map/ppermute | solution.py:46
  44.3 0.6 collective-permute-start.15
  44.9 0.7 input_grad_pieces.1
  45.6 2.9 %collective-permute-start.11 = (bf16[256,896]{1,0:T(8,128)(2,1)S(1)}, bf16[256,896]{1,0:T(8,128)(2,1)S(1)}, u32[]{:S(2)}, u32[]{:S(2)}) collective-permute-start(bf16[256,896]{1,0:T(8,128)(2,1)S(1)} %input_grad_pieces.1), channel_id=1, source_target_pairs={{1,0},{2,1},{3,2},{5,4},{6,5},{7,6},{9,8},{10,9},{11,10},{13,12},{... | collective-permute-start | bytes 1376264 | tf_op jit(solution)/shard_map/ppermute | solution.py:461
  48.6 2.6 %stored_groups.3 = (f32[64,1792]{1,0:T(8,128)S(1)}, f32[64,256]{1,0:T(8,128)S(1)}) custom-call(s32[4]{0:T(128)S(1)} %bitcast.23, bf16[64,3584]{1,0:T(8,128)(2,1)S(1)} %bitcast.19, bf16[1024,1024]{1,0:T(8,128)(2,1)S(1)} %bitcast.15), custom_call_target="tpu_custom_call" | custom-call | flops 1200000000 | bytes 2400000 | tf_op jit(solution)/shard_map/stored_groups/pallas_call | solution.py:250
  51.2 2.9 %own_groups.1 = bf16[64,3584]{1,0:T(8,128)(2,1)S(1)} custom-call(s32[4]{0:T(128)S(1)} %bitcast.24, bf16[64,3584]{1,0:T(8,128)(2,1)S(1)} %bitcast.20, f32[64,1024]{1,0:T(8,128)S(1)} %get-tuple-element.79.k0, bf16[64,1024]{1,0:T(8,128)(2,1)S(1)} %collective-permute-done.14.k1, bf16[64,1024]{1,0:T(8,128)(2,1)S(1)} %collective-permute-done.13.k2, ...), custom_call_target="tpu_custom_call" | custom-call | flops 1000000000 | bytes 2000000 | tf_op jit(solution)/shard_map/own_groups/pallas_call | solution.py:294
  54.2 2.1 %collective-permute-start.19 = (bf16[112,1024]{1,0:T(8,128)(2,1)S(1)}, bf16[112,1024]{1,0:T(8,128)(2,1)S(1)}, u32[]{:S(2)}, u32[]{:S(2)}) collective-permute-start(bf16[112,1024]{1,0:T(8,128)(2,1)S(1)} %add_convert_fusion), channel_id=1, source_target_pairs={{0,24},{4,28},{8,16},{12,20},{16,8},{20,12},{24,0},{28,4},{32,56},... | collective-permute-start | bytes 688136 | tf_op jit(solution)/shard_map/ppermute | solution.py:46
  56.3 3.0 %collective-permute-start.20 = (bf16[64,3584]{1,0:T(8,128)(2,1)S(1)}, bf16[64,3584]{1,0:T(8,128)(2,1)S(1)}, u32[]{:S(2)}, u32[]{:S(2)}) collective-permute-start(bf16[64,3584]{1,0:T(8,128)(2,1)S(1)} %own_groups.1), channel_id=1, source_target_pairs={{0,1},{1,2},{2,3},{4,5},{5,6},{6,7},{8,9},{9,10},{10,11},{12,13},{... | collective-permute-start | bytes 1376264 | tf_op jit(solution)/shard_map/ppermute | solution.py:471
  59.3 0.3 collective-permute-done.11
  59.6 2.8 %collective-permute-start.16 = (bf16[64,896]{1,0:T(8,128)(2,1)S(1)}, bf16[64,896]{1,0:T(8,128)(2,1)S(1)}, u32[]{:S(2)}, u32[]{:S(2)}) collective-permute-start(bf16[64,896]{1,0:T(8,128)(2,1)S(1)} %get-tuple-element.104), channel_id=1, source_target_pairs={{0,64},{4,68},{8,72},{12,76},{16,80},{20,84},{24,88},{28,92},{32,9... | collective-permute-start | bytes 344072 | tf_op jit(solution)/shard_map/ppermute | solution.py:46
  62.4 0.6 collective-permute-start.17
  62.9 0.8 %collective-permute-start.18 = (bf16[64,896]{1,0:T(8,128)(2,1)S(1)}, bf16[64,896]{1,0:T(8,128)(2,1)S(1)}, u32[]{:S(2)}, u32[]{:S(2)}) collective-permute-start(bf16[64,896]{1,0:T(8,128)(2,1)S(1)} %get-tuple-element.102), channel_id=1, source_target_pairs={{0,96},{4,100},{8,104},{12,108},{16,112},{20,116},{24,120},{28,124... | collective-permute-start | bytes 344072 | tf_op jit(solution)/shard_map/ppermute | solution.py:46
  63.8 0.1 convert_add_fusion
  63.9 1.8 %collective-permute-start.21 = (bf16[56,1024]{1,0:T(8,128)(2,1)S(1)}, bf16[56,1024]{1,0:T(8,128)(2,1)S(1)}, u32[]{:S(2)}, u32[]{:S(2)}) collective-permute-start(bf16[56,1024]{1,0:T(8,128)(2,1)S(1)} %slice.41), channel_id=1, source_target_pairs={{0,128},{4,132},{8,136},{12,140},{16,144},{20,148},{24,152},{28,15... | collective-permute-start | bytes 344072 | tf_op jit(solution)/shard_map/ppermute | solution.py:46
  65.6 0.6 collective-permute-done.16.g2
  66.3 1.0 %collective-permute-done.17.g1 = bf16[64,896]{1,0:T(8,128)(2,1)S(1)} collective-permute-done((bf16[64,896]{1,0:T(8,128)(2,1)S(1)}, bf16[64,896]{1,0:T(8,128)(2,1)S(1)}, u32[]{:S(2)}, u32[]{:S(2)}) %collective-permute-start.17) | collective-permute-done | bytes 114720 | tf_op jit(solution)/shard_map/ppermute | solution.py:46
  67.3 1.7 %collective-permute-done.18.g3 = bf16[64,896]{1,0:T(8,128)(2,1)S(1)} collective-permute-done((bf16[64,896]{1,0:T(8,128)(2,1)S(1)}, bf16[64,896]{1,0:T(8,128)(2,1)S(1)}, u32[]{:S(2)}, u32[]{:S(2)}) %collective-permute-start.18) | collective-permute-done | bytes 114720 | tf_op jit(solution)/shard_map/ppermute | solution.py:46
  69.0 3.1 %collective-permute-done.20.act_ref = bf16[64,3584]{1,0:T(8,128)(2,1)S(1)} collective-permute-done((bf16[64,3584]{1,0:T(8,128)(2,1)S(1)}, bf16[64,3584]{1,0:T(8,128)(2,1)S(1)}, u32[]{:S(2)}, u32[]{:S(2)}) %collective-permute-start.20) | collective-permute-done | bytes 458784 | tf_op jit(solution)/shard_map/ppermute | solution.py:471
  72.1 1.1 %join_pieces.1 = (bf16[64,3584]{1,0:T(8,128)(2,1)}, bf16[64,3584]{1,0:T(8,128)(2,1)}) custom-call(bf16[64,896]{1,0:T(8,128)(2,1)S(1)} %get-tuple-element.105.g0, bf16[64,896]{1,0:T(8,128)(2,1)S(1)} %collective-permute-done.17.g1, bf16[64,896]{1,0:T(8,128)(2,1)S(1)} %collective-permute-done.16.g2, bf16[64,896]{1,0:T(8,128)(2,1)S(1)} %collective-permute-done.18.g3, ...), custom_call_target="tpu_custom_call" | custom-call | flops 500000000 | bytes 1000000 | tf_op jit(solution)/shard_map/join_pieces/pallas_call | solution.py:101
  73.2 1.4 %collective-permute-done.21 = bf16[56,1024]{1,0:T(8,128)(2,1)S(1)} collective-permute-done((bf16[56,1024]{1,0:T(8,128)(2,1)S(1)}, bf16[56,1024]{1,0:T(8,128)(2,1)S(1)}, u32[]{:S(2)}, u32[]{:S(2)}) %collective-permute-start.21) | collective-permute-done | bytes 114720 | tf_op jit(solution)/shard_map/ppermute | solution.py:46
  74.7 0.7 fusion
  (28 shorter events, 0.2 us)
Async XLA Ops:
  0.6 12.3 %copy-start.6 = (bf16[1,56,1024]{2,1,0:T(8,128)(2,1)S(1)}, bf16[1,56,1024]{2,1,0:T(8,128)(2,1)}, u32[]{:S(2)}) copy-start(bf16[1,56,1024]{2,1,0:T(8,128)(2,1)} %param.14) | copy-start | bytes 344068
  0.6 14.0 %copy-start.4 = (s32[1,1,4]{2,1,0:T(1,128)S(1)}, s32[1,1,4]{2,1,0:T(1,128)}, u32[]{:S(2)}) copy-start(s32[1,1,4]{2,1,0:T(1,128)} %param.15) | copy-start | bytes 52
  0.7 14.0 %copy-start = (bf16[1,1,1024,1024]{3,2,1,0:T(8,128)(2,1)S(1)}, bf16[1,1,1024,1024]{3,2,1,0:T(8,128)(2,1)}, u32[]{:S(2)}) copy-start(bf16[1,1,1024,1024]{3,2,1,0:T(8,128)(2,1)} %param.13) | copy-start | bytes 6291460
  0.7 14.0 %copy-start.1 = (bf16[1,1,64,3584]{3,2,1,0:T(8,128)(2,1)S(1)}, bf16[1,1,64,3584]{3,2,1,0:T(8,128)(2,1)}, u32[]{:S(2)}) copy-start(bf16[1,1,64,3584]{3,2,1,0:T(8,128)(2,1)} %param.11) | copy-start | bytes 1376260
  0.7 14.0 %copy-start.2 = (bf16[1,1,64,3584]{3,2,1,0:T(8,128)(2,1)S(1)}, bf16[1,1,64,3584]{3,2,1,0:T(8,128)(2,1)}, u32[]{:S(2)}) copy-start(bf16[1,1,64,3584]{3,2,1,0:T(8,128)(2,1)} %param.12) | copy-start | bytes 1376260
  0.7 12.3 %collective-permute-start = (bf16[56,1024]{1,0:T(8,128)(2,1)}, bf16[56,1024]{1,0:T(8,128)(2,1)S(1)}, u32[]{:S(2)}, u32[]{:S(2)}) collective-permute-start(bf16[56,1024]{1,0:T(8,128)(2,1)} %bitcast.25), channel_id=1, source_target_pairs={{0,128},{4,132},{8,136},{12,140},{16,144},{20,148},{24,152},{28,15... | collective-permute-start | bytes 344072 | tf_op jit(solution)/shard_map/ppermute | solution.py:46
  8.7 12.2 %collective-permute-start.2 = (bf16[128,896]{1,0:T(8,128)(2,1)}, bf16[128,896]{1,0:T(8,128)(2,1)S(1)}, u32[]{:S(2)}, u32[]{:S(2)}) collective-permute-start(bf16[128,896]{1,0:T(8,128)(2,1)} %get-tuple-element.57), channel_id=1, source_target_pairs={{0,64},{4,68},{8,72},{12,76},{16,80},{20,84},{24,88},{28,92},{32,9... | collective-permute-start | bytes 688136 | tf_op jit(solution)/shard_map/ppermute | solution.py:46
  11.8 10.8 %collective-permute-start.3 = (bf16[128,896]{1,0:T(8,128)(2,1)}, bf16[128,896]{1,0:T(8,128)(2,1)S(1)}, u32[]{:S(2)}, u32[]{:S(2)}) collective-permute-start(bf16[128,896]{1,0:T(8,128)(2,1)} %get-tuple-element.58), channel_id=1, source_target_pairs={{0,32},{4,36},{8,40},{12,44},{16,48},{20,52},{24,56},{28,60},{32,0... | collective-permute-start | bytes 688136 | tf_op jit(solution)/shard_map/ppermute | solution.py:46
  12.4 10.2 %collective-permute-start.4 = (bf16[128,896]{1,0:T(8,128)(2,1)}, bf16[128,896]{1,0:T(8,128)(2,1)S(1)}, u32[]{:S(2)}, u32[]{:S(2)}) collective-permute-start(bf16[128,896]{1,0:T(8,128)(2,1)} %get-tuple-element.59), channel_id=1, source_target_pairs={{0,96},{4,100},{8,104},{12,108},{16,112},{20,116},{24,120},{28,124... | collective-permute-start | bytes 688136 | tf_op jit(solution)/shard_map/ppermute | solution.py:46
  13.0 7.9 %collective-permute-start.1 = (bf16[112,1024]{1,0:T(8,128)(2,1)S(1)}, bf16[112,1024]{1,0:T(8,128)(2,1)S(1)}, u32[]{:S(2)}, u32[]{:S(2)}) collective-permute-start(bf16[112,1024]{1,0:T(8,128)(2,1)S(1)} %pad_maximum_fusion.2), channel_id=1, source_target_pairs={{0,8},{4,12},{8,0},{12,4},{16,24},{20,28},{24,16},{28,20},{32,40},... | collective-permute-start | bytes 688136 | tf_op jit(solution)/shard_map/ppermute | solution.py:46
  14.7 15.1 %copy-start.3 = (bf16[1,1,64,3584]{3,2,1,0:T(8,128)(2,1)S(1)}, bf16[1,1,64,3584]{3,2,1,0:T(8,128)(2,1)}, u32[]{:S(2)}) copy-start(bf16[1,1,64,3584]{3,2,1,0:T(8,128)(2,1)} %param.9) | copy-start | bytes 1376260
  22.6 13.4 %collective-permute-start.8 = (bf16[224,1024]{1,0:T(8,128)(2,1)S(1)}, bf16[224,1024]{1,0:T(8,128)(2,1)S(1)}, u32[]{:S(2)}, u32[]{:S(2)}) collective-permute-start(bf16[224,1024]{1,0:T(8,128)(2,1)S(1)} %pad_maximum_fusion.1), channel_id=1, source_target_pairs={{0,24},{4,28},{8,16},{12,20},{16,8},{20,12},{24,0},{28,4},{32,56},... | collective-permute-start | bytes 1376264 | tf_op jit(solution)/shard_map/ppermute | solution.py:46
  25.6 6.8 %collective-permute-start.5 = (bf16[64,1024]{1,0:T(8,128)(2,1)S(1)}, bf16[64,1024]{1,0:T(8,128)(2,1)S(1)}, u32[]{:S(2)}, u32[]{:S(2)}) collective-permute-start(bf16[64,1024]{1,0:T(8,128)(2,1)S(1)} %get-tuple-element.60.g0), channel_id=1, source_target_pairs={{0,64},{4,68},{8,72},{12,76},{16,80},{20,84},{24,88},{28,92},{32,9... | collective-permute-start | bytes 393224 | tf_op jit(solution)/shard_map/ppermute | solution.py:46
  28.5 6.4 %collective-permute-start.6 = (bf16[64,1024]{1,0:T(8,128)(2,1)S(1)}, bf16[64,1024]{1,0:T(8,128)(2,1)S(1)}, u32[]{:S(2)}, u32[]{:S(2)}) collective-permute-start(bf16[64,1024]{1,0:T(8,128)(2,1)S(1)} %get-tuple-element.60.g0), channel_id=1, source_target_pairs={{0,96},{4,100},{8,104},{12,108},{16,112},{20,116},{24,120},{28,124... | collective-permute-start | bytes 393224 | tf_op jit(solution)/shard_map/ppermute | solution.py:46
  29.7 5.3 %collective-permute-start.7 = (bf16[64,1024]{1,0:T(8,128)(2,1)S(1)}, bf16[64,1024]{1,0:T(8,128)(2,1)S(1)}, u32[]{:S(2)}, u32[]{:S(2)}) collective-permute-start(bf16[64,1024]{1,0:T(8,128)(2,1)S(1)} %get-tuple-element.60.g0), channel_id=1, source_target_pairs={{0,32},{4,36},{8,40},{12,44},{16,48},{20,52},{24,56},{28,60},{32,0... | collective-permute-start | bytes 393224 | tf_op jit(solution)/shard_map/ppermute | solution.py:46
  29.7 5.3 %copy-start.5 = (bf16[128,896]{1,0:T(8,128)(2,1)S(1)}, bf16[128,896]{1,0:T(8,128)(2,1)}, u32[]{:S(2)}) copy-start(bf16[128,896]{1,0:T(8,128)(2,1)} %get-tuple-element.67.r0) | copy-start | bytes 688132
  35.9 2.6 %collective-permute-start.10 = (bf16[448,1024]{1,0:T(8,128)(2,1)S(1)}, bf16[448,1024]{1,0:T(8,128)(2,1)S(1)}, u32[]{:S(2)}, u32[]{:S(2)}) collective-permute-start(bf16[448,1024]{1,0:T(8,128)(2,1)S(1)} %get-tuple-element.72), channel_id=1, source_target_pairs={{0,4},{4,0},{8,12},{12,8},{16,20},{20,16},{24,28},{28,24},{32,36},... | collective-permute-start | bytes 2752520 | tf_op jit(solution)/shard_map/ppermute | solution.py:46
  36.1 3.7 %collective-permute-start.9 = (bf16[448,1024]{1,0:T(8,128)(2,1)S(1)}, bf16[448,1024]{1,0:T(8,128)(2,1)S(1)}, u32[]{:S(2)}, u32[]{:S(2)}) collective-permute-start(bf16[448,1024]{1,0:T(8,128)(2,1)S(1)} %pad_maximum_fusion.a_ref), channel_id=1, source_target_pairs={{0,4},{4,0},{8,12},{12,8},{16,20},{20,16},{24,28},{28,24},{32,36},... | collective-permute-start | bytes 2752520 | tf_op jit(solution)/shard_map/ppermute | solution.py:46
  38.6 15.5 %collective-permute-start.12 = (bf16[224,1024]{1,0:T(8,128)(2,1)S(1)}, bf16[224,1024]{1,0:T(8,128)(2,1)S(1)}, u32[]{:S(2)}, u32[]{:S(2)}) collective-permute-start(bf16[224,1024]{1,0:T(8,128)(2,1)S(1)} %get-tuple-element.75), channel_id=1, source_target_pairs={{0,8},{4,12},{8,0},{12,4},{16,24},{20,28},{24,16},{28,20},{32,40},... | collective-permute-start | bytes 1376264 | tf_op jit(solution)/shard_map/ppermute | solution.py:46
  40.7 10.5 %collective-permute-start.13 = (bf16[64,1024]{1,0:T(8,128)(2,1)S(1)}, bf16[64,1024]{1,0:T(8,128)(2,1)S(1)}, u32[]{:S(2)}, u32[]{:S(2)}) collective-permute-start(bf16[64,1024]{1,0:T(8,128)(2,1)S(1)} %get-tuple-element.80), channel_id=1, source_target_pairs={{0,64},{4,68},{8,72},{12,76},{16,80},{20,84},{24,88},{28,92},{32,9... | collective-permute-start | bytes 393224 | tf_op jit(solution)/shard_map/ppermute | solution.py:46
  42.8 8.4 %collective-permute-start.14 = (bf16[64,1024]{1,0:T(8,128)(2,1)S(1)}, bf16[64,1024]{1,0:T(8,128)(2,1)S(1)}, u32[]{:S(2)}, u32[]{:S(2)}) collective-permute-start(bf16[64,1024]{1,0:T(8,128)(2,1)S(1)} %get-tuple-element.81), channel_id=1, source_target_pairs={{0,32},{4,36},{8,40},{12,44},{16,48},{20,52},{24,56},{28,60},{32,0... | collective-permute-start | bytes 393224 | tf_op jit(solution)/shard_map/ppermute | solution.py:46
  44.3 6.9 %collective-permute-start.15 = (bf16[64,1024]{1,0:T(8,128)(2,1)S(1)}, bf16[64,1024]{1,0:T(8,128)(2,1)S(1)}, u32[]{:S(2)}, u32[]{:S(2)}) collective-permute-start(bf16[64,1024]{1,0:T(8,128)(2,1)S(1)} %get-tuple-element.82), channel_id=1, source_target_pairs={{0,96},{4,100},{8,104},{12,108},{16,112},{20,116},{24,120},{28,124... | collective-permute-start | bytes 393224 | tf_op jit(solution)/shard_map/ppermute | solution.py:46
  45.6 13.9 %collective-permute-start.11 = (bf16[256,896]{1,0:T(8,128)(2,1)S(1)}, bf16[256,896]{1,0:T(8,128)(2,1)S(1)}, u32[]{:S(2)}, u32[]{:S(2)}) collective-permute-start(bf16[256,896]{1,0:T(8,128)(2,1)S(1)} %input_grad_pieces.1), channel_id=1, source_target_pairs={{1,0},{2,1},{3,2},{5,4},{6,5},{7,6},{9,8},{10,9},{11,10},{13,12},{... | collective-permute-start | bytes 1376264 | tf_op jit(solution)/shard_map/ppermute | solution.py:461
  54.2 9.5 %collective-permute-start.19 = (bf16[112,1024]{1,0:T(8,128)(2,1)S(1)}, bf16[112,1024]{1,0:T(8,128)(2,1)S(1)}, u32[]{:S(2)}, u32[]{:S(2)}) collective-permute-start(bf16[112,1024]{1,0:T(8,128)(2,1)S(1)} %add_convert_fusion), channel_id=1, source_target_pairs={{0,24},{4,28},{8,16},{12,20},{16,8},{20,12},{24,0},{28,4},{32,56},... | collective-permute-start | bytes 688136 | tf_op jit(solution)/shard_map/ppermute | solution.py:46
  56.3 15.8 %collective-permute-start.20 = (bf16[64,3584]{1,0:T(8,128)(2,1)S(1)}, bf16[64,3584]{1,0:T(8,128)(2,1)S(1)}, u32[]{:S(2)}, u32[]{:S(2)}) collective-permute-start(bf16[64,3584]{1,0:T(8,128)(2,1)S(1)} %own_groups.1), channel_id=1, source_target_pairs={{0,1},{1,2},{2,3},{4,5},{5,6},{6,7},{8,9},{9,10},{10,11},{12,13},{... | collective-permute-start | bytes 1376264 | tf_op jit(solution)/shard_map/ppermute | solution.py:471
  59.6 6.7 %collective-permute-start.16 = (bf16[64,896]{1,0:T(8,128)(2,1)S(1)}, bf16[64,896]{1,0:T(8,128)(2,1)S(1)}, u32[]{:S(2)}, u32[]{:S(2)}) collective-permute-start(bf16[64,896]{1,0:T(8,128)(2,1)S(1)} %get-tuple-element.104), channel_id=1, source_target_pairs={{0,64},{4,68},{8,72},{12,76},{16,80},{20,84},{24,88},{28,92},{32,9... | collective-permute-start | bytes 344072 | tf_op jit(solution)/shard_map/ppermute | solution.py:46
  62.4 4.9 %collective-permute-start.17 = (bf16[64,896]{1,0:T(8,128)(2,1)S(1)}, bf16[64,896]{1,0:T(8,128)(2,1)S(1)}, u32[]{:S(2)}, u32[]{:S(2)}) collective-permute-start(bf16[64,896]{1,0:T(8,128)(2,1)S(1)} %get-tuple-element.103), channel_id=1, source_target_pairs={{0,32},{4,36},{8,40},{12,44},{16,48},{20,52},{24,56},{28,60},{32,0... | collective-permute-start | bytes 344072 | tf_op jit(solution)/shard_map/ppermute | solution.py:46
  62.9 6.0 %collective-permute-start.18 = (bf16[64,896]{1,0:T(8,128)(2,1)S(1)}, bf16[64,896]{1,0:T(8,128)(2,1)S(1)}, u32[]{:S(2)}, u32[]{:S(2)}) collective-permute-start(bf16[64,896]{1,0:T(8,128)(2,1)S(1)} %get-tuple-element.102), channel_id=1, source_target_pairs={{0,96},{4,100},{8,104},{12,108},{16,112},{20,116},{24,120},{28,124... | collective-permute-start | bytes 344072 | tf_op jit(solution)/shard_map/ppermute | solution.py:46
  63.9 10.8 %collective-permute-start.21 = (bf16[56,1024]{1,0:T(8,128)(2,1)S(1)}, bf16[56,1024]{1,0:T(8,128)(2,1)S(1)}, u32[]{:S(2)}, u32[]{:S(2)}) collective-permute-start(bf16[56,1024]{1,0:T(8,128)(2,1)S(1)} %slice.41), channel_id=1, source_target_pairs={{0,128},{4,132},{8,136},{12,140},{16,144},{20,148},{24,152},{28,15... | collective-permute-start | bytes 344072 | tf_op jit(solution)/shard_map/ppermute | solution.py:46

commit v6 on v5

--- a/solution.py
+++ b/solution.py
@@ -466,20 +466,22 @@
     own2, own1, own3 = own_came
     fwd_out = own_groups(lengths, front_q, (own0, own1, own2, own3), held)
     sum_came = together((sum_came, fwd_out))[0]
-    sum_leave = (sum3 + sum_came[2 * BLK :].astype(F32)).astype(BF16)
-    fwd_out = together((fwd_out, sum_leave))[0]
+    far_leave = (sum3[BLK:] + sum_came[3 * BLK :].astype(F32)).astype(BF16)
+    far_last = swap(far_leave, y=3)
+    fwd_out = together((fwd_out, far_leave))[0]
     next_act = lax.ppermute(fwd_out, "pipe", [(p, p + 1) for p in range(3)])
-    sum_last = swap(sum_leave, y=3)
-    here = together((here, sum_leave))[0]
+    far_total = sum0[BLK:] + sum_came[BLK : 2 * BLK].astype(F32) + far_last.astype(F32)
+    far_total = far_total.astype(BF16)
+    far_came = swap(far_total, z=1)
+    near_leave = (sum3[:BLK] + sum_came[2 * BLK : 3 * BLK].astype(F32)).astype(BF16)
+    near_last = swap(near_leave, y=3)
+    here = together((here, far_total))[0]
     blocks = [here[at * SEG : (at + 1) * SEG] for at in (0, 1, 3, 2)]
     came = [swap(blocks[r], x=r) for r in (2, 1, 3)]
-    total = sum0 + sum_came[: 2 * BLK].astype(F32) + sum_last.astype(F32)
-    far_total = total[BLK:].astype(BF16)
-    far_came = swap(far_total, z=1)
-    came = together((*came, far_total))[:3]
+    far_came, *came, near_last = together((far_came, *came, near_last))
+    weight_grad = sum0[:BLK] + sum_came[:BLK].astype(F32) + near_last.astype(F32)
+    weight_grad = weight_grad + far_came.astype(F32)
     prev_grad, next_act = join_pieces(blocks[0], came[1], came[0], came[2], next_act)
-    far_came = together((far_came, prev_grad))[0]
-    weight_grad = total[:BLK] + far_came.astype(F32)
     return (next_act[None, None], grad_query[None, None], prev_grad[None, None], weight_grad[None])
 
 

time: 75.9 us -> 78.3 us (1.032)
  waiting for transfers between devices: 15.3 us -> 17.2 us
  starting transfers between devices: 37.6 us -> 38.4 us
    ppermute x20 -> x21, waiting for transfers between devices: 11.9 us -> 17.2 us  [swap(): lax.ppermute(value, 'dp', [(d, partner(d, **steps)) for d in range(64)])]
    ppermute x1, waiting for transfers between devices: 3.14 us -> 0.01 us  [shards(): next_act = lax.ppermute(fwd_out, 'pipe', [(p, p + 1) for p in range(3)])]
    ppermute x20 -> x21, starting transfers between devices: 31.7 us -> 32.6 us  [swap(): lax.ppermute(value, 'dp', [(d, partner(d, **steps)) for d in range(64)])]
  transfers between devices with their start and end apart: 22 -> 23, of which waited for: 12 -> 8; matrix products, arithmetic and copies ran while one was open for 0% -> 1% of each run, Pallas kernels for 27% -> 25%
where the time goes in v6:
time: 78.3 us; the launch traced here: 78.1 us
  starting transfers between devices  38.4 us (49%)
  Pallas kernels  20.6 us (26%)
  waiting for transfers between devices  17.2 us (22%)
  other arithmetic  0.94 us (1%)
  between operations  0.9 us (1%)
    ppermute x21, starting transfers between devices, swap(): lax.ppermute(value, 'dp', [(d, partner(d, **steps)) for d in range(64)])  32.6 us
    ppermute x21, waiting for transfers between devices, swap(): lax.ppermute(value, 'dp', [(d, partner(d, **steps)) for d in range(64)])  17.2 us
    pallas_call x1, Pallas kernels, backward_groups(): pl.pallas_call(backward_kernel, out_shape=[jax.ShapeDtypeStruct(q.shape,...  6.17 us
    pallas_call x2, Pallas kernels, stored_groups(): pl.pallas_call(functools.partial(stored_kernel, first), out_shape=[jax.Sh...  5.24 us
    ppermute x1, starting transfers between devices, shards(): next_act = lax.ppermute(fwd_out, 'pipe', [(p, p + 1) for p in range(3)])  2.95 us
    pallas_call x1, Pallas kernels, own_groups(): pl.pallas_call(own_kernel, out_shape=jax.ShapeDtypeStruct(q.shape, BF16),...  2.94 us
    ppermute x1, starting transfers between devices, shards(): here = lax.ppermute(leave, 'pipe', [(p + 1, p) for p in range(3)])  2.92 us
    pallas_call x1, Pallas kernels, split_inputs(): pl.pallas_call(split_kernel, out_shape=[jax.ShapeDtypeStruct((2 * SEG, 2...  2.52 us
  transfers between devices with their start and end apart: 23, of which 8 were waited for; matrix products, arithmetic and copies ran while one was open for 1% of the time, Pallas kernels for 25%

profile of v6, /device:TPU:64, one launch (start us, length us, event | category | flops | bytes accessed | tf_op | source)
XLA Modules:
  0.0 78.1 jit_solution(10994305737904718681)
XLA Ops:
  0.7 5.5 %collective-permute-start = (bf16[56,1024]{1,0:T(8,128)(2,1)}, bf16[56,1024]{1,0:T(8,128)(2,1)S(1)}, u32[]{:S(2)}, u32[]{:S(2)}) collective-permute-start(bf16[56,1024]{1,0:T(8,128)(2,1)} %bitcast.25), channel_id=1, source_target_pairs={{0,128},{4,132},{8,136},{12,140},{16,144},{20,148},{24,152},{28,15... | collective-permute-start | bytes 344072 | tf_op jit(solution)/shard_map/ppermute | solution.py:46
  6.2 2.5 %split_inputs.1 = (bf16[128,896]{1,0:T(8,128)(2,1)}, bf16[128,896]{1,0:T(8,128)(2,1)}, bf16[128,896]{1,0:T(8,128)(2,1)}, bf16[128,896]{1,0:T(8,128)(2,1)}) custom-call(bf16[64,3584]{1,0:T(8,128)(2,1)} %bitcast.27, bf16[64,3584]{1,0:T(8,128)(2,1)} %bitcast.28), custom_call_target="tpu_custom_call" | custom-call | flops 750000000 | bytes 1500000 | tf_op jit(solution)/shard_map/split_inputs/pallas_call | solution.py:73
  8.7 3.1 %collective-permute-start.2 = (bf16[128,896]{1,0:T(8,128)(2,1)}, bf16[128,896]{1,0:T(8,128)(2,1)S(1)}, u32[]{:S(2)}, u32[]{:S(2)}) collective-permute-start(bf16[128,896]{1,0:T(8,128)(2,1)} %get-tuple-element.58), channel_id=1, source_target_pairs={{0,64},{4,68},{8,72},{12,76},{16,80},{20,84},{24,88},{28,92},{32,9... | collective-permute-start | bytes 688136 | tf_op jit(solution)/shard_map/ppermute | solution.py:46
  11.8 0.6 collective-permute-start.3
  12.4 0.6 collective-permute-start.4
  12.9 0.0 collective-permute-done
  13.0 1.7 %collective-permute-start.1 = (bf16[112,1024]{1,0:T(8,128)(2,1)S(1)}, bf16[112,1024]{1,0:T(8,128)(2,1)S(1)}, u32[]{:S(2)}, u32[]{:S(2)}) collective-permute-start(bf16[112,1024]{1,0:T(8,128)(2,1)S(1)} %pad_maximum_fusion.2), channel_id=1, source_target_pairs={{0,8},{4,12},{8,0},{12,4},{16,24},{20,28},{24,16},{28,20},{32,40},... | collective-permute-start | bytes 688136 | tf_op jit(solution)/shard_map/ppermute | solution.py:46
  14.6 0.0 copy-start.3
  14.7 6.2 %backward_groups.1 = (bf16[64,3584]{1,0:T(8,128)(2,1)}, bf16[64,1024]{1,0:T(8,128)(2,1)S(1)}) custom-call(s32[4]{0:T(128)S(1)} %bitcast.21, bf16[64,3584]{1,0:T(8,128)(2,1)S(1)} %bitcast.16, bf16[64,3584]{1,0:T(8,128)(2,1)S(1)} %bitcast.17, bf16[1024,1024]{1,0:T(8,128)(2,1)S(1)} %bitcast.13), custom_call_target="tpu_custom_call" | custom-call | flops 3500000000 | bytes 7000000 | tf_op jit(solution)/shard_map/backward_groups/pallas_call | solution.py:202
  20.8 0.0 collective-permute-done.1
  20.9 0.0 collective-permute-done.2.r2
  20.9 1.7 %collective-permute-done.3.r1 = bf16[128,896]{1,0:T(8,128)(2,1)S(1)} collective-permute-done((bf16[128,896]{1,0:T(8,128)(2,1)}, bf16[128,896]{1,0:T(8,128)(2,1)S(1)}, u32[]{:S(2)}, u32[]{:S(2)}) %collective-permute-start.3) | collective-permute-done | bytes 229408 | tf_op jit(solution)/shard_map/ppermute | solution.py:46
  22.6 3.0 %collective-permute-start.8 = (bf16[224,1024]{1,0:T(8,128)(2,1)S(1)}, bf16[224,1024]{1,0:T(8,128)(2,1)S(1)}, u32[]{:S(2)}, u32[]{:S(2)}) collective-permute-start(bf16[224,1024]{1,0:T(8,128)(2,1)S(1)} %pad_maximum_fusion.1), channel_id=1, source_target_pairs={{0,24},{4,28},{8,16},{12,20},{16,8},{20,12},{24,0},{28,4},{32,56},... | collective-permute-start | bytes 1376264 | tf_op jit(solution)/shard_map/ppermute | solution.py:46
  25.6 2.9 %collective-permute-start.5 = (bf16[64,1024]{1,0:T(8,128)(2,1)S(1)}, bf16[64,1024]{1,0:T(8,128)(2,1)S(1)}, u32[]{:S(2)}, u32[]{:S(2)}) collective-permute-start(bf16[64,1024]{1,0:T(8,128)(2,1)S(1)} %get-tuple-element.61.g0), channel_id=1, source_target_pairs={{0,64},{4,68},{8,72},{12,76},{16,80},{20,84},{24,88},{28,92},{32,9... | collective-permute-start | bytes 393224 | tf_op jit(solution)/shard_map/ppermute | solution.py:46
  28.5 1.2 %collective-permute-start.6 = (bf16[64,1024]{1,0:T(8,128)(2,1)S(1)}, bf16[64,1024]{1,0:T(8,128)(2,1)S(1)}, u32[]{:S(2)}, u32[]{:S(2)}) collective-permute-start(bf16[64,1024]{1,0:T(8,128)(2,1)S(1)} %get-tuple-element.61.g0), channel_id=1, source_target_pairs={{0,96},{4,100},{8,104},{12,108},{16,112},{20,116},{24,120},{28,124... | collective-permute-start | bytes 393224 | tf_op jit(solution)/shard_map/ppermute | solution.py:46
  29.7 0.0 collective-permute-start.7
  29.7 2.6 %stored_groups.2 = (f32[64,1792]{1,0:T(8,128)S(1)}, f32[64,256]{1,0:T(8,128)S(1)}) custom-call(s32[4]{0:T(128)S(1)} %bitcast.22, bf16[64,3584]{1,0:T(8,128)(2,1)S(1)} %bitcast.18, bf16[1024,1024]{1,0:T(8,128)(2,1)S(1)} %bitcast.14), custom_call_target="tpu_custom_call" | custom-call | flops 1200000000 | bytes 2400000 | tf_op jit(solution)/shard_map/stored_groups/pallas_call | solution.py:250
  32.4 0.1 collective-permute-done.5.g2
  32.4 2.5 %collective-permute-done.6.g3 = bf16[64,1024]{1,0:T(8,128)(2,1)S(1)} collective-permute-done((bf16[64,1024]{1,0:T(8,128)(2,1)S(1)}, bf16[64,1024]{1,0:T(8,128)(2,1)S(1)}, u32[]{:S(2)}, u32[]{:S(2)}) %collective-permute-start.6) | collective-permute-done | bytes 131104 | tf_op jit(solution)/shard_map/ppermute | solution.py:46
  34.9 0.1 collective-permute-done.7.g1
  35.0 0.9 %weight_grad_halves.1 = (bf16[448,1024]{1,0:T(8,128)(2,1)S(1)}, f32[448,1024]{1,0:T(8,128)S(1)}) custom-call(bf16[128,896]{1,0:T(8,128)(2,1)S(1)} %copy-done.5, bf16[128,896]{1,0:T(8,128)(2,1)S(1)} %collective-permute-done.3.r1, bf16[128,896]{1,0:T(8,128)(2,1)S(1)} %collective-permute-done.2.r2, bf16[128,896]{1,0:T(8,128)(2,1)S(1)} %collective-permute-done.4.r3, ...), custom_call_target="tpu_custom_call" | custom-call | flops 750000000 | bytes 1500000 | tf_op jit(solution)/shard_map/weight_grad_halves/pallas_call | solution.py:366
  35.9 0.1 collective-permute-start.10
  36.0 0.0 collective-permute-done.8
  36.0 0.1 pad_maximum_fusion.a_ref
  36.1 0.6 collective-permute-start.9
  36.7 1.8 %collective-permute-done.10.other_ref = bf16[448,1024]{1,0:T(8,128)(2,1)S(1)} collective-permute-done((bf16[448,1024]{1,0:T(8,128)(2,1)S(1)}, bf16[448,1024]{1,0:T(8,128)(2,1)S(1)}, u32[]{:S(2)}, u32[]{:S(2)}) %collective-permute-start.10) | collective-permute-done | bytes 917536 | tf_op jit(solution)/shard_map/ppermute | solution.py:46
  38.5 0.1 chip_sum.1
  38.6 0.2 collective-permute-start.12
  38.8 0.9 %collective-permute-done.9.b_ref = bf16[448,1024]{1,0:T(8,128)(2,1)S(1)} collective-permute-done((bf16[448,1024]{1,0:T(8,128)(2,1)S(1)}, bf16[448,1024]{1,0:T(8,128)(2,1)S(1)}, u32[]{:S(2)}, u32[]{:S(2)}) %collective-permute-start.9) | collective-permute-done | bytes 917536 | tf_op jit(solution)/shard_map/ppermute | solution.py:46
  39.8 0.9 %own_kv_parts.1 = (f32[64,1024]{1,0:T(8,128)S(1)}, bf16[64,1024]{1,0:T(8,128)(2,1)S(1)}, bf16[64,1024]{1,0:T(8,128)(2,1)S(1)}, bf16[64,1024]{1,0:T(8,128)(2,1)S(1)}, bf16[896,1024]{1,0:T(8,128)(2,1)S(1)}) custom-call(bf16[128,896]{1,0:T(8,128)(2,1)S(1)} %copy-done.5, bf16[128,896]{1,0:T(8,128)(2,1)S(1)} %collective-permute-done.3.r1, ...), custom_call_target="tpu_custom_call" | custom-call | flops 750000000 | bytes 1500000 | tf_op jit(solution)/shard_map/own_kv_parts/pallas_call | solution.py:323
  40.7 2.2 %collective-permute-start.13 = (bf16[64,1024]{1,0:T(8,128)(2,1)S(1)}, bf16[64,1024]{1,0:T(8,128)(2,1)S(1)}, u32[]{:S(2)}, u32[]{:S(2)}) collective-permute-start(bf16[64,1024]{1,0:T(8,128)(2,1)S(1)} %get-tuple-element.81), channel_id=1, source_target_pairs={{0,64},{4,68},{8,72},{12,76},{16,80},{20,84},{24,88},{28,92},{32,9... | collective-permute-start | bytes 393224 | tf_op jit(solution)/shard_map/ppermute | solution.py:46
  42.8 1.5 %collective-permute-start.14 = (bf16[64,1024]{1,0:T(8,128)(2,1)S(1)}, bf16[64,1024]{1,0:T(8,128)(2,1)S(1)}, u32[]{:S(2)}, u32[]{:S(2)}) collective-permute-start(bf16[64,1024]{1,0:T(8,128)(2,1)S(1)} %get-tuple-element.82), channel_id=1, source_target_pairs={{0,32},{4,36},{8,40},{12,44},{16,48},{20,52},{24,56},{28,60},{32,0... | collective-permute-start | bytes 393224 | tf_op jit(solution)/shard_map/ppermute | solution.py:46
  44.3 0.6 collective-permute-start.15
  44.9 0.7 input_grad_pieces.1
  45.6 2.9 %collective-permute-start.11 = (bf16[256,896]{1,0:T(8,128)(2,1)S(1)}, bf16[256,896]{1,0:T(8,128)(2,1)S(1)}, u32[]{:S(2)}, u32[]{:S(2)}) collective-permute-start(bf16[256,896]{1,0:T(8,128)(2,1)S(1)} %input_grad_pieces.1), channel_id=1, source_target_pairs={{1,0},{2,1},{3,2},{5,4},{6,5},{7,6},{9,8},{10,9},{11,10},{13,12},{... | collective-permute-start | bytes 1376264 | tf_op jit(solution)/shard_map/ppermute | solution.py:461
  48.6 2.6 %stored_groups.3 = (f32[64,1792]{1,0:T(8,128)S(1)}, f32[64,256]{1,0:T(8,128)S(1)}) custom-call(s32[4]{0:T(128)S(1)} %bitcast.23, bf16[64,3584]{1,0:T(8,128)(2,1)S(1)} %bitcast.19, bf16[1024,1024]{1,0:T(8,128)(2,1)S(1)} %bitcast.15), custom_call_target="tpu_custom_call" | custom-call | flops 1200000000 | bytes 2400000 | tf_op jit(solution)/shard_map/stored_groups/pallas_call | solution.py:250
  51.2 2.9 %own_groups.1 = bf16[64,3584]{1,0:T(8,128)(2,1)S(1)} custom-call(s32[4]{0:T(128)S(1)} %bitcast.24, bf16[64,3584]{1,0:T(8,128)(2,1)S(1)} %bitcast.20, f32[64,1024]{1,0:T(8,128)S(1)} %get-tuple-element.80.k0, bf16[64,1024]{1,0:T(8,128)(2,1)S(1)} %collective-permute-done.14.k1, bf16[64,1024]{1,0:T(8,128)(2,1)S(1)} %collective-permute-done.13.k2, ...), custom_call_target="tpu_custom_call" | custom-call | flops 1000000000 | bytes 2000000 | tf_op jit(solution)/shard_map/own_groups/pallas_call | solution.py:294
  54.2 2.1 %collective-permute-start.16 = (bf16[56,1024]{1,0:T(8,128)(2,1)S(1)}, bf16[56,1024]{1,0:T(8,128)(2,1)S(1)}, u32[]{:S(2)}, u32[]{:S(2)}) collective-permute-start(bf16[56,1024]{1,0:T(8,128)(2,1)S(1)} %get-tuple-element.105), channel_id=1, source_target_pairs={{0,24},{4,28},{8,16},{12,20},{16,8},{20,12},{24,0},{28,4},{32,56},... | collective-permute-start | bytes 344072 | tf_op jit(solution)/shard_map/ppermute | solution.py:46
  56.3 1.2 %collective-permute-start.21 = (bf16[56,1024]{1,0:T(8,128)(2,1)S(1)}, bf16[56,1024]{1,0:T(8,128)(2,1)S(1)}, u32[]{:S(2)}, u32[]{:S(2)}) collective-permute-start(bf16[56,1024]{1,0:T(8,128)(2,1)S(1)} %get-tuple-element.104), channel_id=1, source_target_pairs={{0,24},{4,28},{8,16},{12,20},{16,8},{20,12},{24,0},{28,4},{32,56},... | collective-permute-start | bytes 344072 | tf_op jit(solution)/shard_map/ppermute | solution.py:46
  57.6 3.0 %collective-permute-start.22 = (bf16[64,3584]{1,0:T(8,128)(2,1)S(1)}, bf16[64,3584]{1,0:T(8,128)(2,1)S(1)}, u32[]{:S(2)}, u32[]{:S(2)}) collective-permute-start(bf16[64,3584]{1,0:T(8,128)(2,1)S(1)} %own_groups.1), channel_id=1, source_target_pairs={{0,1},{1,2},{2,3},{4,5},{5,6},{6,7},{8,9},{9,10},{10,11},{12,13},{... | collective-permute-start | bytes 1376264 | tf_op jit(solution)/shard_map/ppermute | solution.py:472
  60.5 1.0 %collective-permute-done.16 = bf16[56,1024]{1,0:T(8,128)(2,1)S(1)} collective-permute-done((bf16[56,1024]{1,0:T(8,128)(2,1)S(1)}, bf16[56,1024]{1,0:T(8,128)(2,1)S(1)}, u32[]{:S(2)}, u32[]{:S(2)}) %collective-permute-start.16) | collective-permute-done | bytes 114720 | tf_op jit(solution)/shard_map/ppermute | solution.py:46
  61.5 1.4 %collective-permute-start.17 = (bf16[56,1024]{1,0:T(8,128)(2,1)S(1)}, bf16[56,1024]{1,0:T(8,128)(2,1)S(1)}, u32[]{:S(2)}, u32[]{:S(2)}) collective-permute-start(bf16[56,1024]{1,0:T(8,128)(2,1)S(1)} %add_convert_fusion.1), channel_id=1, source_target_pairs={{0,128},{4,132},{8,136},{12,140},{16,144},{20,148},{24,152},{28,15... | collective-permute-start | bytes 344072 | tf_op jit(solution)/shard_map/ppermute | solution.py:46
  63.0 1.8 %collective-permute-start.18 = (bf16[64,896]{1,0:T(8,128)(2,1)S(1)}, bf16[64,896]{1,0:T(8,128)(2,1)S(1)}, u32[]{:S(2)}, u32[]{:S(2)}) collective-permute-start(bf16[64,896]{1,0:T(8,128)(2,1)S(1)} %get-tuple-element.108), channel_id=1, source_target_pairs={{0,64},{4,68},{8,72},{12,76},{16,80},{20,84},{24,88},{28,92},{32,9... | collective-permute-start | bytes 344072 | tf_op jit(solution)/shard_map/ppermute | solution.py:46
  64.7 1.9 %collective-permute-start.19 = (bf16[64,896]{1,0:T(8,128)(2,1)S(1)}, bf16[64,896]{1,0:T(8,128)(2,1)S(1)}, u32[]{:S(2)}, u32[]{:S(2)}) collective-permute-start(bf16[64,896]{1,0:T(8,128)(2,1)S(1)} %get-tuple-element.107), channel_id=1, source_target_pairs={{0,32},{4,36},{8,40},{12,44},{16,48},{20,52},{24,56},{28,60},{32,0... | collective-permute-start | bytes 344072 | tf_op jit(solution)/shard_map/ppermute | solution.py:46
  66.7 0.5 collective-permute-start.20
  67.2 9.1 %collective-permute-done.17 = bf16[56,1024]{1,0:T(8,128)(2,1)S(1)} collective-permute-done((bf16[56,1024]{1,0:T(8,128)(2,1)S(1)}, bf16[56,1024]{1,0:T(8,128)(2,1)S(1)}, u32[]{:S(2)}, u32[]{:S(2)}) %collective-permute-start.17) | collective-permute-done | bytes 114720 | tf_op jit(solution)/shard_map/ppermute | solution.py:46
  76.2 0.7 add_bitcast_fusion
  77.0 1.1 %join_pieces.1 = (bf16[64,3584]{1,0:T(8,128)(2,1)}, bf16[64,3584]{1,0:T(8,128)(2,1)}) custom-call(bf16[64,896]{1,0:T(8,128)(2,1)S(1)} %get-tuple-element.109.g0, bf16[64,896]{1,0:T(8,128)(2,1)S(1)} %collective-permute-done.19.g1, bf16[64,896]{1,0:T(8,128)(2,1)S(1)} %collective-permute-done.18.g2, bf16[64,896]{1,0:T(8,128)(2,1)S(1)} %collective-permute-done.20.g3, ...), custom_call_target="tpu_custom_call" | custom-call | flops 500000000 | bytes 1000000 | tf_op jit(solution)/shard_map/join_pieces/pallas_call | solution.py:101
  (29 shorter events, 0.2 us)
Async XLA Ops:
  0.6 12.3 %copy-start.6 = (bf16[1,56,1024]{2,1,0:T(8,128)(2,1)S(1)}, bf16[1,56,1024]{2,1,0:T(8,128)(2,1)}, u32[]{:S(2)}) copy-start(bf16[1,56,1024]{2,1,0:T(8,128)(2,1)} %param.14) | copy-start | bytes 344068
  0.6 14.0 %copy-start.4 = (s32[1,1,4]{2,1,0:T(1,128)S(1)}, s32[1,1,4]{2,1,0:T(1,128)}, u32[]{:S(2)}) copy-start(s32[1,1,4]{2,1,0:T(1,128)} %param.15) | copy-start | bytes 52
  0.7 14.0 %copy-start = (bf16[1,1,1024,1024]{3,2,1,0:T(8,128)(2,1)S(1)}, bf16[1,1,1024,1024]{3,2,1,0:T(8,128)(2,1)}, u32[]{:S(2)}) copy-start(bf16[1,1,1024,1024]{3,2,1,0:T(8,128)(2,1)} %param.13) | copy-start | bytes 6291460
  0.7 14.0 %copy-start.1 = (bf16[1,1,64,3584]{3,2,1,0:T(8,128)(2,1)S(1)}, bf16[1,1,64,3584]{3,2,1,0:T(8,128)(2,1)}, u32[]{:S(2)}) copy-start(bf16[1,1,64,3584]{3,2,1,0:T(8,128)(2,1)} %param.11) | copy-start | bytes 1376260
  0.7 14.0 %copy-start.2 = (bf16[1,1,64,3584]{3,2,1,0:T(8,128)(2,1)S(1)}, bf16[1,1,64,3584]{3,2,1,0:T(8,128)(2,1)}, u32[]{:S(2)}) copy-start(bf16[1,1,64,3584]{3,2,1,0:T(8,128)(2,1)} %param.12) | copy-start | bytes 1376260
  0.7 12.3 %collective-permute-start = (bf16[56,1024]{1,0:T(8,128)(2,1)}, bf16[56,1024]{1,0:T(8,128)(2,1)S(1)}, u32[]{:S(2)}, u32[]{:S(2)}) collective-permute-start(bf16[56,1024]{1,0:T(8,128)(2,1)} %bitcast.25), channel_id=1, source_target_pairs={{0,128},{4,132},{8,136},{12,140},{16,144},{20,148},{24,152},{28,15... | collective-permute-start | bytes 344072 | tf_op jit(solution)/shard_map/ppermute | solution.py:46
  8.7 12.2 %collective-permute-start.2 = (bf16[128,896]{1,0:T(8,128)(2,1)}, bf16[128,896]{1,0:T(8,128)(2,1)S(1)}, u32[]{:S(2)}, u32[]{:S(2)}) collective-permute-start(bf16[128,896]{1,0:T(8,128)(2,1)} %get-tuple-element.58), channel_id=1, source_target_pairs={{0,64},{4,68},{8,72},{12,76},{16,80},{20,84},{24,88},{28,92},{32,9... | collective-permute-start | bytes 688136 | tf_op jit(solution)/shard_map/ppermute | solution.py:46
  11.8 10.8 %collective-permute-start.3 = (bf16[128,896]{1,0:T(8,128)(2,1)}, bf16[128,896]{1,0:T(8,128)(2,1)S(1)}, u32[]{:S(2)}, u32[]{:S(2)}) collective-permute-start(bf16[128,896]{1,0:T(8,128)(2,1)} %get-tuple-element.59), channel_id=1, source_target_pairs={{0,32},{4,36},{8,40},{12,44},{16,48},{20,52},{24,56},{28,60},{32,0... | collective-permute-start | bytes 688136 | tf_op jit(solution)/shard_map/ppermute | solution.py:46
  12.4 10.2 %collective-permute-start.4 = (bf16[128,896]{1,0:T(8,128)(2,1)}, bf16[128,896]{1,0:T(8,128)(2,1)S(1)}, u32[]{:S(2)}, u32[]{:S(2)}) collective-permute-start(bf16[128,896]{1,0:T(8,128)(2,1)} %get-tuple-element.60), channel_id=1, source_target_pairs={{0,96},{4,100},{8,104},{12,108},{16,112},{20,116},{24,120},{28,124... | collective-permute-start | bytes 688136 | tf_op jit(solution)/shard_map/ppermute | solution.py:46
  13.0 7.9 %collective-permute-start.1 = (bf16[112,1024]{1,0:T(8,128)(2,1)S(1)}, bf16[112,1024]{1,0:T(8,128)(2,1)S(1)}, u32[]{:S(2)}, u32[]{:S(2)}) collective-permute-start(bf16[112,1024]{1,0:T(8,128)(2,1)S(1)} %pad_maximum_fusion.2), channel_id=1, source_target_pairs={{0,8},{4,12},{8,0},{12,4},{16,24},{20,28},{24,16},{28,20},{32,40},... | collective-permute-start | bytes 688136 | tf_op jit(solution)/shard_map/ppermute | solution.py:46
  14.6 15.1 %copy-start.3 = (bf16[1,1,64,3584]{3,2,1,0:T(8,128)(2,1)S(1)}, bf16[1,1,64,3584]{3,2,1,0:T(8,128)(2,1)}, u32[]{:S(2)}) copy-start(bf16[1,1,64,3584]{3,2,1,0:T(8,128)(2,1)} %param.9) | copy-start | bytes 1376260
  22.6 13.4 %collective-permute-start.8 = (bf16[224,1024]{1,0:T(8,128)(2,1)S(1)}, bf16[224,1024]{1,0:T(8,128)(2,1)S(1)}, u32[]{:S(2)}, u32[]{:S(2)}) collective-permute-start(bf16[224,1024]{1,0:T(8,128)(2,1)S(1)} %pad_maximum_fusion.1), channel_id=1, source_target_pairs={{0,24},{4,28},{8,16},{12,20},{16,8},{20,12},{24,0},{28,4},{32,56},... | collective-permute-start | bytes 1376264 | tf_op jit(solution)/shard_map/ppermute | solution.py:46
  25.6 6.8 %collective-permute-start.5 = (bf16[64,1024]{1,0:T(8,128)(2,1)S(1)}, bf16[64,1024]{1,0:T(8,128)(2,1)S(1)}, u32[]{:S(2)}, u32[]{:S(2)}) collective-permute-start(bf16[64,1024]{1,0:T(8,128)(2,1)S(1)} %get-tuple-element.61.g0), channel_id=1, source_target_pairs={{0,64},{4,68},{8,72},{12,76},{16,80},{20,84},{24,88},{28,92},{32,9... | collective-permute-start | bytes 393224 | tf_op jit(solution)/shard_map/ppermute | solution.py:46
  28.5 6.4 %collective-permute-start.6 = (bf16[64,1024]{1,0:T(8,128)(2,1)S(1)}, bf16[64,1024]{1,0:T(8,128)(2,1)S(1)}, u32[]{:S(2)}, u32[]{:S(2)}) collective-permute-start(bf16[64,1024]{1,0:T(8,128)(2,1)S(1)} %get-tuple-element.61.g0), channel_id=1, source_target_pairs={{0,96},{4,100},{8,104},{12,108},{16,112},{20,116},{24,120},{28,124... | collective-permute-start | bytes 393224 | tf_op jit(solution)/shard_map/ppermute | solution.py:46
  29.7 5.3 %collective-permute-start.7 = (bf16[64,1024]{1,0:T(8,128)(2,1)S(1)}, bf16[64,1024]{1,0:T(8,128)(2,1)S(1)}, u32[]{:S(2)}, u32[]{:S(2)}) collective-permute-start(bf16[64,1024]{1,0:T(8,128)(2,1)S(1)} %get-tuple-element.61.g0), channel_id=1, source_target_pairs={{0,32},{4,36},{8,40},{12,44},{16,48},{20,52},{24,56},{28,60},{32,0... | collective-permute-start | bytes 393224 | tf_op jit(solution)/shard_map/ppermute | solution.py:46
  29.7 5.3 %copy-start.5 = (bf16[128,896]{1,0:T(8,128)(2,1)S(1)}, bf16[128,896]{1,0:T(8,128)(2,1)}, u32[]{:S(2)}) copy-start(bf16[128,896]{1,0:T(8,128)(2,1)} %get-tuple-element.68.r0) | copy-start | bytes 688132
  35.9 2.6 %collective-permute-start.10 = (bf16[448,1024]{1,0:T(8,128)(2,1)S(1)}, bf16[448,1024]{1,0:T(8,128)(2,1)S(1)}, u32[]{:S(2)}, u32[]{:S(2)}) collective-permute-start(bf16[448,1024]{1,0:T(8,128)(2,1)S(1)} %get-tuple-element.73), channel_id=1, source_target_pairs={{0,4},{4,0},{8,12},{12,8},{16,20},{20,16},{24,28},{28,24},{32,36},... | collective-permute-start | bytes 2752520 | tf_op jit(solution)/shard_map/ppermute | solution.py:46
  36.1 3.7 %collective-permute-start.9 = (bf16[448,1024]{1,0:T(8,128)(2,1)S(1)}, bf16[448,1024]{1,0:T(8,128)(2,1)S(1)}, u32[]{:S(2)}, u32[]{:S(2)}) collective-permute-start(bf16[448,1024]{1,0:T(8,128)(2,1)S(1)} %pad_maximum_fusion.a_ref), channel_id=1, source_target_pairs={{0,4},{4,0},{8,12},{12,8},{16,20},{20,16},{24,28},{28,24},{32,36},... | collective-permute-start | bytes 2752520 | tf_op jit(solution)/shard_map/ppermute | solution.py:46
  38.6 15.5 %collective-permute-start.12 = (bf16[224,1024]{1,0:T(8,128)(2,1)S(1)}, bf16[224,1024]{1,0:T(8,128)(2,1)S(1)}, u32[]{:S(2)}, u32[]{:S(2)}) collective-permute-start(bf16[224,1024]{1,0:T(8,128)(2,1)S(1)} %get-tuple-element.76), channel_id=1, source_target_pairs={{0,8},{4,12},{8,0},{12,4},{16,24},{20,28},{24,16},{28,20},{32,40},... | collective-permute-start | bytes 1376264 | tf_op jit(solution)/shard_map/ppermute | solution.py:46
  40.7 10.5 %collective-permute-start.13 = (bf16[64,1024]{1,0:T(8,128)(2,1)S(1)}, bf16[64,1024]{1,0:T(8,128)(2,1)S(1)}, u32[]{:S(2)}, u32[]{:S(2)}) collective-permute-start(bf16[64,1024]{1,0:T(8,128)(2,1)S(1)} %get-tuple-element.81), channel_id=1, source_target_pairs={{0,64},{4,68},{8,72},{12,76},{16,80},{20,84},{24,88},{28,92},{32,9... | collective-permute-start | bytes 393224 | tf_op jit(solution)/shard_map/ppermute | solution.py:46
  42.8 8.4 %collective-permute-start.14 = (bf16[64,1024]{1,0:T(8,128)(2,1)S(1)}, bf16[64,1024]{1,0:T(8,128)(2,1)S(1)}, u32[]{:S(2)}, u32[]{:S(2)}) collective-permute-start(bf16[64,1024]{1,0:T(8,128)(2,1)S(1)} %get-tuple-element.82), channel_id=1, source_target_pairs={{0,32},{4,36},{8,40},{12,44},{16,48},{20,52},{24,56},{28,60},{32,0... | collective-permute-start | bytes 393224 | tf_op jit(solution)/shard_map/ppermute | solution.py:46
  44.3 6.9 %collective-permute-start.15 = (bf16[64,1024]{1,0:T(8,128)(2,1)S(1)}, bf16[64,1024]{1,0:T(8,128)(2,1)S(1)}, u32[]{:S(2)}, u32[]{:S(2)}) collective-permute-start(bf16[64,1024]{1,0:T(8,128)(2,1)S(1)} %get-tuple-element.83), channel_id=1, source_target_pairs={{0,96},{4,100},{8,104},{12,108},{16,112},{20,116},{24,120},{28,124... | collective-permute-start | bytes 393224 | tf_op jit(solution)/shard_map/ppermute | solution.py:46
  45.6 17.3 %collective-permute-start.11 = (bf16[256,896]{1,0:T(8,128)(2,1)S(1)}, bf16[256,896]{1,0:T(8,128)(2,1)S(1)}, u32[]{:S(2)}, u32[]{:S(2)}) collective-permute-start(bf16[256,896]{1,0:T(8,128)(2,1)S(1)} %input_grad_pieces.1), channel_id=1, source_target_pairs={{1,0},{2,1},{3,2},{5,4},{6,5},{7,6},{9,8},{10,9},{11,10},{13,12},{... | collective-permute-start | bytes 1376264 | tf_op jit(solution)/shard_map/ppermute | solution.py:461
  54.2 7.3 %collective-permute-start.16 = (bf16[56,1024]{1,0:T(8,128)(2,1)S(1)}, bf16[56,1024]{1,0:T(8,128)(2,1)S(1)}, u32[]{:S(2)}, u32[]{:S(2)}) collective-permute-start(bf16[56,1024]{1,0:T(8,128)(2,1)S(1)} %get-tuple-element.105), channel_id=1, source_target_pairs={{0,24},{4,28},{8,16},{12,20},{16,8},{20,12},{24,0},{28,4},{32,56},... | collective-permute-start | bytes 344072 | tf_op jit(solution)/shard_map/ppermute | solution.py:46
  56.3 10.3 %collective-permute-start.21 = (bf16[56,1024]{1,0:T(8,128)(2,1)S(1)}, bf16[56,1024]{1,0:T(8,128)(2,1)S(1)}, u32[]{:S(2)}, u32[]{:S(2)}) collective-permute-start(bf16[56,1024]{1,0:T(8,128)(2,1)S(1)} %get-tuple-element.104), channel_id=1, source_target_pairs={{0,24},{4,28},{8,16},{12,20},{16,8},{20,12},{24,0},{28,4},{32,56},... | collective-permute-start | bytes 344072 | tf_op jit(solution)/shard_map/ppermute | solution.py:46
  57.6 19.4 %collective-permute-start.22 = (bf16[64,3584]{1,0:T(8,128)(2,1)S(1)}, bf16[64,3584]{1,0:T(8,128)(2,1)S(1)}, u32[]{:S(2)}, u32[]{:S(2)}) collective-permute-start(bf16[64,3584]{1,0:T(8,128)(2,1)S(1)} %own_groups.1), channel_id=1, source_target_pairs={{0,1},{1,2},{2,3},{4,5},{5,6},{6,7},{8,9},{9,10},{10,11},{12,13},{... | collective-permute-start | bytes 1376264 | tf_op jit(solution)/shard_map/ppermute | solution.py:472
  61.5 14.7 %collective-permute-start.17 = (bf16[56,1024]{1,0:T(8,128)(2,1)S(1)}, bf16[56,1024]{1,0:T(8,128)(2,1)S(1)}, u32[]{:S(2)}, u32[]{:S(2)}) collective-permute-start(bf16[56,1024]{1,0:T(8,128)(2,1)S(1)} %add_convert_fusion.1), channel_id=1, source_target_pairs={{0,128},{4,132},{8,136},{12,140},{16,144},{20,148},{24,152},{28,15... | collective-permute-start | bytes 344072 | tf_op jit(solution)/shard_map/ppermute | solution.py:46
  63.0 13.3 %collective-permute-start.18 = (bf16[64,896]{1,0:T(8,128)(2,1)S(1)}, bf16[64,896]{1,0:T(8,128)(2,1)S(1)}, u32[]{:S(2)}, u32[]{:S(2)}) collective-permute-start(bf16[64,896]{1,0:T(8,128)(2,1)S(1)} %get-tuple-element.108), channel_id=1, source_target_pairs={{0,64},{4,68},{8,72},{12,76},{16,80},{20,84},{24,88},{28,92},{32,9... | collective-permute-start | bytes 344072 | tf_op jit(solution)/shard_map/ppermute | solution.py:46
  64.7 11.5 %collective-permute-start.19 = (bf16[64,896]{1,0:T(8,128)(2,1)S(1)}, bf16[64,896]{1,0:T(8,128)(2,1)S(1)}, u32[]{:S(2)}, u32[]{:S(2)}) collective-permute-start(bf16[64,896]{1,0:T(8,128)(2,1)S(1)} %get-tuple-element.107), channel_id=1, source_target_pairs={{0,32},{4,36},{8,40},{12,44},{16,48},{20,52},{24,56},{28,60},{32,0... | collective-permute-start | bytes 344072 | tf_op jit(solution)/shard_map/ppermute | solution.py:46
  66.7 9.6 %collective-permute-start.20 = (bf16[64,896]{1,0:T(8,128)(2,1)S(1)}, bf16[64,896]{1,0:T(8,128)(2,1)S(1)}, u32[]{:S(2)}, u32[]{:S(2)}) collective-permute-start(bf16[64,896]{1,0:T(8,128)(2,1)S(1)} %get-tuple-element.106), channel_id=1, source_target_pairs={{0,96},{4,100},{8,104},{12,108},{16,112},{20,116},{24,120},{28,124... | collective-permute-start | bytes 344072 | tf_op jit(solution)/shard_map/ppermute | solution.py:46
